TPU v7x, 32 devices: a whole 2x2x4 slice. The times are simulated.
32 devices in a mesh: lat: 4 (over x, core), lon: 8 (over z, y).
Axes of the slice: x: 2, y: 2, z: 4, core: 2. Of those that a mesh axis runs over, the one named last changes fastest.
Arguments:
- tracers: float32 [256, 1152, 256], P(('lat', 'lon')), may hold values from 0.1 to 3
- phys_fine: bfloat16 [192, 3072, 144], P('lat', 'lon'), may hold values from -2 to 30, as said below
- mix_coarse: bfloat16 [64, 1024, 48], P('lat', 'lon'), may hold values from 0.0049743652 to 0.19921875
- surf_light: float32 [192, 3072], P('lat', 'lon'), may hold values from 0.5 to 4
- land_mask: int32 [64, 1024], P('lat', 'lon'), may hold values from 0 to 1, as said below
- owner_map: int32 [4, 64], P('lat'), may hold values from -1 to 255, as said below
Outputs:
- tracers_out: float32 [256, 1152, 256], P(('lat', 'lon'))
- heating: bfloat16 [48, 192, 3072], P(None, 'lat', 'lon')
Inputs may be any that keep to these rules, and one draw needn't show every extreme that they name: `owner_map`: -1 marks a block whose columns are all land, any other value is the slot that holds the block. Slots are numbered band by band, 64 to a band, owner by owner within a band with 8 slots each, and a block's slot lies in its own band. Every band has a multiple of 8 wet blocks. The wet blocks of a band, taken in order of longitude, are held by the owners in turn: the next wet block after one held by owner o is held by owner o + 1 (after 8 - 1 comes 0), also from the band's last wet block to its first; the r-th wet block of a band (from 0) lies in slot r // 8 of its owner. In some band every slot holds a block. `land_mask`: 1 for an ocean column, 0 for land; every column of a block that owner_map marks -1 is land. `phys_fine`: channel c * 48 + l holds level l of: c = 0 the eastward velocity on a fine cell's east face and c = 1 the northward velocity on its north face, as fractions of a cell per step within -0.15 to 0.15; c = 2 temperature within -2 to 30.
All inputs are finite; a program needn't handle non-finite values.
Results may differ from a plain program's by a relative error of at most 0.001.
Values sent between devices are 32-bit elements; how exact they have to be, the bound alone decides.
No kernel may reach another device: no remote copies, remote signals or barrier semaphores. Data moves between devices by JAX's collectives and lax.ppermute only.
A program may use at most 192 MiB of HBM per device.

v0:
```python
import functools

import jax
import jax.numpy as jnp
from jax import lax
from jax.experimental import pallas as pl
from jax.experimental.pallas import tpu as pltpu
from jax.sharding import PartitionSpec as P

ITERS = 2
LANES = 128
SUB = 8

diffuse_rate = 0.08
nano_chl_index = 10
diat_chl_index = 11

SLOT_TILE, SLOT_FULL, SLOT_WEST, SLOT_EAST, TILE_OWNER, TILE_WET, TILE_BASE = range(7)
TABLE_ROWS = 8

OPEN_EAST, OPEN_NORTH, OPEN_WEST, OPEN_SOUTH, LIGHT, WET = range(6)

VMEM_LIMIT = 48 * 1024 * 1024


def positive(value):
    return jnp.maximum(value, 0.0)


def lane_ids(rows=SUB):
    return lax.broadcasted_iota(jnp.int32, (rows, LANES), 1)


def turned(value, by):
    by = by % LANES
    return value if by == 0 else pltpu.roll(value, by, 1)


def along(axis, by, closed):
    size = lax.axis_size(axis)
    pairs = [(i, (i + by) % size) for i in range(size)]
    return [p for p in pairs if closed or p[1] == p[0] + by]


def table_kernel(slot_count, tile_blocks, lon_count, row_ref, out_ref, used_ref):
    me = lax.axis_index("lon")
    block_count = row_ref.shape[1]
    width = out_ref.shape[1]

    def clear(i, carry):
        for r in range(TABLE_ROWS):
            out_ref[r, i] = 0
        return carry

    lax.fori_loop(0, width, clear, 0)

    def unuse(i, carry):
        used_ref[0, i] = 0
        used_ref[1, i] = 0
        return carry

    lax.fori_loop(0, lon_count, unuse, 0)
    out_ref[TILE_BASE, 0] = me * tile_blocks

    def visit(k, carry):
        code = row_ref[0, k]
        safe = jnp.maximum(code, 0)
        owner = lax.rem(lax.div(safe, slot_count), lon_count)
        slot = lax.rem(safe, slot_count)
        tile = lax.div(k, tile_blocks)

        @pl.when((code >= 0) & (owner == me))
        def _():
            west = row_ref[0, lax.rem(k + block_count - 1, block_count)]
            east = row_ref[0, lax.rem(k + 1, block_count)]
            out_ref[SLOT_TILE, slot] = tile
            out_ref[SLOT_FULL, slot] = 1
            out_ref[SLOT_WEST, slot] = lax.rem(jnp.maximum(west, 0), slot_count)
            out_ref[SLOT_EAST, slot] = lax.rem(jnp.maximum(east, 0), slot_count)
            used_ref[0, tile] = 1

        @pl.when((code >= 0) & (tile == me))
        def _():
            local = lax.rem(k, tile_blocks)
            out_ref[TILE_OWNER, local] = owner
            out_ref[TILE_WET, local] = 1
            used_ref[1, owner] = 1

        return carry

    lax.fori_loop(0, block_count, visit, 0)

    def give(target, filled, line, count):
        def one(i, carry):
            def look(j, done):
                take = (done == 0) & (used_ref[line, j] == 0)

                @pl.when(take)
                def _():
                    out_ref[target, i] = j
                    used_ref[line, j] = 1

                return jnp.where(take, 1, done)

            lax.fori_loop(0, lon_count, look, out_ref[filled, i])
            return carry

        lax.fori_loop(0, count, one, 0)

    give(SLOT_TILE, SLOT_FULL, 0, slot_count)
    give(TILE_OWNER, TILE_WET, 1, tile_blocks)


def routing(row, slot_count, tile_blocks):
    lon_count = lax.axis_size("lon")
    width = max(slot_count, tile_blocks, lon_count)
    return pl.pallas_call(
        functools.partial(table_kernel, slot_count, tile_blocks, lon_count),
        out_shape=jax.ShapeDtypeStruct((TABLE_ROWS, width), jnp.int32),
        in_specs=[pl.BlockSpec(memory_space=pltpu.SMEM)],
        out_specs=pl.BlockSpec(memory_space=pltpu.SMEM),
        scratch_shapes=[pltpu.SMEM((2, lon_count), jnp.int32)],
        name="routing",
    )(row)


def pack_row(cells, group, side, start):
    ids = lane_ids() >> (side.bit_length() - 1)
    packed = None
    for g in range(group):
        piece = turned(cells[g], side * g - start)
        packed = piece if packed is None else jnp.where(ids == g, piece, packed)
    return packed


def pack_col(cells, group, side, start, offset, base):
    ids = lane_ids() & (side - 1)
    packed = base
    for g in range(group):
        piece = turned(cells[g], offset + g - start)
        packed = piece if packed is None else jnp.where(ids == offset + g, piece, packed)
    return packed


def edges_kernel(levels, side, table_ref, cell_ref, south_ref, north_ref, west_ref, east_ref):
    group = LANES // side
    halves = cell_ref.shape[2] // LANES
    rounds = cell_ref.shape[1] // levels // group
    level_tiles = levels // SUB

    def body(lt, carry):
        for i in range(rounds):
            row = pl.multiple_of(i * levels + lt * SUB, SUB)
            west = east = None
            for h in range(halves):
                cells = []
                for g in range(group):
                    at = pl.multiple_of((i * group + g) * levels + lt * SUB, SUB)
                    cells.append(cell_ref[0, pl.ds(at, SUB), h * LANES : (h + 1) * LANES])
                west = pack_col(cells, group, side, 0, h * group, west)
                east = pack_col(cells, group, side, side - 1, h * group, east)
                if h == 0:
                    south_ref[0, pl.ds(row, SUB), :] = pack_row(cells, group, side, 0)
                if h == halves - 1:
                    north_ref[0, pl.ds(row, SUB), :] = pack_row(cells, group, side, LANES - side)
            west_ref[0, pl.ds(row, SUB), :] = west
            east_ref[0, pl.ds(row, SUB), :] = east
        return carry

    lax.fori_loop(0, level_tiles, body, 0)


def edge_shapes(slot_count, lon_count, rows):
    f32 = jnp.float32
    shapes = [
        jax.ShapeDtypeStruct((lon_count, rows, LANES), f32),
        jax.ShapeDtypeStruct((lon_count, rows, LANES), f32),
        jax.ShapeDtypeStruct((slot_count, rows, LANES), f32),
        jax.ShapeDtypeStruct((slot_count, rows, LANES), f32),
    ]
    by_tile = pl.BlockSpec((1, rows, LANES), lambda s, t: (t[SLOT_TILE, s], 0, 0))
    by_slot = pl.BlockSpec((1, rows, LANES), lambda s, t: (s, 0, 0))
    return shapes, [by_tile, by_tile, by_slot, by_slot]


def first_edges(table, tracers, levels, side):
    slot_count, channels, cell_count = tracers.shape
    lon_count = lax.axis_size("lon")
    rows = channels * side // LANES
    shapes, specs = edge_shapes(slot_count, lon_count, rows)
    return pl.pallas_call(
        functools.partial(edges_kernel, levels, side),
        out_shape=shapes,
        grid_spec=pltpu.PrefetchScalarGridSpec(
            num_scalar_prefetch=1,
            grid=(slot_count,),
            in_specs=[pl.BlockSpec((1, channels, cell_count), lambda s, t: (s, 0, 0))],
            out_specs=specs,
        ),
        compiler_params=pltpu.CompilerParams(vmem_limit_bytes=VMEM_LIMIT),
        name="first_edges",
    )(table, tracers)


def react(mixed, par_light, warm_factor):
    (
        carbon_dis,
        alkalinity,
        oxygen,
        nitrate,
        ammonium,
        phosphate,
        silicate,
        iron_free,
        nano_carbon,
        diat_carbon,
        nano_chl,
        diat_chl,
        nano_iron,
        diat_iron,
        diat_silica,
        micro_zoo,
        meso_zoo,
        dissolved_org,
        small_part,
        big_part,
        small_iron,
        big_iron,
        big_silica,
        calcite,
    ) = mixed
    nitrogen = positive(nitrate) + positive(ammonium)
    limit_nitro = nitrogen / (0.5 + nitrogen)
    limit_phos = positive(phosphate) / (0.3 + positive(phosphate))
    limit_iron = positive(iron_free) / (0.2 + positive(iron_free))
    limit_sil = positive(silicate) / (1.0 + positive(silicate))
    nutr_nano = jnp.minimum(jnp.minimum(limit_nitro, limit_phos), limit_iron)
    nutr_diat = jnp.minimum(nutr_nano, limit_sil)
    lit = warm_factor * par_light
    prod_nano = 0.1 * lit / (par_light + 0.5) * nutr_nano * nano_carbon
    prod_diat = 0.12 * lit / (par_light + 1.0) * nutr_diat * diat_carbon
    ammon_share = (positive(ammonium) + 0.01) / (nitrogen + 0.02)
    graze_nano = 0.08 * warm_factor * micro_zoo / (1.0 + positive(nano_carbon))
    graze_diat = 0.06 * warm_factor * meso_zoo / (1.0 + positive(diat_carbon))
    loss_nano = graze_nano + 0.02
    loss_diat = graze_diat + 0.02
    eaten_nano = graze_nano * nano_carbon
    eaten_diat = graze_diat * diat_carbon
    death_micro = 0.03 * micro_zoo * positive(micro_zoo)
    death_meso = 0.03 * meso_zoo * positive(meso_zoo)
    remin_doc = 0.03 * warm_factor * dissolved_org
    remin_poc = 0.02 * warm_factor * small_part
    remin_goc = 0.01 * warm_factor * big_part
    nitrify = 0.05 * ammonium
    melt_si = 0.02 * big_silica
    melt_cal = 0.01 * calcite
    melt_sfe = 0.02 * small_iron
    melt_bfe = 0.01 * big_iron
    uptake = prod_nano + prod_diat
    remin_total = remin_doc + remin_poc + remin_goc
    calcify = 0.02 * prod_nano
    gained = remin_total - uptake
    shell = melt_cal - calcify
    by_ammon = ammon_share * uptake
    by_nitrate = 0.16 * (uptake - by_ammon - nitrify)
    return [
        carbon_dis + gained + shell,
        alkalinity + 2.0 * shell + by_nitrate,
        oxygen - 1.3 * gained - 0.32 * nitrify,
        nitrate - by_nitrate,
        ammonium + 0.16 * (remin_total - by_ammon - nitrify),
        phosphate + 0.01 * gained,
        silicate + melt_si - 0.15 * prod_diat,
        iron_free + melt_sfe + melt_bfe - 0.005 * uptake,
        nano_carbon + prod_nano - loss_nano * nano_carbon,
        diat_carbon + prod_diat - loss_diat * diat_carbon,
        nano_chl + 0.03 * prod_nano - loss_nano * nano_chl,
        diat_chl + 0.03 * prod_diat - loss_diat * diat_chl,
        nano_iron + 0.005 * prod_nano - loss_nano * nano_iron,
        diat_iron + 0.005 * prod_diat - loss_diat * diat_iron,
        diat_silica + 0.15 * prod_diat - loss_diat * diat_silica,
        micro_zoo + 0.3 * eaten_nano - death_micro,
        meso_zoo + 0.3 * eaten_diat - death_meso,
        dissolved_org + 0.3 * eaten_nano + 0.02 * nano_carbon - remin_doc,
        small_part + 0.4 * eaten_nano + death_micro - remin_poc,
        big_part + 0.4 * eaten_diat + 0.02 * diat_carbon + death_meso - remin_goc,
        small_iron + loss_nano * nano_iron - melt_sfe,
        big_iron + loss_diat * diat_iron - melt_bfe,
        big_silica + loss_diat * diat_silica - melt_si,
        calcite + calcify - melt_cal,
    ]


def step_kernel(levels, side, last, table_ref, cell_ref, phys_ref, rim_ref, rim_w_ref, rim_e_ref, *refs):
    if last:
        out_ref, chl_ref, coef_ref, moved_ref = refs
        edge_refs = ()
    else:
        out_ref, south_ref, north_ref, west_ref, east_ref, coef_ref, moved_ref = refs
        edge_refs = (south_ref, north_ref, west_ref, east_ref)
    channels, cell_count = cell_ref.shape[1:]
    tracer_count = channels // levels
    group = LANES // side
    halves = cell_count // LANES
    rounds = tracer_count // group
    level_tiles = levels // SUB
    rows = rounds * levels
    slot = pl.program_id(0)
    full = table_ref[SLOT_FULL, slot] == 1
    spans = [slice(h * LANES, (h + 1) * LANES) for h in range(halves)]

    @pl.when(jnp.logical_not(full))
    def _():
        out_ref[...] = jnp.zeros_like(out_ref)
        for ref in edge_refs:
            ref[...] = jnp.zeros_like(ref)
        if last:
            chl_ref[...] = jnp.zeros_like(chl_ref)

    @pl.when(full)
    def _():
        lane = lane_ids()
        sub = lax.broadcasted_iota(jnp.int32, (SUB, LANES), 0)
        col = lane & (side - 1)
        first_col = col == 0
        last_col = col == side - 1
        first_row = lane < side
        last_row = lane >= LANES - side
        flag_row = 4 * levels
        pack_at = flag_row + SUB

        def flag(f, h):
            return phys_ref[0, flag_row + f : flag_row + f + 1, spans[h]]

        def southward(values, edge):
            out = []
            for h in range(halves):
                before = edge if h == 0 else turned(values[h - 1], side)
                out.append(jnp.where(first_row, before, turned(values[h], side)))
            return out

        def northward(values, edge):
            out = []
            for h in range(halves):
                after = edge if h == halves - 1 else turned(values[h + 1], -side)
                out.append(jnp.where(last_row, after, turned(values[h], -side)))
            return out

        above_mix = [jnp.zeros((SUB, LANES), jnp.float32)] * halves
        west_pack = phys_ref[0, pack_at : pack_at + SUB, spans[0]]
        south_pack = phys_ref[0, pack_at : pack_at + SUB, spans[1]]
        for lt in range(level_tiles):
            at = slice(lt * SUB, (lt + 1) * SUB)
            east_face = [phys_ref[0, lt * SUB : (lt + 1) * SUB, spans[h]] for h in range(halves)]
            north_face = [
                phys_ref[0, levels + lt * SUB : levels + (lt + 1) * SUB, spans[h]] for h in range(halves)
            ]
            south_face = southward(north_face, turned(south_pack, -side * lt))
            for h in range(halves):
                open_e, open_n, open_w, open_s = (flag(f, h) for f in range(4))
                west_face = jnp.where(
                    first_col, turned(west_pack, -(h * group + lt)), turned(east_face[h], 1)
                )
                flow_e = east_face[h] * open_e
                flow_n = north_face[h] * open_n
                flow_w = west_face * open_w
                flow_s = south_face[h] * open_s
                out_e, in_e = jnp.maximum(flow_e, 0.0), jnp.minimum(flow_e, 0.0)
                out_n, in_n = jnp.maximum(flow_n, 0.0), jnp.minimum(flow_n, 0.0)
                in_w, out_w = jnp.maximum(flow_w, 0.0), jnp.minimum(flow_w, 0.0)
                in_s, out_s = jnp.maximum(flow_s, 0.0), jnp.minimum(flow_s, 0.0)
                drift = diffuse_rate * (open_w + open_e + open_s + open_n)
                coef_ref[0, at, spans[h]] = 1.0 - (out_e - out_w) - (out_n - out_s) - drift
                coef_ref[1, at, spans[h]] = diffuse_rate * open_e - in_e
                coef_ref[2, at, spans[h]] = diffuse_rate * open_w + in_w
                coef_ref[3, at, spans[h]] = diffuse_rate * open_n - in_n
                coef_ref[4, at, spans[h]] = diffuse_rate * open_s + in_s
                mix = phys_ref[0, 3 * levels + lt * SUB : 3 * levels + (lt + 1) * SUB, spans[h]]
                mix_up = pltpu.roll(jnp.where(sub == SUB - 1, above_mix[h], mix), 1, 0)
                above_mix[h] = mix
                if lt == level_tiles - 1:
                    mix = jnp.where(sub == SUB - 1, 0.0, mix)
                coef_ref[5, at, spans[h]] = 1.0 - mix - mix_up
                coef_ref[6, at, spans[h]] = mix
                coef_ref[7, at, spans[h]] = mix_up

        blank = jnp.zeros((SUB, cell_count), jnp.float32)
        moved_ref[0:SUB, :] = blank
        moved_ref[SUB + channels : 2 * SUB + channels, :] = blank

        def advect(lt, carry):
            at = pl.multiple_of(lt * SUB, SUB)
            coef = [[coef_ref[n, pl.ds(at, SUB), spans[h]] for n in range(5)] for h in range(halves)]
            for i in range(rounds):
                row = pl.multiple_of(i * levels + lt * SUB, SUB)
                rim_s = rim_ref[0, pl.ds(row, SUB), :]
                rim_n = rim_ref[0, pl.ds(pl.multiple_of(rows + row, SUB), SUB), :]
                rim_w = rim_w_ref[0, pl.ds(row, SUB), :]
                rim_e = rim_e_ref[0, pl.ds(row, SUB), :]
                for g in range(group):
                    chan = pl.multiple_of((i * group + g) * levels + lt * SUB, SUB)
                    here = [cell_ref[0, pl.ds(chan, SUB), spans[h]] for h in range(halves)]
                    south = southward(here, turned(rim_s, -side * g))
                    north = northward(here, turned(rim_n, LANES - side - side * g))
                    for h in range(halves):
                        at_w = h * group + g
                        west = jnp.where(first_col, turned(rim_w, -at_w), turned(here[h], 1))
                        east = jnp.where(last_col, turned(rim_e, side - 1 - at_w), turned(here[h], -1))
                        c, e, w, n, s = coef[h]
                        moved_ref[pl.ds(pl.multiple_of(SUB + chan, SUB), SUB), spans[h]] = (
                            c * here[h] + (e * east + w * west) + (n * north[h] + s * south[h])
                        )
            return carry

        lax.fori_loop(0, level_tiles, advect, 0)

        def reacting(lt, carry):
            at = pl.multiple_of(lt * SUB, SUB)
            depths = []
            for h in range(halves):
                mix_c, mix_d, mix_u = (coef_ref[n, pl.ds(at, SUB), spans[h]] for n in (5, 6, 7))
                mixed = []
                for t in range(tracer_count):
                    base = t * levels + lt * SUB
                    before = moved_ref[pl.ds(pl.multiple_of(base, SUB), SUB), spans[h]]
                    now = moved_ref[pl.ds(pl.multiple_of(base + SUB, SUB), SUB), spans[h]]
                    after = moved_ref[pl.ds(pl.multiple_of(base + 2 * SUB, SUB), SUB), spans[h]]
                    up = pltpu.roll(jnp.where(sub == SUB - 1, before, now), 1, 0)
                    down = pltpu.roll(jnp.where(sub == 0, after, now), SUB - 1, 0)
                    mixed.append(mix_c * now + mix_d * down + mix_u * up)
                absorb = 0.04 + 0.02 * (
                    positive(mixed[nano_chl_index]) + positive(mixed[diat_chl_index])
                )
                total = absorb
                for by in (1, 2, 4):
                    total = total + jnp.where(sub >= by, pltpu.roll(total, by, 0), 0.0)
                above = carry[h] + (total - absorb)
                depths.append(carry[h] + total[SUB - 1 : SUB, :])
                light = flag(LIGHT, h)
                wet = flag(WET, h)
                par_light = light * jnp.exp(-(above + 0.5 * absorb))
                warm = phys_ref[0, pl.ds(pl.multiple_of(2 * levels + lt * SUB, SUB), SUB), spans[h]]
                new = [value * wet for value in react(mixed, par_light, warm)]
                for t in range(tracer_count):
                    out_ref[0, pl.ds(pl.multiple_of(t * levels + lt * SUB, SUB), SUB), spans[h]] = new[t]
                if last:
                    chl_ref[0, pl.ds(at, SUB), spans[h]] = positive(new[nano_chl_index]) + positive(
                        new[diat_chl_index]
                    )
                else:
                    for i in range(rounds):
                        row = pl.multiple_of(i * levels + lt * SUB, SUB)
                        cells = new[i * group : (i + 1) * group]
                        west = None if h == 0 else west_ref[0, pl.ds(row, SUB), :]
                        east = None if h == 0 else east_ref[0, pl.ds(row, SUB), :]
                        west_ref[0, pl.ds(row, SUB), :] = pack_col(cells, group, side, 0, h * group, west)
                        east_ref[0, pl.ds(row, SUB), :] = pack_col(
                            cells, group, side, side - 1, h * group, east
                        )
                        if h == 0:
                            south_ref[0, pl.ds(row, SUB), :] = pack_row(cells, group, side, 0)
                        if h == halves - 1:
                            north_ref[0, pl.ds(row, SUB), :] = pack_row(cells, group, side, LANES - side)
            return tuple(depths)

        start = tuple(jnp.zeros((1, LANES), jnp.float32) for _ in range(halves))
        lax.fori_loop(0, level_tiles, reacting, start)


def step(table, cells, phys, rims, rim_w, rim_e, levels, side, last):
    slot_count, channels, cell_count = cells.shape
    lon_count = lax.axis_size("lon")
    rows = channels * side // LANES
    phys_rows = phys.shape[1]
    f32 = jnp.float32
    by_slot = pl.BlockSpec((1, channels, cell_count), lambda s, t: (s, 0, 0))
    shapes = [jax.ShapeDtypeStruct(cells.shape, f32)]
    specs = [by_slot]
    if last:
        shapes.append(jax.ShapeDtypeStruct((lon_count, levels, cell_count), f32))
        specs.append(pl.BlockSpec((1, levels, cell_count), lambda s, t: (t[SLOT_TILE, s], 0, 0)))
    else:
        more_shapes, more_specs = edge_shapes(slot_count, lon_count, rows)
        shapes += more_shapes
        specs += more_specs
    return pl.pallas_call(
        functools.partial(step_kernel, levels, side, last),
        out_shape=shapes,
        grid_spec=pltpu.PrefetchScalarGridSpec(
            num_scalar_prefetch=1,
            grid=(slot_count,),
            in_specs=[
                by_slot,
                pl.BlockSpec((1, phys_rows, cell_count), lambda s, t: (t[SLOT_TILE, s], 0, 0)),
                pl.BlockSpec((1, 2 * rows, LANES), lambda s, t: (t[SLOT_TILE, s], 0, 0)),
                pl.BlockSpec((1, rows, LANES), lambda s, t: (t[SLOT_WEST, s], 0, 0)),
                pl.BlockSpec((1, rows, LANES), lambda s, t: (t[SLOT_EAST, s], 0, 0)),
            ],
            out_specs=specs,
            scratch_shapes=[
                pltpu.VMEM((8, levels, cell_count), f32),
                pltpu.VMEM((channels + 2 * SUB, cell_count), f32),
            ],
        ),
        compiler_params=pltpu.CompilerParams(vmem_limit_bytes=VMEM_LIMIT),
        name="step",
    )(table, cells, phys, rims, rim_w, rim_e)


def coarsen_kernel(
    levels,
    side,
    factor,
    table_ref,
    fine_ref,
    mix_ref,
    light_ref,
    land_ref,
    south_ref,
    north_ref,
    west_ref,
    east_ref,
    pick_ref,
    out_ref,
    rows_ref,
):
    row = pl.program_id(0)
    row_count = pl.num_programs(0)
    tile_blocks = land_ref.shape[1] // side
    halves = side * side // LANES
    group = LANES // side
    fine_cols = light_ref.shape[1]
    f32 = jnp.float32
    picks = pick_ref[...]

    east_face = jnp.zeros((levels, LANES), f32)
    temp_mean = jnp.zeros((levels, LANES), f32)
    for r in range(factor):
        got = jnp.dot(fine_ref[r], picks, preferred_element_type=f32)
        east_face += got[0:levels, 0:LANES]
        temp_mean += got[2 * levels : 3 * levels, LANES : 2 * LANES]
        if r == factor - 1:
            north_face = got[levels : 2 * levels, LANES : 2 * LANES]
    rows_ref[row, 0:levels, :] = east_face * (1.0 / factor)
    rows_ref[row, levels : 2 * levels, :] = north_face * (1.0 / factor)
    rows_ref[row, 2 * levels : 3 * levels, :] = jnp.exp(0.0639 * (temp_mean * (1.0 / (factor * factor))))
    rows_ref[row, 3 * levels : 4 * levels, :] = mix_ref[0].astype(f32)

    @pl.when(row == row_count - 1)
    def _():
        lane = lane_ids()
        group_id = lane >> (side.bit_length() - 1)
        col_id = lane & (side - 1)
        flag_row = 4 * levels
        pack_at = flag_row + SUB
        wet = land_ref[...].astype(f32)
        sides = wet.shape
        lane2 = lax.broadcasted_iota(jnp.int32, sides, 1)
        sub2 = lax.broadcasted_iota(jnp.int32, sides, 0)
        diagonal = lane2 == sub2
        rim_w = jnp.sum(jnp.where(diagonal, west_ref[SUB : SUB + 1, :], 0.0), axis=1, keepdims=True)
        rim_e = jnp.sum(jnp.where(diagonal, east_ref[0:1, :], 0.0), axis=1, keepdims=True)
        wet_w = jnp.where(lane2 == 0, rim_w, pltpu.roll(wet, 1, 1))
        wet_e = jnp.where(lane2 == LANES - 1, rim_e, pltpu.roll(wet, LANES - 1, 1))
        wet_s = jnp.where(sub2 == 0, south_ref[levels : levels + 1, 0:LANES], pltpu.roll(wet, 1, 0))
        wet_n = jnp.where(sub2 == side - 1, north_ref[0:1, 0:LANES], pltpu.roll(wet, side - 1, 0))
        fold_r = lax.broadcasted_iota(jnp.int32, (side, side * factor), 0)
        fold_c = lax.broadcasted_iota(jnp.int32, (side, side * factor), 1)
        fold_d = fold_c - factor * fold_r
        fold = jnp.where((fold_d >= 0) & (fold_d < factor), 1.0, 0.0)
        narrow = picks[:, LANES : 2 * LANES].astype(f32)
        light_rows = jnp.dot(fold, light_ref[...], precision=lax.Precision.HIGHEST, preferred_element_type=f32)
        light_mean = jnp.dot(
            light_rows, narrow, precision=lax.Precision.HIGHEST, preferred_element_type=f32
        ) * (1.0 / (factor * factor))
        flags = [wet * wet_e, wet * wet_n, wet * wet_w, wet * wet_s, light_mean, wet]
        for r in range(side):
            for f, value in enumerate(flags):
                rows_ref[r, flag_row + f : flag_row + f + 1, :] = value[r : r + 1, :]
            rows_ref[r, flag_row + len(flags) : flag_row + SUB, :] = jnp.zeros((SUB - len(flags), LANES), f32)

        def place(q, carry):
            at = pl.multiple_of(q * SUB, SUB)
            for h in range(halves):
                values = [rows_ref[h * group + r, pl.ds(at, SUB), :] for r in range(group)]
                for b in range(tile_blocks):
                    block = None
                    for r in range(group):
                        piece = turned(values[r], side * (r - b))
                        block = piece if block is None else jnp.where(group_id == r, piece, block)
                    owner = table_ref[TILE_OWNER, b]
                    out_ref[owner, pl.ds(at, SUB), h * LANES : (h + 1) * LANES] = block
            return carry

        lax.fori_loop(0, pack_at // SUB, place, 0)

        fine_v = south_ref[0:levels, 0:fine_cols].astype(jnp.bfloat16)
        north_below = jnp.dot(fine_v, picks, preferred_element_type=f32)[:, LANES : 2 * LANES] * (1.0 / factor)
        for b in range(tile_blocks):
            owner = table_ref[TILE_OWNER, b]
            south_pack = jnp.zeros((SUB, LANES), f32)
            for lt in range(levels // SUB):
                piece = turned(north_below[lt * SUB : (lt + 1) * SUB, :], side * (lt - b))
                south_pack = jnp.where(group_id == lt, piece, south_pack)
            if b == 0:
                west_pack = west_ref[0:SUB, :]
            else:
                beside = table_ref[TILE_OWNER, b - 1]
                west_pack = jnp.zeros((SUB, LANES), f32)
                for h in range(halves):
                    for lt in range(levels // SUB):
                        face = out_ref[beside, lt * SUB : (lt + 1) * SUB, h * LANES : (h + 1) * LANES]
                        piece = turned(face, h * group + lt - (side - 1))
                        west_pack = jnp.where(col_id == h * group + lt, piece, west_pack)
            out_ref[owner, pack_at : pack_at + SUB, 0:LANES] = west_pack
            out_ref[owner, pack_at : pack_at + SUB, LANES : 2 * LANES] = south_pack


def coarsen(table, fine, mix, light, land, from_south, from_north, from_west, from_east, picks):
    lon_count = lax.axis_size("lon")
    side, tile_cols = land.shape
    levels = mix.shape[1]
    factor = fine.shape[0] // side
    fine_cols = fine.shape[2]
    phys_rows = 4 * levels + 2 * SUB
    f32 = jnp.float32

    def whole(x):
        return pl.BlockSpec(x.shape, lambda i, t: (0,) * x.ndim)

    return pl.pallas_call(
        functools.partial(coarsen_kernel, levels, side, factor),
        out_shape=jax.ShapeDtypeStruct((lon_count, phys_rows, side * side), f32),
        grid_spec=pltpu.PrefetchScalarGridSpec(
            num_scalar_prefetch=1,
            grid=(side,),
            in_specs=[
                pl.BlockSpec((factor, 3 * levels, fine_cols), lambda i, t: (i, 0, 0)),
                pl.BlockSpec((1, levels, tile_cols), lambda i, t: (i, 0, 0)),
                whole(light),
                whole(land),
                whole(from_south),
                whole(from_north),
                whole(from_west),
                whole(from_east),
                whole(picks),
            ],
            out_specs=pl.BlockSpec((lon_count, phys_rows, side * side), lambda i, t: (0, 0, 0)),
            scratch_shapes=[pltpu.VMEM((side, 4 * levels + SUB, LANES), f32)],
        ),
        compiler_params=pltpu.CompilerParams(vmem_limit_bytes=VMEM_LIMIT),
        name="coarsen",
    )(table, fine, mix, light, land, from_south, from_north, from_west, from_east, picks)


def owner_of(codes, block, slot_count, lon_count):
    return lax.rem(lax.div(jnp.maximum(codes[0, block], 0), slot_count), lon_count)


def hand_kernel(table_ref, below_ref, above_ref, south_ref, north_ref, out_ref):
    b = pl.program_id(0)
    rows = south_ref.shape[1]
    block = table_ref[TILE_BASE, 0] + b
    out_ref[0, 0:rows, :] = jnp.where(below_ref[0, block] >= 0, south_ref[0], 0.0)
    out_ref[0, rows : 2 * rows, :] = jnp.where(above_ref[0, block] >= 0, north_ref[0], 0.0)


def hand_on(table, codes_below, codes_above, from_south, from_north, slot_count, tile_blocks):
    lon_count, rows, width = from_south.shape

    def spot(t, b):
        return t[TILE_BASE, 0] + b

    return pl.pallas_call(
        hand_kernel,
        out_shape=jax.ShapeDtypeStruct((lon_count, 2 * rows, width), jnp.float32),
        grid_spec=pltpu.PrefetchScalarGridSpec(
            num_scalar_prefetch=3,
            grid=(tile_blocks,),
            in_specs=[
                pl.BlockSpec(
                    (1, rows, width),
                    lambda b, t, lo, hi: (owner_of(lo, spot(t, b), slot_count, lon_count), 0, 0),
                ),
                pl.BlockSpec(
                    (1, rows, width),
                    lambda b, t, lo, hi: (owner_of(hi, spot(t, b), slot_count, lon_count), 0, 0),
                ),
            ],
            out_specs=pl.BlockSpec((1, 2 * rows, width), lambda b, t, lo, hi: (t[TILE_OWNER, b], 0, 0)),
        ),
        compiler_params=pltpu.CompilerParams(vmem_limit_bytes=VMEM_LIMIT),
        name="hand_on",
    )(table, codes_below, codes_above, from_south, from_north)


def heat_kernel(levels, side, factor, table_ref, chl_ref, light_ref, land_ref, widen_ref, out_ref, rows_ref, wide_ref):
    tile_blocks = land_ref.shape[1] // side
    halves = side * side // LANES
    group = LANES // side
    fine_cols = light_ref.shape[1]
    fine_rows = light_ref.shape[0]
    f32 = jnp.float32
    group_id = lane_ids() >> (side.bit_length() - 1)

    def place(lt, carry):
        at = pl.multiple_of(lt * SUB, SUB)
        for h in range(halves):
            blocks = []
            for b in range(tile_blocks):
                owner = table_ref[TILE_OWNER, b]
                values = chl_ref[owner, pl.ds(at, SUB), h * LANES : (h + 1) * LANES]
                blocks.append(jnp.where(table_ref[TILE_WET, b] == 1, values, 0.0))
            for r in range(group):
                line = None
                for b in range(tile_blocks):
                    piece = turned(blocks[b], side * (b - r))
                    line = piece if line is None else jnp.where(group_id == b, piece, line)
                rows_ref[pl.ds(pl.multiple_of((h * group + r) * levels + lt * SUB, SUB), SUB), :] = line
        return carry

    lax.fori_loop(0, levels // SUB, place, 0)
    wet = land_ref[...].astype(f32)
    widen = widen_ref[...]
    above = jnp.zeros_like(wet)
    passing = jnp.ones_like(wet)
    for l in range(levels):
        chl = rows_ref[pl.ds(l, side, stride=levels), :]
        above = above + (0.04 + 0.02 * chl)
        through = jnp.exp(-above)
        kept = (passing - through) * wet
        passing = through
        high = kept.astype(jnp.bfloat16)
        low = (kept - high.astype(f32)).astype(jnp.bfloat16)
        wide_ref[l * side : (l + 1) * side, :] = jnp.dot(
            high, widen, preferred_element_type=f32
        ) + jnp.dot(low, widen, preferred_element_type=f32)

    sub = lax.broadcasted_iota(jnp.int32, (SUB, LANES), 0)
    sources = []
    for m in range(fine_rows // SUB):
        start = (m * SUB // factor) // SUB * SUB
        index = jnp.zeros_like(sub)
        for r in range(1, side):
            index = index + jnp.where(sub + m * SUB >= r * factor, 1, 0)
        sources.append((start, index - start))

    def spread(l, carry):
        for c in range(fine_cols // LANES):
            span = slice(c * LANES, (c + 1) * LANES)
            for m in range(0, fine_rows // SUB, 2):
                both = []
                for n in (m, m + 1):
                    start, index = sources[n]
                    lines = wide_ref[pl.ds(pl.multiple_of(l * side + start, SUB), SUB), span]
                    lines = jnp.take_along_axis(lines, index, axis=0)
                    both.append(lines * light_ref[n * SUB : (n + 1) * SUB, span])
                out_ref[l, m * SUB : (m + 2) * SUB, span] = jnp.concatenate(both, axis=0).astype(jnp.bfloat16)
        return carry

    lax.fori_loop(0, levels, spread, 0)


def heat(table, chl, light, land, levels, widen):
    side = land.shape[0]
    factor = light.shape[0] // side
    vmem = pl.BlockSpec(memory_space=pltpu.VMEM)
    return pl.pallas_call(
        functools.partial(heat_kernel, levels, side, factor),
        out_shape=jax.ShapeDtypeStruct((levels,) + light.shape, jnp.bfloat16),
        in_specs=[pl.BlockSpec(memory_space=pltpu.SMEM), vmem, vmem, vmem, vmem],
        out_specs=vmem,
        scratch_shapes=[
            pltpu.VMEM((side * levels, LANES), jnp.float32),
            pltpu.VMEM((side * levels, light.shape[1]), jnp.float32),
        ],
        compiler_params=pltpu.CompilerParams(vmem_limit_bytes=VMEM_LIMIT),
        name="heat",
    )(table, chl, light, land, widen)


def widened(x, rows, width):
    return jnp.pad(x, ((0, rows - x.shape[0]), (0, width - x.shape[1])))


def on_device(tracers, phys_fine, mix_coarse, surf_light, land_mask, owner_map):
    f32 = jnp.float32
    slot_count = tracers.shape[0]
    side = land_mask.shape[0]
    levels = mix_coarse.shape[2]
    tile_blocks = land_mask.shape[1] // side
    factor = phys_fine.shape[0] // side
    fine_cols = phys_fine.shape[1]
    block_count = owner_map.shape[1]
    group = LANES // side

    fine = jnp.transpose(phys_fine, (0, 2, 1))
    mix = jnp.transpose(mix_coarse, (0, 2, 1))
    wet = land_mask.astype(f32)
    codes = owner_map.astype(f32) + 1.0
    width = max(fine_cols, block_count)

    northward = jnp.concatenate(
        [
            widened(fine[-1, levels : 2 * levels, :].astype(f32), levels, width),
            widened(wet[-1:], 1, width),
            widened(codes, 1, width),
        ],
        axis=0,
    )
    southward = jnp.concatenate([widened(wet[:1], 1, width), widened(codes, 1, width)], axis=0)
    last_face = jnp.mean(
        fine[:, :levels, fine_cols - 1].astype(f32).reshape(side, factor, levels), axis=1
    )
    face_pack = jnp.pad(
        last_face.reshape(side // group, group, levels // SUB, SUB).transpose(3, 1, 0, 2),
        ((0, 0), (0, 0), (0, 0), (0, group - levels // SUB)),
    ).reshape(SUB, LANES)
    eastward = jnp.concatenate([face_pack, widened(wet[:, -1][None], 1, LANES)], axis=0)
    westward = widened(wet[:, 0][None], 1, LANES)

    from_south = lax.ppermute(northward, "lat", along("lat", 1, False))
    from_north = lax.ppermute(southward, "lat", along("lat", -1, False))
    from_west = lax.ppermute(eastward, "lon", along("lon", 1, True))
    from_east = lax.ppermute(westward, "lon", along("lon", -1, True))
    codes_below = from_south[levels + 1 :, :block_count].astype(jnp.int32) - 1
    codes_above = from_north[1:, :block_count].astype(jnp.int32) - 1

    fine_id = jnp.arange(fine_cols)[:, None]
    coarse_id = jnp.arange(land_mask.shape[1])[None, :]
    member = (fine_id // factor == coarse_id).astype(jnp.bfloat16)
    final = (fine_id == factor * coarse_id + factor - 1).astype(jnp.bfloat16)
    picks = jnp.concatenate([final, member], axis=1)

    table = routing(owner_map, slot_count, tile_blocks)
    south, north, west, east = first_edges(table, tracers, levels, side)
    phys = coarsen(
        table, fine, mix, surf_light, land_mask, from_south, from_north, from_west, from_east, picks
    )
    phys = lax.all_to_all(phys, "lon", 0, 0, tiled=True)

    current = tracers
    for step_index in range(ITERS):
        rim_w = lax.ppermute(east, "lon", along("lon", 1, True))
        rim_e = lax.ppermute(west, "lon", along("lon", -1, True))
        rim_s = lax.ppermute(north, "lat", along("lat", 1, False))
        rim_n = lax.ppermute(south, "lat", along("lat", -1, False))
        rim_s = lax.all_to_all(rim_s, "lon", 0, 0, tiled=True)
        rim_n = lax.all_to_all(rim_n, "lon", 0, 0, tiled=True)
        rims = hand_on(table, codes_below, codes_above, rim_s, rim_n, slot_count, tile_blocks)
        rims = lax.all_to_all(rims, "lon", 0, 0, tiled=True)
        last = step_index == ITERS - 1
        got = step(table, current, phys, rims, rim_w, rim_e, levels, side, last)
        if last:
            current, chl = got
        else:
            current, south, north, west, east = got
    chl = lax.all_to_all(chl, "lon", 0, 0, tiled=True)
    heating = heat(table, chl, surf_light, land_mask, levels, jnp.transpose(member))
    return current, heating


def solution(mesh):
    in_specs = (
        P(("lat", "lon"), None, None),
        P("lat", "lon", None),
        P("lat", "lon", None),
        P("lat", "lon"),
        P("lat", "lon"),
        P("lat", None),
    )
    out_specs = (P(("lat", "lon"), None, None), P(None, "lat", "lon"))
    return jax.shard_map(
        on_device, mesh=mesh, in_specs=in_specs, out_specs=out_specs, check_vma=False
    )
```

profile of v0, /device:TPU:0, one launch (start us, length us, event | category | flops | bytes accessed | tf_op | source)
XLA Modules:
  0.0 362.3 jit_solution(7150689911997882293)
XLA Ops:
  0.6 4.8 %routing.1.table_ref = s32[8,8]{1,0:T(8,128)} custom-call(s32[1,64]{1,0:T(1,128)} %row_ref.1), custom_call_target="tpu_custom_call" | custom-call | tf_op jit(solution)/shard_map/routing/pallas_call | solution.py:117
  6.1 12.1 %first_edges.1 = (f32[8,144,128]{2,1,0:T(8,128)S(1)}, f32[8,144,128]{2,1,0:T(8,128)S(1)}, f32[8,144,128]{2,1,0:T(8,128)S(1)}, f32[8,144,128]{2,1,0:T(8,128)S(1)}) custom-call(s32[8,8]{1,0:T(8,128)S(1)} %copy-done.10, f32[8,1152,256]{2,1,0:T(8,128)} %cell_ref.3), custom_call_target="tpu_custom_call" | custom-call | tf_op jit(solution)/shard_map/first_edges/pallas_call | solution.py:191
  19.9 3.2 collective-permute-start.4
  24.0 6.7 %all-to-all-start.1 = ((f32[8,144,128]{2,1,0:T(8,128)}), f32[8,144,128]{2,1,0:T(8,128)S(1)}, u32[]{:S(2)}, u32[]{:S(2)}) async-start(f32[8,144,128]{2,1,0:T(8,128)} %collective-permute-done.4), calls=%async_computation.1 | async-start | bytes 1179648 | tf_op jit(solution)/shard_map/all_to_all | solution.py:848
  33.0 9.1 %collective-permute-start = (f32[50,384]{1,0:T(8,128)S(1)}, f32[50,384]{1,0:T(8,128)S(1)}, u32[]{:S(2)}, u32[]{:S(2)}) collective-permute-start(f32[50,384]{1,0:T(8,128)S(1)} %fusion.1), channel_id=1, source_target_pairs={{0,8},{8,16},{16,24},{1,9},{9,17},{17,25},{2,10},{10,18},{18,26},{... | collective-permute-start | bytes 230408 | tf_op jit(solution)/shard_map/ppermute | solution.py:822
  43.4 5.7 %all-to-all-start.2 = ((f32[8,144,128]{2,1,0:T(8,128)}), f32[8,144,128]{2,1,0:T(8,128)S(1)}, u32[]{:S(2)}, u32[]{:S(2)}) async-start(f32[8,144,128]{2,1,0:T(8,128)} %collective-permute-done.5), calls=%async_computation.2 | async-start | bytes 1179648 | tf_op jit(solution)/shard_map/all_to_all | solution.py:849
  51.5 2.1 collective-permute-start.2
  53.5 2.8 collective-permute-start.3
  57.6 3.0 collective-permute-done.2.west_ref
  60.6 18.0 %coarsen.1 = f32[8,208,256]{2,1,0:T(8,128)} custom-call(s32[8,8]{1,0:T(8,128)S(1)} %copy-done.11, bf16[48,144,384]{2,1,0:T(8,128)(2,1)} %bitcast.13, bf16[16,48,128]{2,1,0:T(8,128)(2,1)S(1)} %bitcast.10, f32[48,384]{1,0:T(8,128)S(1)} %copy-done.9, s32[16,128]{1,0:T(8,128)S(1)} %copy-done.13, f32[50,384]{1,0:T(8,128)S(1)} %collective-permute-done.south_ref, ...), custom_call_target="tpu_custom_call" | custom-call | tf_op jit(solution)/shard_map/coarsen/pallas_call | solution.py:631
  78.6 6.5 %all-to-all-start = ((f32[8,208,256]{2,1,0:T(8,128)}), f32[8,208,256]{2,1,0:T(8,128)S(1)}, u32[]{:S(2)}, u32[]{:S(2)}) async-start(f32[8,208,256]{2,1,0:T(8,128)} %coarsen.1), calls=%async_computation | async-start | bytes 3407872 | tf_op jit(solution)/shard_map/all_to_all | solution.py:840
  87.1 38.5 %all-to-all-done.phys_ref = f32[8,208,256]{2,1,0:T(8,128)S(1)} async-done(((f32[8,208,256]{2,1,0:T(8,128)}), f32[8,208,256]{2,1,0:T(8,128)S(1)}, u32[]{:S(2)}, u32[]{:S(2)}) %all-to-all-start) | async-done | bytes 1703968 | tf_op jit(solution)/shard_map/all_to_all | solution.py:840
  125.6 4.3 %all-to-all-start.3 = ((f32[8,288,128]{2,1,0:T(8,128)}), f32[8,288,128]{2,1,0:T(8,128)S(1)}, u32[]{:S(2)}, u32[]{:S(2)}) async-start(f32[8,288,128]{2,1,0:T(8,128)} %copy-done.2), calls=%async_computation.3 | async-start | bytes 2359296 | tf_op jit(solution)/shard_map/all_to_all | solution.py:851
  129.9 2.0 collective-permute-start.6
  131.9 2.7 collective-permute-start.7
  134.6 34.2 %collective-permute-done.6.rim_w_ref = f32[8,144,128]{2,1,0:T(8,128)S(1)} collective-permute-done((f32[8,144,128]{2,1,0:T(8,128)}, f32[8,144,128]{2,1,0:T(8,128)S(1)}, u32[]{:S(2)}, u32[]{:S(2)}) %collective-permute-start.6) | collective-permute-done | bytes 589856 | tf_op jit(solution)/shard_map/ppermute | solution.py:844
  168.8 2.0 collective-permute-done.7.rim_e_ref
  172.7 39.6 %step.2 = (f32[8,1152,256]{2,1,0:T(8,128)}, f32[8,144,128]{2,1,0:T(8,128)S(1)}, f32[8,144,128]{2,1,0:T(8,128)S(1)}, f32[8,144,128]{2,1,0:T(8,128)S(1)}, f32[8,144,128]{2,1,0:T(8,128)S(1)}) custom-call(s32[8,8]{1,0:T(8,128)S(1)} %copy-done.11, f32[8,1152,256]{2,1,0:T(8,128)} %cell_ref.3, f32[8,208,256]{2,1,0:T(8,128)} %copy-done, ...), custom_call_target="tpu_custom_call" | custom-call | tf_op jit(solution)/shard_map/step/pallas_call | solution.py:486
  214.8 2.2 collective-permute-start.8
  217.9 5.0 %all-to-all-start.4 = ((f32[8,144,128]{2,1,0:T(8,128)}), f32[8,144,128]{2,1,0:T(8,128)S(1)}, u32[]{:S(2)}, u32[]{:S(2)}) async-start(f32[8,144,128]{2,1,0:T(8,128)} %collective-permute-done.8), calls=%async_computation.4 | async-start | bytes 1179648 | tf_op jit(solution)/shard_map/all_to_all | solution.py:848
  224.2 7.1 %collective-permute-done.9 = f32[8,144,128]{2,1,0:T(8,128)S(1)} collective-permute-done((f32[8,144,128]{2,1,0:T(8,128)}, f32[8,144,128]{2,1,0:T(8,128)S(1)}, u32[]{:S(2)}, u32[]{:S(2)}) %collective-permute-start.9) | collective-permute-done | bytes 589856 | tf_op jit(solution)/shard_map/ppermute | solution.py:847
  231.3 3.9 %all-to-all-done.4.south_ref = f32[8,144,128]{2,1,0:T(8,128)S(1)} async-done(((f32[8,144,128]{2,1,0:T(8,128)}), f32[8,144,128]{2,1,0:T(8,128)S(1)}, u32[]{:S(2)}, u32[]{:S(2)}) %all-to-all-start.4) | async-done | bytes 589856 | tf_op jit(solution)/shard_map/all_to_all | solution.py:848
  235.2 23.0 %all_to_all.40.north_ref = f32[8,144,128]{2,1,0:T(8,128)S(1)} all-to-all(f32[8,144,128]{2,1,0:T(8,128)S(1)} %collective-permute-done.9), channel_id=1, replica_groups=mesh['lat'=4,'lon'=8] {'lon'}, dimensions={0} | all-to-all | bytes 1179648 | tf_op jit(solution)/shard_map/all_to_all | solution.py:849
  260.2 4.3 %all-to-all-start.6 = ((f32[8,288,128]{2,1,0:T(8,128)}), f32[8,288,128]{2,1,0:T(8,128)S(1)}, u32[]{:S(2)}, u32[]{:S(2)}) async-start(f32[8,288,128]{2,1,0:T(8,128)} %copy-done.3), calls=%async_computation.6 | async-start | bytes 2359296 | tf_op jit(solution)/shard_map/all_to_all | solution.py:851
  264.5 2.0 collective-permute-start.10
  266.5 2.7 collective-permute-start.11
  269.2 34.2 %collective-permute-done.10.rim_w_ref = f32[8,144,128]{2,1,0:T(8,128)S(1)} collective-permute-done((f32[8,144,128]{2,1,0:T(8,128)}, f32[8,144,128]{2,1,0:T(8,128)S(1)}, u32[]{:S(2)}, u32[]{:S(2)}) %collective-permute-start.10) | collective-permute-done | bytes 589856 | tf_op jit(solution)/shard_map/ppermute | solution.py:844
  303.4 2.7 collective-permute-done.11.rim_e_ref
  308.0 30.9 %step.3 = (f32[8,1152,256]{2,1,0:T(8,128)}, f32[8,48,256]{2,1,0:T(8,128)S(1)}) custom-call(s32[8,8]{1,0:T(8,128)S(1)} %copy-done.11, f32[8,1152,256]{2,1,0:T(8,128)} %get-tuple-element.17.cell_ref, f32[8,208,256]{2,1,0:T(8,128)S(1)} %copy-done.1, f32[8,288,128]{2,1,0:T(8,128)S(1)} %all-to-all-done.6.rim_ref, ...), custom_call_target="tpu_custom_call" | custom-call | tf_op jit(solution)/shard_map/step/pallas_call | solution.py:486
  339.6 4.5 %all-to-all-start.7 = ((f32[8,48,256]{2,1,0:T(8,128)}), f32[8,48,256]{2,1,0:T(8,128)S(1)}, u32[]{:S(2)}, u32[]{:S(2)}) async-start(f32[8,48,256]{2,1,0:T(8,128)} %copy-done.8), calls=%async_computation.7 | async-start | bytes 786432 | tf_op jit(solution)/shard_map/all_to_all | solution.py:858
  344.2 12.0 %all-to-all-done.7.chl_ref = f32[8,48,256]{2,1,0:T(8,128)S(1)} async-done(((f32[8,48,256]{2,1,0:T(8,128)}), f32[8,48,256]{2,1,0:T(8,128)S(1)}, u32[]{:S(2)}, u32[]{:S(2)}) %all-to-all-start.7) | async-done | bytes 393248 | tf_op jit(solution)/shard_map/all_to_all | solution.py:858
  356.8 5.4 %heat.1 = bf16[48,48,384]{2,1,0:T(8,128)(2,1)} custom-call(s32[8,8]{1,0:T(8,128)S(1)} %copy-done.11, f32[8,48,256]{2,1,0:T(8,128)S(1)} %all-to-all-done.7.chl_ref, f32[48,384]{1,0:T(8,128)S(1)} %copy-done.9, s32[16,128]{1,0:T(8,128)S(1)} %copy-done.14, bf16[128,384]{1,0:T(8,128)(2,1)S(1)} %fusion.widen_ref), custom_call_target="tpu_custom_call" | custom-call | tf_op jit(solution)/shard_map/heat/pallas_call | solution.py:768
  (90 shorter events, 24.3 us)
Async XLA Ops:
  6.1 26.0 %copy-start.13 = (s32[16,128]{1,0:T(8,128)S(1)}, s32[16,128]{1,0:T(8,128)}, u32[]{:S(2)}) copy-start(s32[16,128]{1,0:T(8,128)} %land_ref.3) | copy-start | bytes 24580
  6.1 26.0 %copy-start.24 = (s32[1,64]{1,0:T(1,128)S(1)}, s32[1,64]{1,0:T(1,128)}, u32[]{:S(2)}) copy-start(s32[1,64]{1,0:T(1,128)} %row_ref.1) | copy-start | bytes 772
  19.9 4.1 %collective-permute-start.4 = (f32[8,144,128]{2,1,0:T(8,128)S(1)}, f32[8,144,128]{2,1,0:T(8,128)}, u32[]{:S(2)}, u32[]{:S(2)}) collective-permute-start(f32[8,144,128]{2,1,0:T(8,128)S(1)} %get-tuple-element.13), channel_id=1, source_target_pairs={{0,8},{8,16},{16,24},{1,9},{9,17},{17,25},{2,10},{10,18},{18,26},{... | collective-permute-start | bytes 1769480 | tf_op jit(solution)/shard_map/ppermute | solution.py:846
  24.0 19.4 %all-to-all-start.1 = ((f32[8,144,128]{2,1,0:T(8,128)}), f32[8,144,128]{2,1,0:T(8,128)S(1)}, u32[]{:S(2)}, u32[]{:S(2)}) async-start(f32[8,144,128]{2,1,0:T(8,128)} %collective-permute-done.4), calls=%async_computation.1 | async-start | bytes 1179648 | tf_op jit(solution)/shard_map/all_to_all | solution.py:848
  30.7 30.0 %copy-start.9 = (f32[48,384]{1,0:T(8,128)S(1)}, f32[48,384]{1,0:T(8,128)}, u32[]{:S(2)}) copy-start(f32[48,384]{1,0:T(8,128)} %light_ref.3) | copy-start | bytes 221188
  30.7 30.0 %copy-start.11 = (s32[8,8]{1,0:T(8,128)S(1)}, s32[8,8]{1,0:T(8,128)}, u32[]{:S(2)}) copy-start(s32[8,8]{1,0:T(8,128)} %routing.1.table_ref) | copy-start | bytes 772
  30.7 30.0 %copy-start.12 = (bf16[16,128,48]{1,2,0:T(8,128)(2,1)S(1)}, bf16[16,128,48]{1,2,0:T(8,128)(2,1)}, u32[]{:S(2)}) copy-start(bf16[16,128,48]{1,2,0:T(8,128)(2,1)} %param.8) | copy-start | bytes 589828
  30.7 12.7 %collective-permute-start.5 = (f32[8,144,128]{2,1,0:T(8,128)S(1)}, f32[8,144,128]{2,1,0:T(8,128)}, u32[]{:S(2)}, u32[]{:S(2)}) collective-permute-start(f32[8,144,128]{2,1,0:T(8,128)S(1)} %get-tuple-element.14), channel_id=1, source_target_pairs={{8,0},{16,8},{24,16},{9,1},{17,9},{25,17},{10,2},{18,10},{26,18},{... | collective-permute-start | bytes 1769480 | tf_op jit(solution)/shard_map/ppermute | solution.py:847
  33.0 27.7 %collective-permute-start = (f32[50,384]{1,0:T(8,128)S(1)}, f32[50,384]{1,0:T(8,128)S(1)}, u32[]{:S(2)}, u32[]{:S(2)}) collective-permute-start(f32[50,384]{1,0:T(8,128)S(1)} %fusion.1), channel_id=1, source_target_pairs={{0,8},{8,16},{16,24},{1,9},{9,17},{17,25},{2,10},{10,18},{18,26},{... | collective-permute-start | bytes 230408 | tf_op jit(solution)/shard_map/ppermute | solution.py:822
  42.1 15.5 %collective-permute-start.1 = (f32[2,384]{1,0:T(2,128)S(1)}, f32[2,384]{1,0:T(2,128)S(1)}, u32[]{:S(2)}, u32[]{:S(2)}) collective-permute-start(f32[2,384]{1,0:T(2,128)S(1)} %fusion.4), channel_id=1, source_target_pairs={{8,0},{16,8},{24,16},{9,1},{17,9},{25,17},{10,2},{18,10},{26,18},{... | collective-permute-start | bytes 9224 | tf_op jit(solution)/shard_map/ppermute | solution.py:823
  43.4 35.2 %all-to-all-start.2 = ((f32[8,144,128]{2,1,0:T(8,128)}), f32[8,144,128]{2,1,0:T(8,128)S(1)}, u32[]{:S(2)}, u32[]{:S(2)}) async-start(f32[8,144,128]{2,1,0:T(8,128)} %collective-permute-done.5), calls=%async_computation.2 | async-start | bytes 1179648 | tf_op jit(solution)/shard_map/all_to_all | solution.py:849
  51.5 9.2 %collective-permute-start.2 = (f32[9,128]{1,0:T(8,128)S(1)}, f32[9,128]{1,0:T(8,128)S(1)}, u32[]{:S(2)}, u32[]{:S(2)}) collective-permute-start(f32[9,128]{1,0:T(8,128)S(1)} %select_maximum_fusion.1), channel_id=1, source_target_pairs={{0,1},{1,2},{2,3},{3,4},{4,5},{5,6},{6,7},{7,0},{8,9},{9,10},{10,1... | collective-permute-start | bytes 13832 | tf_op jit(solution)/shard_map/ppermute | solution.py:824
  53.5 4.1 %collective-permute-start.3 = (f32[1,128]{1,0:T(1,128)S(1)}, f32[1,128]{1,0:T(1,128)S(1)}, u32[]{:S(2)}, u32[]{:S(2)}) collective-permute-start(f32[1,128]{1,0:T(1,128)S(1)} %pad.28), channel_id=1, source_target_pairs={{0,7},{1,0},{2,1},{3,2},{4,3},{5,4},{6,5},{7,6},{8,15},{9,8},{10,9... | collective-permute-start | bytes 1544 | tf_op jit(solution)/shard_map/ppermute | solution.py:825
  56.3 22.3 %copy-start.22 = (s32[384]{0:T(512)}, s32[384]{0:T(512)S(1)}, u32[]{:S(2)}) copy-start(s32[384]{0:T(512)S(1)} %add_select_fusion) | copy-start | bytes 4612
  78.6 47.0 %all-to-all-start = ((f32[8,208,256]{2,1,0:T(8,128)}), f32[8,208,256]{2,1,0:T(8,128)S(1)}, u32[]{:S(2)}, u32[]{:S(2)}) async-start(f32[8,208,256]{2,1,0:T(8,128)} %coarsen.1), calls=%async_computation | async-start | bytes 3407872 | tf_op jit(solution)/shard_map/all_to_all | solution.py:840
  85.1 40.5 %copy-start.15 = (s32[1,64]{1,0:T(1,128)}, s32[1,64]{1,0:T(1,128)S(1)}, u32[]{:S(2)}) copy-start(s32[1,64]{1,0:T(1,128)S(1)} %fusion.9.below_ref) | copy-start | bytes 772
  125.6 46.0 %copy-start = (f32[8,208,256]{2,1,0:T(8,128)}, f32[8,208,256]{2,1,0:T(8,128)S(1)}, u32[]{:S(2)}) copy-start(f32[8,208,256]{2,1,0:T(8,128)S(1)} %all-to-all-done.phys_ref) | copy-start | bytes 5111812
  125.6 46.0 %all-to-all-start.3 = ((f32[8,288,128]{2,1,0:T(8,128)}), f32[8,288,128]{2,1,0:T(8,128)S(1)}, u32[]{:S(2)}, u32[]{:S(2)}) async-start(f32[8,288,128]{2,1,0:T(8,128)} %copy-done.2), calls=%async_computation.3 | async-start | bytes 2359296 | tf_op jit(solution)/shard_map/all_to_all | solution.py:851
  129.9 38.9 %collective-permute-start.6 = (f32[8,144,128]{2,1,0:T(8,128)}, f32[8,144,128]{2,1,0:T(8,128)S(1)}, u32[]{:S(2)}, u32[]{:S(2)}) collective-permute-start(f32[8,144,128]{2,1,0:T(8,128)} %copy-done.18), channel_id=1, source_target_pairs={{0,1},{1,2},{2,3},{3,4},{4,5},{5,6},{6,7},{7,0},{8,9},{9,10},{10,1... | collective-permute-start | bytes 1769480 | tf_op jit(solution)/shard_map/ppermute | solution.py:844
  131.9 38.9 %collective-permute-start.7 = (f32[8,144,128]{2,1,0:T(8,128)}, f32[8,144,128]{2,1,0:T(8,128)S(1)}, u32[]{:S(2)}, u32[]{:S(2)}) collective-permute-start(f32[8,144,128]{2,1,0:T(8,128)} %copy-done.17), channel_id=1, source_target_pairs={{0,7},{1,0},{2,1},{3,2},{4,3},{5,4},{6,5},{7,6},{8,15},{9,8},{10,9... | collective-permute-start | bytes 1769480 | tf_op jit(solution)/shard_map/ppermute | solution.py:845
  171.6 1.1 copy-start.5
  214.8 43.4 %copy-start.16 = (s32[1,64]{1,0:T(1,128)S(1)}, s32[1,64]{1,0:T(1,128)}, u32[]{:S(2)}) copy-start(s32[1,64]{1,0:T(1,128)} %copy-done.15) | copy-start | bytes 772
  214.8 3.2 collective-permute-start.8
  217.9 17.3 %all-to-all-start.4 = ((f32[8,144,128]{2,1,0:T(8,128)}), f32[8,144,128]{2,1,0:T(8,128)S(1)}, u32[]{:S(2)}, u32[]{:S(2)}) async-start(f32[8,144,128]{2,1,0:T(8,128)} %collective-permute-done.8), calls=%async_computation.4 | async-start | bytes 1179648 | tf_op jit(solution)/shard_map/all_to_all | solution.py:848
  222.9 8.4 %collective-permute-start.9 = (f32[8,144,128]{2,1,0:T(8,128)}, f32[8,144,128]{2,1,0:T(8,128)S(1)}, u32[]{:S(2)}, u32[]{:S(2)}) collective-permute-start(f32[8,144,128]{2,1,0:T(8,128)} %copy-done.21), channel_id=1, source_target_pairs={{8,0},{16,8},{24,16},{9,1},{17,9},{25,17},{10,2},{18,10},{26,18},{... | collective-permute-start | bytes 1769480 | tf_op jit(solution)/shard_map/ppermute | solution.py:847
  260.2 46.7 %copy-start.1 = (f32[8,208,256]{2,1,0:T(8,128)S(1)}, f32[8,208,256]{2,1,0:T(8,128)}, u32[]{:S(2)}) copy-start(f32[8,208,256]{2,1,0:T(8,128)} %copy-done) | copy-start | bytes 5111812
  260.2 46.7 %all-to-all-start.6 = ((f32[8,288,128]{2,1,0:T(8,128)}), f32[8,288,128]{2,1,0:T(8,128)S(1)}, u32[]{:S(2)}, u32[]{:S(2)}) async-start(f32[8,288,128]{2,1,0:T(8,128)} %copy-done.3), calls=%async_computation.6 | async-start | bytes 2359296 | tf_op jit(solution)/shard_map/all_to_all | solution.py:851
  264.5 38.9 %collective-permute-start.10 = (f32[8,144,128]{2,1,0:T(8,128)}, f32[8,144,128]{2,1,0:T(8,128)S(1)}, u32[]{:S(2)}, u32[]{:S(2)}) collective-permute-start(f32[8,144,128]{2,1,0:T(8,128)} %copy-done.20), channel_id=1, source_target_pairs={{0,1},{1,2},{2,3},{3,4},{4,5},{5,6},{6,7},{7,0},{8,9},{9,10},{10,1... | collective-permute-start | bytes 1769480 | tf_op jit(solution)/shard_map/ppermute | solution.py:844
  266.5 39.6 %collective-permute-start.11 = (f32[8,144,128]{2,1,0:T(8,128)}, f32[8,144,128]{2,1,0:T(8,128)S(1)}, u32[]{:S(2)}, u32[]{:S(2)}) collective-permute-start(f32[8,144,128]{2,1,0:T(8,128)} %copy-done.19), channel_id=1, source_target_pairs={{0,7},{1,0},{2,1},{3,2},{4,3},{5,4},{6,5},{7,6},{8,15},{9,8},{10,9... | collective-permute-start | bytes 1769480 | tf_op jit(solution)/shard_map/ppermute | solution.py:845
  306.9 1.1 copy-start.7
  308.0 36.1 %copy-start.23 = (s32[384]{0:T(512)S(1)}, s32[384]{0:T(512)}, u32[]{:S(2)}) copy-start(s32[384]{0:T(512)} %copy-done.22) | copy-start | bytes 4612
  339.6 16.5 %all-to-all-start.7 = ((f32[8,48,256]{2,1,0:T(8,128)}), f32[8,48,256]{2,1,0:T(8,128)S(1)}, u32[]{:S(2)}, u32[]{:S(2)}) async-start(f32[8,48,256]{2,1,0:T(8,128)} %copy-done.8), calls=%async_computation.7 | async-start | bytes 786432 | tf_op jit(solution)/shard_map/all_to_all | solution.py:858
  (12 other events, 10.0 us)
where the time goes:
time: 360 us; the launch traced here: 362 us
  waiting for transfers between devices  140 us (39%)
  Pallas kernels  113 us (31%)
  starting transfers between devices  69.8 us (19%)
  blocking collectives  23 us (6%)
  local copies, waits for them, and re-layouts  12.7 us (4%)
    pallas_call x2, Pallas kernels, step(): pl.pallas_call(functools.partial(step_kernel, levels, side, last), out_sh...  70.5 us
    ppermute x2, waiting for transfers between devices, on_device(): rim_w = lax.ppermute(east, 'lon', along('lon', 1, True))  68.3 us
    all_to_all x1, waiting for transfers between devices, on_device(): phys = lax.all_to_all(phys, 'lon', 0, 0, tiled=True)  38.5 us
    all_to_all x1, blocking collectives, on_device(): rim_n = lax.all_to_all(rim_n, 'lon', 0, 0, tiled=True)  23 us
    pallas_call x1, Pallas kernels, coarsen(): pl.pallas_call(functools.partial(coarsen_kernel, levels, side, factor), o...  18 us
    unnamed x51, local copies, waits for them, and re-layouts  12.3 us
    pallas_call x1, Pallas kernels, first_edges(): pl.pallas_call(functools.partial(edges_kernel, levels, side), out_shape=s...  12.1 us
    all_to_all x1, waiting for transfers between devices, on_device(): chl = lax.all_to_all(chl, 'lon', 0, 0, tiled=True)  12 us
  transfers between devices with their start and end apart: 19, of which 12 were waited for; matrix products, arithmetic and copies ran while one was open for 1% of the time, Pallas kernels for 5%

commit v1 on v0

--- a/solution.py
+++ b/solution.py
@@ -36,6 +36,18 @@
     return value if by == 0 else pltpu.roll(value, by, 1)
 
 
+def quotient(value, by):
+    if by & (by - 1) == 0:
+        return lax.shift_right_logical(value, jnp.int32(by.bit_length() - 1))
+    return lax.div(value, jnp.int32(by))
+
+
+def remainder(value, by):
+    if by & (by - 1) == 0:
+        return value & (by - 1)
+    return lax.rem(value, jnp.int32(by))
+
+
 def along(axis, by, closed):
     size = lax.axis_size(axis)
     pairs = [(i, (i + by) % size) for i in range(size)]
@@ -65,30 +77,30 @@
     def visit(k, carry):
         code = row_ref[0, k]
         safe = jnp.maximum(code, 0)
-        owner = lax.rem(lax.div(safe, slot_count), lon_count)
-        slot = lax.rem(safe, slot_count)
-        tile = lax.div(k, tile_blocks)
+        owner = remainder(quotient(safe, slot_count), lon_count)
+        slot = remainder(safe, slot_count)
+        tile = quotient(k, tile_blocks)
 
         @pl.when((code >= 0) & (owner == me))
         def _():
-            west = row_ref[0, lax.rem(k + block_count - 1, block_count)]
-            east = row_ref[0, lax.rem(k + 1, block_count)]
+            west = row_ref[0, remainder(k + block_count - 1, block_count)]
+            east = row_ref[0, remainder(k + 1, block_count)]
             out_ref[SLOT_TILE, slot] = tile
             out_ref[SLOT_FULL, slot] = 1
-            out_ref[SLOT_WEST, slot] = lax.rem(jnp.maximum(west, 0), slot_count)
-            out_ref[SLOT_EAST, slot] = lax.rem(jnp.maximum(east, 0), slot_count)
+            out_ref[SLOT_WEST, slot] = remainder(jnp.maximum(west, 0), slot_count)
+            out_ref[SLOT_EAST, slot] = remainder(jnp.maximum(east, 0), slot_count)
             used_ref[0, tile] = 1
 
         @pl.when((code >= 0) & (tile == me))
         def _():
-            local = lax.rem(k, tile_blocks)
+            local = remainder(k, tile_blocks)
             out_ref[TILE_OWNER, local] = owner
             out_ref[TILE_WET, local] = 1
             used_ref[1, owner] = 1
 
         return carry
 
-    lax.fori_loop(0, block_count, visit, 0)
+    lax.fori_loop(0, block_count, visit, 0, unroll=4)
 
     def give(target, filled, line, count):
         def one(i, carry):
@@ -102,7 +114,10 @@
 
                 return jnp.where(take, 1, done)
 
-            lax.fori_loop(0, lon_count, look, out_ref[filled, i])
+            @pl.when(out_ref[filled, i] == 0)
+            def _():
+                lax.fori_loop(0, lon_count, look, 0)
+
             return carry
 
         lax.fori_loop(0, count, one, 0)
@@ -124,66 +139,75 @@
     )(row)
 
 
-def pack_row(cells, group, side, start):
-    ids = lane_ids() >> (side.bit_length() - 1)
-    packed = None
-    for g in range(group):
-        piece = turned(cells[g], side * g - start)
-        packed = piece if packed is None else jnp.where(ids == g, piece, packed)
+def merged(pieces, ids):
+    packed = pieces[0]
+    for g in range(1, len(pieces)):
+        packed = jnp.where(ids == g, pieces[g], packed)
     return packed
 
 
-def pack_col(cells, group, side, start, offset, base):
-    ids = lane_ids() & (side - 1)
-    packed = base
-    for g in range(group):
-        piece = turned(cells[g], offset + g - start)
-        packed = piece if packed is None else jnp.where(ids == offset + g, piece, packed)
-    return packed
-
-
-def edges_kernel(levels, side, table_ref, cell_ref, south_ref, north_ref, west_ref, east_ref):
+def pack_columns(first, second, side):
+    lane = lane_ids()
+    odd = (lane & 1) == 1
+    here = (lane & (side - 1)) >> 1
+    there = ((lane + 1) & (side - 1)) >> 1
+    even_ends = merged([turned(v, 1 + 2 * g) for g, v in enumerate(first)], here)
+    odd_ends = merged([turned(v, 2 * g) for g, v in enumerate(second)], there)
+    return jnp.where(odd, even_ends, odd_ends), jnp.where(odd, odd_ends, even_ends)
+
+
+def pack_rows(first, second, side):
+    lane = lane_ids()
+    low = lane < LANES // 2
+    lead = (lane & side) == 0
+    here = lane >> side.bit_length()
+    there = ((lane + side) & (LANES - 1)) >> side.bit_length()
+    count = LANES // (2 * side)
+    both = [jnp.where(low, a, b) for a, b in zip(first, second)]
+    early = merged([turned(both[g], side + 2 * side * g) for g in range(count)], here)
+    late = merged([turned(both[count + g], 2 * side * g) for g in range(count)], there)
+    return jnp.where(lead, late, early), jnp.where(lead, early, late)
+
+
+def edges_kernel(levels, side, table_ref, cell_ref, *refs):
+    rows_ref, west_ref, east_ref = refs[-3:]
     group = LANES // side
-    halves = cell_ref.shape[2] // LANES
     rounds = cell_ref.shape[1] // levels // group
     level_tiles = levels // SUB
+    rows = rounds * levels
 
     def body(lt, carry):
         for i in range(rounds):
             row = pl.multiple_of(i * levels + lt * SUB, SUB)
-            west = east = None
-            for h in range(halves):
-                cells = []
-                for g in range(group):
-                    at = pl.multiple_of((i * group + g) * levels + lt * SUB, SUB)
-                    cells.append(cell_ref[0, pl.ds(at, SUB), h * LANES : (h + 1) * LANES])
-                west = pack_col(cells, group, side, 0, h * group, west)
-                east = pack_col(cells, group, side, side - 1, h * group, east)
-                if h == 0:
-                    south_ref[0, pl.ds(row, SUB), :] = pack_row(cells, group, side, 0)
-                if h == halves - 1:
-                    north_ref[0, pl.ds(row, SUB), :] = pack_row(cells, group, side, LANES - side)
+            first, second = [], []
+            for g in range(group):
+                at = pl.multiple_of((i * group + g) * levels + lt * SUB, SUB)
+                first.append(cell_ref[0, pl.ds(at, SUB), 0:LANES])
+                second.append(cell_ref[0, pl.ds(at, SUB), LANES : 2 * LANES])
+            west, east = pack_columns(first, second, side)
+            south, north = pack_rows(first, second, side)
             west_ref[0, pl.ds(row, SUB), :] = west
             east_ref[0, pl.ds(row, SUB), :] = east
+            rows_ref[0, pl.ds(row, SUB), :] = south
+            rows_ref[0, pl.ds(pl.multiple_of(rows + row, SUB), SUB), :] = north
         return carry
 
-    lax.fori_loop(0, level_tiles, body, 0)
+    lax.fori_loop(0, level_tiles, body, 0, unroll=True)
 
 
 def edge_shapes(slot_count, lon_count, rows):
     f32 = jnp.float32
     shapes = [
-        jax.ShapeDtypeStruct((lon_count, rows, LANES), f32),
-        jax.ShapeDtypeStruct((lon_count, rows, LANES), f32),
+        jax.ShapeDtypeStruct((lon_count, 2 * rows, LANES), f32),
         jax.ShapeDtypeStruct((slot_count, rows, LANES), f32),
         jax.ShapeDtypeStruct((slot_count, rows, LANES), f32),
     ]
-    by_tile = pl.BlockSpec((1, rows, LANES), lambda s, t: (t[SLOT_TILE, s], 0, 0))
+    by_tile = pl.BlockSpec((1, 2 * rows, LANES), lambda s, t: (t[SLOT_TILE, s], 0, 0))
     by_slot = pl.BlockSpec((1, rows, LANES), lambda s, t: (s, 0, 0))
-    return shapes, [by_tile, by_tile, by_slot, by_slot]
-
-
-def first_edges(table, tracers, levels, side):
+    return shapes, [by_tile, by_slot, by_slot]
+
+
+def first_edges(table, tracers, levels, side, *after):
     slot_count, channels, cell_count = tracers.shape
     lon_count = lax.axis_size("lon")
     rows = channels * side // LANES
@@ -194,12 +218,13 @@
         grid_spec=pltpu.PrefetchScalarGridSpec(
             num_scalar_prefetch=1,
             grid=(slot_count,),
-            in_specs=[pl.BlockSpec((1, channels, cell_count), lambda s, t: (s, 0, 0))],
+            in_specs=[pl.BlockSpec((1, channels, cell_count), lambda s, t: (s, 0, 0))]
+            + [pl.BlockSpec(memory_space=pl.ANY)] * len(after),
             out_specs=specs,
         ),
         compiler_params=pltpu.CompilerParams(vmem_limit_bytes=VMEM_LIMIT),
         name="first_edges",
-    )(table, tracers)
+    )(table, tracers, *after)
 
 
 def react(mixed, par_light, warm_factor):
@@ -293,11 +318,11 @@
 
 def step_kernel(levels, side, last, table_ref, cell_ref, phys_ref, rim_ref, rim_w_ref, rim_e_ref, *refs):
     if last:
-        out_ref, chl_ref, coef_ref, moved_ref = refs
+        out_ref, chl_ref, coef_ref, moved_ref, ends_ref = refs
         edge_refs = ()
     else:
-        out_ref, south_ref, north_ref, west_ref, east_ref, coef_ref, moved_ref = refs
-        edge_refs = (south_ref, north_ref, west_ref, east_ref)
+        out_ref, rows_ref, west_ref, east_ref, coef_ref, moved_ref, ends_ref = refs
+        edge_refs = (rows_ref, west_ref, east_ref)
     channels, cell_count = cell_ref.shape[1:]
     tracer_count = channels // levels
     group = LANES // side
@@ -384,6 +409,10 @@
                 coef_ref[6, at, spans[h]] = mix
                 coef_ref[7, at, spans[h]] = mix_up
 
+        odd = (lane & 1) == 1
+        for at in range(0, rows, SUB):
+            ends_ref[at : at + SUB, :] = turned(rim_w_ref[0, at : at + SUB, :], 2 - 2 * side)
+
         blank = jnp.zeros((SUB, cell_count), jnp.float32)
         moved_ref[0:SUB, :] = blank
         moved_ref[SUB + channels : 2 * SUB + channels, :] = blank
@@ -393,30 +422,35 @@
             coef = [[coef_ref[n, pl.ds(at, SUB), spans[h]] for n in range(5)] for h in range(halves)]
             for i in range(rounds):
                 row = pl.multiple_of(i * levels + lt * SUB, SUB)
-                rim_s = rim_ref[0, pl.ds(row, SUB), :]
-                rim_n = rim_ref[0, pl.ds(pl.multiple_of(rows + row, SUB), SUB), :]
-                rim_w = rim_w_ref[0, pl.ds(row, SUB), :]
-                rim_e = rim_e_ref[0, pl.ds(row, SUB), :]
+                rims = [
+                    rim_ref[0, pl.ds(row, SUB), :],
+                    rim_ref[0, pl.ds(pl.multiple_of(rows + row, SUB), SUB), :],
+                ]
+                ends_w = ends_ref[pl.ds(row, SUB), :]
+                ends_e = rim_e_ref[0, pl.ds(row, SUB), :]
+                sides = [jnp.where(odd, ends_e, ends_w), jnp.where(odd, ends_w, ends_e)]
                 for g in range(group):
                     chan = pl.multiple_of((i * group + g) * levels + lt * SUB, SUB)
                     here = [cell_ref[0, pl.ds(chan, SUB), spans[h]] for h in range(halves)]
-                    south = southward(here, turned(rim_s, -side * g))
-                    north = northward(here, turned(rim_n, LANES - side - side * g))
+                    rim = turned(rims[2 * g // group], -side - 2 * side * (g % (group // 2)))
+                    south = southward(here, rim)
+                    north = northward(here, rim)
                     for h in range(halves):
-                        at_w = h * group + g
-                        west = jnp.where(first_col, turned(rim_w, -at_w), turned(here[h], 1))
-                        east = jnp.where(last_col, turned(rim_e, side - 1 - at_w), turned(here[h], -1))
+                        ends = turned(sides[h], side - 2 + h - 2 * g)
+                        west = jnp.where(first_col, ends, turned(here[h], 1))
+                        east = jnp.where(last_col, ends, turned(here[h], -1))
                         c, e, w, n, s = coef[h]
                         moved_ref[pl.ds(pl.multiple_of(SUB + chan, SUB), SUB), spans[h]] = (
                             c * here[h] + (e * east + w * west) + (n * north[h] + s * south[h])
                         )
             return carry
 
-        lax.fori_loop(0, level_tiles, advect, 0)
+        lax.fori_loop(0, level_tiles, advect, 0, unroll=True)
 
         def reacting(lt, carry):
             at = pl.multiple_of(lt * SUB, SUB)
             depths = []
+            halves_new = []
             for h in range(halves):
                 mix_c, mix_d, mix_u = (coef_ref[n, pl.ds(at, SUB), spans[h]] for n in (5, 6, 7))
                 mixed = []
@@ -447,24 +481,21 @@
                     chl_ref[0, pl.ds(at, SUB), spans[h]] = positive(new[nano_chl_index]) + positive(
                         new[diat_chl_index]
                     )
-                else:
-                    for i in range(rounds):
-                        row = pl.multiple_of(i * levels + lt * SUB, SUB)
-                        cells = new[i * group : (i + 1) * group]
-                        west = None if h == 0 else west_ref[0, pl.ds(row, SUB), :]
-                        east = None if h == 0 else east_ref[0, pl.ds(row, SUB), :]
-                        west_ref[0, pl.ds(row, SUB), :] = pack_col(cells, group, side, 0, h * group, west)
-                        east_ref[0, pl.ds(row, SUB), :] = pack_col(
-                            cells, group, side, side - 1, h * group, east
-                        )
-                        if h == 0:
-                            south_ref[0, pl.ds(row, SUB), :] = pack_row(cells, group, side, 0)
-                        if h == halves - 1:
-                            north_ref[0, pl.ds(row, SUB), :] = pack_row(cells, group, side, LANES - side)
+                halves_new.append(new)
+            if not last:
+                for i in range(rounds):
+                    row = pl.multiple_of(i * levels + lt * SUB, SUB)
+                    first, second = (new[i * group : (i + 1) * group] for new in halves_new)
+                    west, east = pack_columns(first, second, side)
+                    south, north = pack_rows(first, second, side)
+                    west_ref[0, pl.ds(row, SUB), :] = west
+                    east_ref[0, pl.ds(row, SUB), :] = east
+                    rows_ref[0, pl.ds(row, SUB), :] = south
+                    rows_ref[0, pl.ds(pl.multiple_of(rows + row, SUB), SUB), :] = north
             return tuple(depths)
 
         start = tuple(jnp.zeros((1, LANES), jnp.float32) for _ in range(halves))
-        lax.fori_loop(0, level_tiles, reacting, start)
+        lax.fori_loop(0, level_tiles, reacting, start, unroll=True)
 
 
 def step(table, cells, phys, rims, rim_w, rim_e, levels, side, last):
@@ -500,6 +531,7 @@
             scratch_shapes=[
                 pltpu.VMEM((8, levels, cell_count), f32),
                 pltpu.VMEM((channels + 2 * SUB, cell_count), f32),
+                pltpu.VMEM((rows, LANES), f32),
             ],
         ),
         compiler_params=pltpu.CompilerParams(vmem_limit_bytes=VMEM_LIMIT),
@@ -654,25 +686,33 @@
 
 
 def owner_of(codes, block, slot_count, lon_count):
-    return lax.rem(lax.div(jnp.maximum(codes[0, block], 0), slot_count), lon_count)
-
-
-def hand_kernel(table_ref, below_ref, above_ref, south_ref, north_ref, out_ref):
+    return remainder(quotient(jnp.maximum(codes[0, block], 0), slot_count), lon_count)
+
+
+def hand_kernel(side, table_ref, below_ref, above_ref, south_ref, north_ref, *refs):
+    out_ref = refs[-1]
     b = pl.program_id(0)
     rows = south_ref.shape[1]
     block = table_ref[TILE_BASE, 0] + b
-    out_ref[0, 0:rows, :] = jnp.where(below_ref[0, block] >= 0, south_ref[0], 0.0)
-    out_ref[0, rows : 2 * rows, :] = jnp.where(above_ref[0, block] >= 0, north_ref[0], 0.0)
-
-
-def hand_on(table, codes_below, codes_above, from_south, from_north, slot_count, tile_blocks):
+    lead = (lane_ids(rows) & side) == 0
+    south = jnp.where(below_ref[0, block] >= 0, south_ref[0], 0.0)
+    north = jnp.where(above_ref[0, block] >= 0, north_ref[0], 0.0)
+    out_ref[0, 0:rows, :] = jnp.where(lead, turned(north, -side), turned(south, side))
+    out_ref[0, rows : 2 * rows, :] = jnp.where(lead, north, turned(south, 2 * side))
+
+
+def hand_on(
+    table, codes_below, codes_above, from_south, from_north, joined, side, slot_count, tile_blocks, *after
+):
     lon_count, rows, width = from_south.shape
+    if joined:
+        rows = rows // 2
 
     def spot(t, b):
         return t[TILE_BASE, 0] + b
 
     return pl.pallas_call(
-        hand_kernel,
+        functools.partial(hand_kernel, side),
         out_shape=jax.ShapeDtypeStruct((lon_count, 2 * rows, width), jnp.float32),
         grid_spec=pltpu.PrefetchScalarGridSpec(
             num_scalar_prefetch=3,
@@ -684,14 +724,31 @@
                 ),
                 pl.BlockSpec(
                     (1, rows, width),
-                    lambda b, t, lo, hi: (owner_of(hi, spot(t, b), slot_count, lon_count), 0, 0),
+                    lambda b, t, lo, hi: (owner_of(hi, spot(t, b), slot_count, lon_count), int(joined), 0),
                 ),
-            ],
+            ]
+            + [pl.BlockSpec(memory_space=pl.ANY)] * len(after),
             out_specs=pl.BlockSpec((1, 2 * rows, width), lambda b, t, lo, hi: (t[TILE_OWNER, b], 0, 0)),
         ),
         compiler_params=pltpu.CompilerParams(vmem_limit_bytes=VMEM_LIMIT),
         name="hand_on",
-    )(table, codes_below, codes_above, from_south, from_north)
+    )(table, codes_below, codes_above, from_south, from_north, *after)
+
+
+def gate_kernel(*refs):
+    pass
+
+
+def gate(x, *others):
+    anywhere = pl.BlockSpec(memory_space=pl.ANY)
+    return pl.pallas_call(
+        gate_kernel,
+        out_shape=jax.ShapeDtypeStruct(x.shape, x.dtype),
+        in_specs=[anywhere] * (1 + len(others)),
+        out_specs=anywhere,
+        input_output_aliases={0: 0},
+        name="gate",
+    )(x, *others)
 
 
 def heat_kernel(levels, side, factor, table_ref, chl_ref, light_ref, land_ref, widen_ref, out_ref, rows_ref, wide_ref):
@@ -777,6 +834,29 @@
         compiler_params=pltpu.CompilerParams(vmem_limit_bytes=VMEM_LIMIT),
         name="heat",
     )(table, chl, light, land, widen)
+
+
+def part_kernel(rows, both_ref, *refs):
+    south_ref, north_ref = refs[-2:]
+    south_ref[...] = both_ref[:, 0:rows, :]
+    north_ref[...] = both_ref[:, rows : 2 * rows, :]
+
+
+def part(both, *after):
+    count, rows, width = both.shape
+    rows = rows // 2
+    half = jax.ShapeDtypeStruct((count, rows, width), both.dtype)
+    spec = pl.BlockSpec((1, rows, width), lambda i: (i, 0, 0))
+    return pl.pallas_call(
+        functools.partial(part_kernel, rows),
+        out_shape=[half, half],
+        grid=(count,),
+        in_specs=[pl.BlockSpec((1, 2 * rows, width), lambda i: (i, 0, 0))]
+        + [pl.BlockSpec(memory_space=pl.ANY)] * len(after),
+        out_specs=[spec, spec],
+        compiler_params=pltpu.CompilerParams(vmem_limit_bytes=VMEM_LIMIT),
+        name="part",
+    )(both, *after)
 
 
 def widened(x, rows, width):
@@ -833,28 +913,60 @@
     picks = jnp.concatenate([final, member], axis=1)
 
     table = routing(owner_map, slot_count, tile_blocks)
-    south, north, west, east = first_edges(table, tracers, levels, side)
+    edge_rows, west, east = first_edges(
+        table, tracers, levels, side, from_south, from_north, from_west, from_east
+    )
     phys = coarsen(
         table, fine, mix, surf_light, land_mask, from_south, from_north, from_west, from_east, picks
     )
+    rows = edge_rows.shape[1] // 2
+
+    def hand(from_south, from_north, joined, *after):
+        handed = hand_on(
+            table,
+            codes_below,
+            codes_above,
+            from_south,
+            from_north,
+            joined,
+            side,
+            slot_count,
+            tile_blocks,
+            *after,
+        )
+        return lax.all_to_all(handed, "lon", 0, 0, tiled=True)
+
+    def to_north(x):
+        return lax.ppermute(x, "lat", along("lat", 1, False))
+
+    def to_south(x):
+        return lax.ppermute(x, "lat", along("lat", -1, False))
+
+    def beside(west, east):
+        return (
+            lax.ppermute(east, "lon", along("lon", 1, True)),
+            lax.ppermute(west, "lon", along("lon", -1, True)),
+        )
+
+    rim_w, rim_e = beside(west, east)
+    tile_rows = lax.all_to_all(edge_rows, "lon", 0, 0, tiled=True)
+    phys = gate(phys, rim_w, rim_e, tile_rows)
+    south, north = part(tile_rows, phys)
     phys = lax.all_to_all(phys, "lon", 0, 0, tiled=True)
+    rims = hand(to_north(north), to_south(south), False)
 
     current = tracers
     for step_index in range(ITERS):
-        rim_w = lax.ppermute(east, "lon", along("lon", 1, True))
-        rim_e = lax.ppermute(west, "lon", along("lon", -1, True))
-        rim_s = lax.ppermute(north, "lat", along("lat", 1, False))
-        rim_n = lax.ppermute(south, "lat", along("lat", -1, False))
-        rim_s = lax.all_to_all(rim_s, "lon", 0, 0, tiled=True)
-        rim_n = lax.all_to_all(rim_n, "lon", 0, 0, tiled=True)
-        rims = hand_on(table, codes_below, codes_above, rim_s, rim_n, slot_count, tile_blocks)
-        rims = lax.all_to_all(rims, "lon", 0, 0, tiled=True)
         last = step_index == ITERS - 1
         got = step(table, current, phys, rims, rim_w, rim_e, levels, side, last)
         if last:
             current, chl = got
-        else:
-            current, south, north, west, east = got
+            break
+        current, edge_rows, west, east = got
+        rim_w, rim_e = beside(west, east)
+        moved_rows = jnp.concatenate([to_north(edge_rows[:, rows:]), to_south(edge_rows[:, :rows])], axis=1)
+        tile_rows = lax.all_to_all(moved_rows, "lon", 0, 0, tiled=True)
+        rims = hand(tile_rows, tile_rows, True, rim_w, rim_e)
     chl = lax.all_to_all(chl, "lon", 0, 0, tiled=True)
     heating = heat(table, chl, surf_light, land_mask, levels, jnp.transpose(member))
     return current, heating

time: 360 us -> 312 us (0.87); the launches traced: 362 us -> 309 us
  blocking collectives: 23 us -> 109 us
  waiting for transfers between devices: 140 us -> 70.4 us
  Pallas kernels: 113 us -> 77.3 us
  starting transfers between devices: 69.8 us -> 38.9 us
  local copies, waits for them, and re-layouts: 12.7 us -> 7.16 us
    all_to_all x1 -> x3, blocking collectives: 23 us -> 109 us  [the longest x2 64.8 us: hand(): return lax.all_to_all(handed, 'lon', 0, 0, tiled=True)]
    all_to_all x6 -> x2, waiting for transfers between devices: 42.4 us -> 0.01 us  [the longest x1 0.01 us: on_device(): tile_rows = lax.all_to_all(edge_rows, 'lon', 0, 0, tiled=True)]
    pallas_call x2, Pallas kernels: 70.5 us -> 38.8 us  [step(): pl.pallas_call(functools.partial(step_kernel, levels, side, last), out_sh...]
    all_to_all x6 -> x2, starting transfers between devices: 32.4 us -> 7.94 us  [the longest x1 4.37 us: on_device(): tile_rows = lax.all_to_all(edge_rows, 'lon', 0, 0, tiled=True)]
    ppermute x8, waiting for transfers between devices: 82 us -> 58 us  [the longest x2 47.1 us: beside(): lax.ppermute(east, 'lon', along('lon', 1, True))]
    ppermute x1, starting transfers between devices: 9.1 us -> 2.36 us  [on_device(): from_south = lax.ppermute(northward, 'lat', along('lat', 1, False))]
    unnamed x51 -> x31, local copies, waits for them, and re-layouts: 12.3 us -> 6.64 us
  transfers between devices with their start and end apart: 19 -> 15, of which waited for: 12 -> 9; matrix products, arithmetic and copies ran while one was open for 1% -> 1% of each run, Pallas kernels for 5% -> 6%
where the time goes in v1:
time: 312 us; the launch traced here: 309 us
  blocking collectives  109 us (35%)
  Pallas kernels  77.3 us (25%)
  waiting for transfers between devices  70.4 us (23%)
  starting transfers between devices  38.9 us (12%)
  local copies, waits for them, and re-layouts  7.16 us (2%)
  other arithmetic  5.14 us (2%)
    all_to_all x2, blocking collectives, hand(): return lax.all_to_all(handed, 'lon', 0, 0, tiled=True)  64.8 us
    ppermute x2, waiting for transfers between devices, beside(): lax.ppermute(east, 'lon', along('lon', 1, True))  47.1 us
    all_to_all x1, blocking collectives, on_device(): phys = lax.all_to_all(phys, 'lon', 0, 0, tiled=True)  44.5 us
    pallas_call x2, Pallas kernels, step(): pl.pallas_call(functools.partial(step_kernel, levels, side, last), out_sh...  38.8 us
    pallas_call x1, Pallas kernels, coarsen(): pl.pallas_call(functools.partial(coarsen_kernel, levels, side, factor), o...  16.8 us
    all_to_all x1, waiting for transfers between devices, on_device(): chl = lax.all_to_all(chl, 'lon', 0, 0, tiled=True)  12.4 us
    pallas_call x1, Pallas kernels, first_edges(): pl.pallas_call(functools.partial(edges_kernel, levels, side), out_shape=s...  9.46 us
    unnamed x31, local copies, waits for them, and re-layouts  6.64 us
  transfers between devices with their start and end apart: 15, of which 9 were waited for; matrix products, arithmetic and copies ran while one was open for 1% of the time, Pallas kernels for 6%

profile of v1, /device:TPU:0, one launch (start us, length us, event | category | flops | bytes accessed | tf_op | source)
XLA Modules:
  0.0 309.3 jit_solution(11556698960055969955)
XLA Ops:
  2.8 2.4 collective-permute-start
  5.2 1.6 convert_reduce_fusion
  7.5 2.4 collective-permute-start.2
  11.2 3.1 %collective-permute-start.3 = (f32[1,128]{1,0:T(1,128)S(1)}, f32[1,128]{1,0:T(1,128)S(1)}, u32[]{:S(2)}, u32[]{:S(2)}) collective-permute-start(f32[1,128]{1,0:T(1,128)S(1)} %pad.28), channel_id=1, source_target_pairs={{0,7},{1,0},{2,1},{3,2},{4,3},{5,4},{6,5},{7,6},{8,15},{9,8},{10,9... | collective-permute-start | bytes 1544 | tf_op jit(solution)/shard_map/ppermute | solution.py:905
  14.3 3.2 %routing.1.table_ref = s32[8,8]{1,0:T(8,128)} custom-call(s32[1,64]{1,0:T(1,128)} %row_ref.1), custom_call_target="tpu_custom_call" | custom-call | tf_op jit(solution)/shard_map/routing/pallas_call | solution.py:132
  18.3 9.5 %first_edges.1 = (f32[8,288,128]{2,1,0:T(8,128)}, f32[8,144,128]{2,1,0:T(8,128)S(1)}, f32[8,144,128]{2,1,0:T(8,128)}) custom-call(s32[8,8]{1,0:T(8,128)S(1)} %copy-done.11, f32[8,1152,256]{2,1,0:T(8,128)} %cell_ref.3, f32[50,384]{1,0:T(8,128)S(1)} %collective-permute-done.south_ref.refs_0_, f32[2,384]{1,0:T(2,128)S(1)} %collective-permute-done.1.north_ref.refs_1_, ...), custom_call_target="tpu_custom_call" | custom-call | tf_op jit(solution)/shard_map/first_edges/pallas_call | solution.py:215
  27.8 4.4 %all-to-all-start = ((f32[8,288,128]{2,1,0:T(8,128)}), f32[8,288,128]{2,1,0:T(8,128)S(1)}, u32[]{:S(2)}, u32[]{:S(2)}) async-start(f32[8,288,128]{2,1,0:T(8,128)} %get-tuple-element.15), calls=%async_computation | async-start | bytes 2359296 | tf_op jit(solution)/shard_map/all_to_all | solution.py:952
  32.2 2.0 collective-permute-start.4
  34.2 2.7 collective-permute-start.5
  37.1 16.8 %coarsen.1.refs_0_ = f32[8,208,256]{2,1,0:T(8,128)S(1)} custom-call(s32[8,8]{1,0:T(8,128)S(1)} %copy-done.12, bf16[48,144,384]{2,1,0:T(8,128)(2,1)} %bitcast.13, bf16[16,48,128]{2,1,0:T(8,128)(2,1)S(1)} %bitcast.10, f32[48,384]{1,0:T(8,128)S(1)} %copy-done.10, s32[16,128]{1,0:T(8,128)S(1)} %copy-done.14, ...), custom_call_target="tpu_custom_call" | custom-call | tf_op jit(solution)/shard_map/coarsen/pallas_call | solution.py:663
  55.1 15.8 %collective-permute-done.4.refs_1_.rim_w_ref = f32[8,144,128]{2,1,0:T(8,128)S(1)} collective-permute-done((f32[8,144,128]{2,1,0:T(8,128)}, f32[8,144,128]{2,1,0:T(8,128)S(1)}, u32[]{:S(2)}, u32[]{:S(2)}) %collective-permute-start.4) | collective-permute-done | bytes 589856 | tf_op jit(solution)/shard_map/ppermute | solution.py:947
  70.9 2.7 collective-permute-done.5.refs_2_.rim_e_ref
  75.4 1.5 copy-done.1
  78.3 2.1 collective-permute-start.6
  81.9 2.6 collective-permute-done.7.north_ref
  84.6 1.7 hand_on.2
  86.3 31.4 %all_to_all.30.rim_ref = f32[8,288,128]{2,1,0:T(8,128)S(1)} all-to-all(f32[8,288,128]{2,1,0:T(8,128)S(1)} %hand_on.2), channel_id=1, replica_groups=mesh['lat'=4,'lon'=8] {'lon'}, dimensions={0} | all-to-all | bytes 2359296 | tf_op jit(solution)/shard_map/all_to_all | solution.py:937
  117.7 44.5 %all_to_all.31.phys_ref = f32[8,208,256]{2,1,0:T(8,128)} all-to-all(f32[8,208,256]{2,1,0:T(8,128)S(1)} %copy-done.2), channel_id=1, replica_groups=mesh['lat'=4,'lon'=8] {'lon'}, dimensions={0} | all-to-all | bytes 3407872 | tf_op jit(solution)/shard_map/all_to_all | solution.py:955
  162.3 20.4 %step.2 = (f32[8,1152,256]{2,1,0:T(8,128)}, f32[8,288,128]{2,1,0:T(8,128)S(1)}, f32[8,144,128]{2,1,0:T(8,128)S(1)}, f32[8,144,128]{2,1,0:T(8,128)}) custom-call(s32[8,8]{1,0:T(8,128)S(1)} %copy-done.12, f32[8,1152,256]{2,1,0:T(8,128)} %cell_ref.3, f32[8,208,256]{2,1,0:T(8,128)} %all_to_all.31.phys_ref, f32[8,288,128]{2,1,0:T(8,128)S(1)} %all_to_all.30.rim_ref, ...), custom_call_target="tpu_custom_call" | custom-call | tf_op jit(solution)/shard_map/step/pallas_call | solution.py:517
  182.8 3.2 %collective-permute-start.8 = (f32[8,144,128]{2,1,0:T(8,128)S(1)}, f32[8,144,128]{2,1,0:T(8,128)S(1)}, u32[]{:S(2)}, u32[]{:S(2)}) collective-permute-start(f32[8,144,128]{2,1,0:T(8,128)S(1)} %get-tuple-element.26), channel_id=1, source_target_pairs={{0,8},{8,16},{16,24},{1,9},{9,17},{17,25},{2,10},{10,18},{18,26},{... | collective-permute-start | bytes 1769480 | tf_op jit(solution)/shard_map/ppermute | solution.py:940
  187.6 2.3 collective-permute-done.9
  191.0 3.6 %all-to-all-start.3 = ((f32[8,288,128]{2,1,0:T(8,128)}), f32[8,288,128]{2,1,0:T(8,128)S(1)}, u32[]{:S(2)}, u32[]{:S(2)}) async-start(f32[8,288,128]{2,1,0:T(8,128)} %pad_maximum_fusion), calls=%async_computation.3 | async-start | bytes 2359296 | tf_op jit(solution)/shard_map/all_to_all | solution.py:968
  194.6 1.9 collective-permute-start.10
  196.5 2.9 collective-permute-start.11
  199.4 31.4 %collective-permute-done.10.refs_0_.rim_w_ref = f32[8,144,128]{2,1,0:T(8,128)S(1)} collective-permute-done((f32[8,144,128]{2,1,0:T(8,128)}, f32[8,144,128]{2,1,0:T(8,128)S(1)}, u32[]{:S(2)}, u32[]{:S(2)}) %collective-permute-start.10) | collective-permute-done | bytes 589856 | tf_op jit(solution)/shard_map/ppermute | solution.py:947
  230.7 2.7 collective-permute-done.11.refs_1_.rim_e_ref
  233.5 1.7 hand_on.3
  235.2 33.4 %all_to_all.32.rim_ref = f32[8,288,128]{2,1,0:T(8,128)S(1)} all-to-all(f32[8,288,128]{2,1,0:T(8,128)S(1)} %hand_on.3), channel_id=1, replica_groups=mesh['lat'=4,'lon'=8] {'lon'}, dimensions={0} | all-to-all | bytes 2359296 | tf_op jit(solution)/shard_map/all_to_all | solution.py:937
  268.6 18.4 %step.3 = (f32[8,1152,256]{2,1,0:T(8,128)}, f32[8,48,256]{2,1,0:T(8,128)}) custom-call(s32[8,8]{1,0:T(8,128)S(1)} %copy-done.12, f32[8,1152,256]{2,1,0:T(8,128)} %get-tuple-element.18.cell_ref, f32[8,208,256]{2,1,0:T(8,128)S(1)} %copy-done.3, f32[8,288,128]{2,1,0:T(8,128)S(1)} %all_to_all.32.rim_ref, ...), custom_call_target="tpu_custom_call" | custom-call | tf_op jit(solution)/shard_map/step/pallas_call | solution.py:517
  286.9 4.4 %all-to-all-start.5 = ((f32[8,48,256]{2,1,0:T(8,128)}), f32[8,48,256]{2,1,0:T(8,128)S(1)}, u32[]{:S(2)}, u32[]{:S(2)}) async-start(f32[8,48,256]{2,1,0:T(8,128)} %get-tuple-element.23), calls=%async_computation.5 | async-start | bytes 786432 | tf_op jit(solution)/shard_map/all_to_all | solution.py:970
  291.4 12.4 %all-to-all-done.5.chl_ref = f32[8,48,256]{2,1,0:T(8,128)S(1)} async-done(((f32[8,48,256]{2,1,0:T(8,128)}), f32[8,48,256]{2,1,0:T(8,128)S(1)}, u32[]{:S(2)}, u32[]{:S(2)}) %all-to-all-start.5) | async-done | bytes 393248 | tf_op jit(solution)/shard_map/all_to_all | solution.py:970
  303.8 5.4 %heat.1 = bf16[48,48,384]{2,1,0:T(8,128)(2,1)} custom-call(s32[8,8]{1,0:T(8,128)S(1)} %copy-done.12, f32[8,48,256]{2,1,0:T(8,128)S(1)} %all-to-all-done.5.chl_ref, f32[48,384]{1,0:T(8,128)S(1)} %copy-done.10, s32[16,128]{1,0:T(8,128)S(1)} %copy-done.14, bf16[128,384]{1,0:T(8,128)(2,1)S(1)} %fusion.widen_ref), custom_call_target="tpu_custom_call" | custom-call | tf_op jit(solution)/shard_map/heat/pallas_call | solution.py:825
  (68 shorter events, 13.8 us)
Async XLA Ops:
  2.8 14.8 %collective-permute-start = (f32[50,384]{1,0:T(8,128)S(1)}, f32[50,384]{1,0:T(8,128)S(1)}, u32[]{:S(2)}, u32[]{:S(2)}) collective-permute-start(f32[50,384]{1,0:T(8,128)S(1)} %fusion.1), channel_id=1, source_target_pairs={{0,8},{8,16},{16,24},{1,9},{9,17},{17,25},{2,10},{10,18},{18,26},{... | collective-permute-start | bytes 230408 | tf_op jit(solution)/shard_map/ppermute | solution.py:902
  7.5 10.1 %collective-permute-start.2 = (f32[9,128]{1,0:T(8,128)S(1)}, f32[9,128]{1,0:T(8,128)S(1)}, u32[]{:S(2)}, u32[]{:S(2)}) collective-permute-start(f32[9,128]{1,0:T(8,128)S(1)} %select_maximum_fusion.1), channel_id=1, source_target_pairs={{0,1},{1,2},{2,3},{3,4},{4,5},{5,6},{6,7},{7,0},{8,9},{9,10},{10,1... | collective-permute-start | bytes 13832 | tf_op jit(solution)/shard_map/ppermute | solution.py:904
  9.9 7.7 %collective-permute-start.1 = (f32[2,384]{1,0:T(2,128)S(1)}, f32[2,384]{1,0:T(2,128)S(1)}, u32[]{:S(2)}, u32[]{:S(2)}) collective-permute-start(f32[2,384]{1,0:T(2,128)S(1)} %fusion.4), channel_id=1, source_target_pairs={{8,0},{16,8},{24,16},{9,1},{17,9},{25,17},{10,2},{18,10},{26,18},{... | collective-permute-start | bytes 9224 | tf_op jit(solution)/shard_map/ppermute | solution.py:903
  11.2 6.4 %collective-permute-start.3 = (f32[1,128]{1,0:T(1,128)S(1)}, f32[1,128]{1,0:T(1,128)S(1)}, u32[]{:S(2)}, u32[]{:S(2)}) collective-permute-start(f32[1,128]{1,0:T(1,128)S(1)} %pad.28), channel_id=1, source_target_pairs={{0,7},{1,0},{2,1},{3,2},{4,3},{5,4},{6,5},{7,6},{8,15},{9,8},{10,9... | collective-permute-start | bytes 1544 | tf_op jit(solution)/shard_map/ppermute | solution.py:905
  17.6 0.7 copy-start.11
  27.8 9.3 %copy-start.10 = (f32[48,384]{1,0:T(8,128)S(1)}, f32[48,384]{1,0:T(8,128)}, u32[]{:S(2)}) copy-start(f32[48,384]{1,0:T(8,128)} %light_ref.3) | copy-start | bytes 221188
  27.8 9.3 %copy-start.12 = (s32[8,8]{1,0:T(8,128)S(1)}, s32[8,8]{1,0:T(8,128)}, u32[]{:S(2)}) copy-start(s32[8,8]{1,0:T(8,128)} %routing.1.table_ref) | copy-start | bytes 772
  27.8 9.4 %copy-start.13 = (bf16[16,128,48]{1,2,0:T(8,128)(2,1)S(1)}, bf16[16,128,48]{1,2,0:T(8,128)(2,1)}, u32[]{:S(2)}) copy-start(bf16[16,128,48]{1,2,0:T(8,128)(2,1)} %param.8) | copy-start | bytes 589828
  27.8 9.4 %copy-start.14 = (s32[16,128]{1,0:T(8,128)S(1)}, s32[16,128]{1,0:T(8,128)}, u32[]{:S(2)}) copy-start(s32[16,128]{1,0:T(8,128)} %land_ref.3) | copy-start | bytes 24580
  27.8 45.8 %all-to-all-start = ((f32[8,288,128]{2,1,0:T(8,128)}), f32[8,288,128]{2,1,0:T(8,128)S(1)}, u32[]{:S(2)}, u32[]{:S(2)}) async-start(f32[8,288,128]{2,1,0:T(8,128)} %get-tuple-element.15), calls=%async_computation | async-start | bytes 2359296 | tf_op jit(solution)/shard_map/all_to_all | solution.py:952
  32.2 38.7 %collective-permute-start.4 = (f32[8,144,128]{2,1,0:T(8,128)}, f32[8,144,128]{2,1,0:T(8,128)S(1)}, u32[]{:S(2)}, u32[]{:S(2)}) collective-permute-start(f32[8,144,128]{2,1,0:T(8,128)} %get-tuple-element.13), channel_id=1, source_target_pairs={{0,1},{1,2},{2,3},{3,4},{4,5},{5,6},{6,7},{7,0},{8,9},{9,10},{10,1... | collective-permute-start | bytes 1769480 | tf_op jit(solution)/shard_map/ppermute | solution.py:947
  34.2 39.4 %collective-permute-start.5 = (f32[8,144,128]{2,1,0:T(8,128)S(1)}, f32[8,144,128]{2,1,0:T(8,128)S(1)}, u32[]{:S(2)}, u32[]{:S(2)}) collective-permute-start(f32[8,144,128]{2,1,0:T(8,128)S(1)} %get-tuple-element.14), channel_id=1, source_target_pairs={{0,7},{1,0},{2,1},{3,2},{4,3},{5,4},{6,5},{7,6},{8,15},{9,8},{10,9... | collective-permute-start | bytes 1769480 | tf_op jit(solution)/shard_map/ppermute | solution.py:948
  53.9 1.2 copy-start
  70.9 2.7 copy-start.6
  73.6 0.8 copy-start.8
  74.4 1.0 copy-start.4
  75.4 1.5 copy-start.1
  76.8 1.3 copy-start.5
  78.3 3.6 %collective-permute-start.6 = (f32[8,144,128]{2,1,0:T(8,128)S(1)}, f32[8,144,128]{2,1,0:T(8,128)S(1)}, u32[]{:S(2)}, u32[]{:S(2)}) collective-permute-start(f32[8,144,128]{2,1,0:T(8,128)S(1)} %get-tuple-element.16), channel_id=1, source_target_pairs={{0,8},{8,16},{16,24},{1,9},{9,17},{17,25},{2,10},{10,18},{18,26},{... | collective-permute-start | bytes 1769480 | tf_op jit(solution)/shard_map/ppermute | solution.py:940
  80.4 4.2 %collective-permute-start.7 = (f32[8,144,128]{2,1,0:T(8,128)S(1)}, f32[8,144,128]{2,1,0:T(8,128)S(1)}, u32[]{:S(2)}, u32[]{:S(2)}) collective-permute-start(f32[8,144,128]{2,1,0:T(8,128)S(1)} %get-tuple-element.17), channel_id=1, source_target_pairs={{8,0},{16,8},{24,16},{9,1},{17,9},{25,17},{10,2},{18,10},{26,18},{... | collective-permute-start | bytes 1769480 | tf_op jit(solution)/shard_map/ppermute | solution.py:943
  86.3 31.4 %copy-start.2 = (f32[8,208,256]{2,1,0:T(8,128)S(1)}, f32[8,208,256]{2,1,0:T(8,128)}, u32[]{:S(2)}) copy-start(f32[8,208,256]{2,1,0:T(8,128)} %gate.1.refs_0_) | copy-start | bytes 5111812
  117.7 44.6 %copy-start.7 = (f32[8,144,128]{2,1,0:T(8,128)S(1)}, f32[8,144,128]{2,1,0:T(8,128)}, u32[]{:S(2)}) copy-start(f32[8,144,128]{2,1,0:T(8,128)} %copy-done.6) | copy-start | bytes 1769476
  117.7 44.6 %copy-start.9 = (f32[8,144,128]{2,1,0:T(8,128)S(1)}, f32[8,144,128]{2,1,0:T(8,128)}, u32[]{:S(2)}) copy-start(f32[8,144,128]{2,1,0:T(8,128)} %copy-done.8) | copy-start | bytes 1769476
  182.8 4.8 %collective-permute-start.8 = (f32[8,144,128]{2,1,0:T(8,128)S(1)}, f32[8,144,128]{2,1,0:T(8,128)S(1)}, u32[]{:S(2)}, u32[]{:S(2)}) collective-permute-start(f32[8,144,128]{2,1,0:T(8,128)S(1)} %get-tuple-element.26), channel_id=1, source_target_pairs={{0,8},{8,16},{16,24},{1,9},{9,17},{17,25},{2,10},{10,18},{18,26},{... | collective-permute-start | bytes 1769480 | tf_op jit(solution)/shard_map/ppermute | solution.py:940
  186.1 3.9 %collective-permute-start.9 = (f32[8,144,128]{2,1,0:T(8,128)S(1)}, f32[8,144,128]{2,1,0:T(8,128)S(1)}, u32[]{:S(2)}, u32[]{:S(2)}) collective-permute-start(f32[8,144,128]{2,1,0:T(8,128)S(1)} %get-tuple-element.27), channel_id=1, source_target_pairs={{8,0},{16,8},{24,16},{9,1},{17,9},{25,17},{10,2},{18,10},{26,18},{... | collective-permute-start | bytes 1769480 | tf_op jit(solution)/shard_map/ppermute | solution.py:943
  191.0 42.4 %all-to-all-start.3 = ((f32[8,288,128]{2,1,0:T(8,128)}), f32[8,288,128]{2,1,0:T(8,128)S(1)}, u32[]{:S(2)}, u32[]{:S(2)}) async-start(f32[8,288,128]{2,1,0:T(8,128)} %pad_maximum_fusion), calls=%async_computation.3 | async-start | bytes 2359296 | tf_op jit(solution)/shard_map/all_to_all | solution.py:968
  194.6 36.1 %collective-permute-start.10 = (f32[8,144,128]{2,1,0:T(8,128)}, f32[8,144,128]{2,1,0:T(8,128)S(1)}, u32[]{:S(2)}, u32[]{:S(2)}) collective-permute-start(f32[8,144,128]{2,1,0:T(8,128)} %get-tuple-element.20), channel_id=1, source_target_pairs={{0,1},{1,2},{2,3},{3,4},{4,5},{5,6},{6,7},{7,0},{8,9},{9,10},{10,1... | collective-permute-start | bytes 1769480 | tf_op jit(solution)/shard_map/ppermute | solution.py:947
  196.5 36.9 %collective-permute-start.11 = (f32[8,144,128]{2,1,0:T(8,128)S(1)}, f32[8,144,128]{2,1,0:T(8,128)S(1)}, u32[]{:S(2)}, u32[]{:S(2)}) collective-permute-start(f32[8,144,128]{2,1,0:T(8,128)S(1)} %get-tuple-element.21), channel_id=1, source_target_pairs={{0,7},{1,0},{2,1},{3,2},{4,3},{5,4},{6,5},{7,6},{8,15},{9,8},{10,9... | collective-permute-start | bytes 1769480 | tf_op jit(solution)/shard_map/ppermute | solution.py:948
  235.2 33.4 %copy-start.3 = (f32[8,208,256]{2,1,0:T(8,128)S(1)}, f32[8,208,256]{2,1,0:T(8,128)}, u32[]{:S(2)}) copy-start(f32[8,208,256]{2,1,0:T(8,128)} %all_to_all.31.phys_ref) | copy-start | bytes 5111812
  286.9 16.9 %all-to-all-start.5 = ((f32[8,48,256]{2,1,0:T(8,128)}), f32[8,48,256]{2,1,0:T(8,128)S(1)}, u32[]{:S(2)}, u32[]{:S(2)}) async-start(f32[8,48,256]{2,1,0:T(8,128)} %get-tuple-element.23), calls=%async_computation.5 | async-start | bytes 786432 | tf_op jit(solution)/shard_map/all_to_all | solution.py:970

commit v2 on v1

v2 whole, which is shorter than its diff:
```python
import functools

import jax
import jax.numpy as jnp
from jax import lax
from jax.experimental import pallas as pl
from jax.experimental.pallas import tpu as pltpu
from jax.sharding import PartitionSpec as P

LANES = 128
SUB = 8

diffuse_rate = 0.08
nano_chl_index = 10
diat_chl_index = 11

SLOT_TILE, SLOT_FULL, SLOT_WEST, SLOT_EAST, TILE_OWNER, TILE_WET, TILE_BASE = range(7)
TABLE_ROWS = 8

OPEN_EAST, OPEN_NORTH, OPEN_WEST, OPEN_SOUTH, LIGHT, WET = range(6)

VMEM_LIMIT = 48 * 1024 * 1024


def positive(value):
    return jnp.maximum(value, 0.0)


def lane_ids(rows=SUB):
    return lax.broadcasted_iota(jnp.int32, (rows, LANES), 1)


def turned(value, by):
    by = by % LANES
    return value if by == 0 else pltpu.roll(value, by, 1)


def quotient(value, by):
    if by & (by - 1) == 0:
        return lax.shift_right_logical(value, jnp.int32(by.bit_length() - 1))
    return lax.div(value, jnp.int32(by))


def remainder(value, by):
    if by & (by - 1) == 0:
        return value & (by - 1)
    return lax.rem(value, jnp.int32(by))


def along(axis, by, closed):
    size = lax.axis_size(axis)
    pairs = [(i, (i + by) % size) for i in range(size)]
    return [p for p in pairs if closed or p[1] == p[0] + by]


def table_kernel(slot_count, tile_blocks, lon_count, row_ref, out_ref, used_ref):
    me = lax.axis_index("lon")
    block_count = row_ref.shape[1]
    width = out_ref.shape[1]

    def clear(i, carry):
        for r in range(TABLE_ROWS):
            out_ref[r, i] = 0
        return carry

    lax.fori_loop(0, width, clear, 0)

    def unuse(i, carry):
        used_ref[0, i] = 0
        used_ref[1, i] = 0
        return carry

    lax.fori_loop(0, lon_count, unuse, 0)
    out_ref[TILE_BASE, 0] = me * tile_blocks

    def visit(k, carry):
        code = row_ref[0, k]
        safe = jnp.maximum(code, 0)
        owner = remainder(quotient(safe, slot_count), lon_count)
        slot = remainder(safe, slot_count)
        tile = quotient(k, tile_blocks)

        @pl.when((code >= 0) & (owner == me))
        def _():
            west = row_ref[0, remainder(k + block_count - 1, block_count)]
            east = row_ref[0, remainder(k + 1, block_count)]
            out_ref[SLOT_TILE, slot] = tile
            out_ref[SLOT_FULL, slot] = 1
            out_ref[SLOT_WEST, slot] = remainder(jnp.maximum(west, 0), slot_count)
            out_ref[SLOT_EAST, slot] = remainder(jnp.maximum(east, 0), slot_count)
            used_ref[0, tile] = 1

        @pl.when((code >= 0) & (tile == me))
        def _():
            local = remainder(k, tile_blocks)
            out_ref[TILE_OWNER, local] = owner
            out_ref[TILE_WET, local] = 1
            used_ref[1, owner] = 1

        return carry

    lax.fori_loop(0, block_count, visit, 0, unroll=4)

    def give(target, filled, line, count):
        def one(i, carry):
            def look(j, done):
                take = (done == 0) & (used_ref[line, j] == 0)

                @pl.when(take)
                def _():
                    out_ref[target, i] = j
                    used_ref[line, j] = 1

                return jnp.where(take, 1, done)

            @pl.when(out_ref[filled, i] == 0)
            def _():
                lax.fori_loop(0, lon_count, look, 0)

            return carry

        lax.fori_loop(0, count, one, 0)

    give(SLOT_TILE, SLOT_FULL, 0, slot_count)
    give(TILE_OWNER, TILE_WET, 1, tile_blocks)


def routing(row, slot_count, tile_blocks):
    lon_count = lax.axis_size("lon")
    width = max(slot_count, tile_blocks, lon_count)
    return pl.pallas_call(
        functools.partial(table_kernel, slot_count, tile_blocks, lon_count),
        out_shape=jax.ShapeDtypeStruct((TABLE_ROWS, width), jnp.int32),
        in_specs=[pl.BlockSpec(memory_space=pltpu.SMEM)],
        out_specs=pl.BlockSpec(memory_space=pltpu.SMEM),
        scratch_shapes=[pltpu.SMEM((2, lon_count), jnp.int32)],
        name="routing",
    )(row)


def merged(pieces, ids):
    packed = pieces[0]
    for g in range(1, len(pieces)):
        packed = jnp.where(ids == g, pieces[g], packed)
    return packed


def pack_columns(first, second, side):
    lane = lane_ids()
    odd = (lane & 1) == 1
    here = (lane & (side - 1)) >> 1
    there = ((lane + 1) & (side - 1)) >> 1
    even_ends = merged([turned(v, 1 + 2 * g) for g, v in enumerate(first)], here)
    odd_ends = merged([turned(v, 2 * g) for g, v in enumerate(second)], there)
    return jnp.where(odd, even_ends, odd_ends), jnp.where(odd, odd_ends, even_ends)


def pack_quads(first, second, side):
    low = lane_ids() < LANES // 2
    both = [jnp.where(low, a, b) for a, b in zip(first, second)]
    turns = [turned(v, 2 * side + (g % 2) * (LANES // 2)) for g, v in enumerate(both)]
    return [jnp.where(low, turns[g], turns[g + 1]) for g in range(0, len(turns), 2)]


def regroup(values, side):
    values = list(values)
    ids = lane_ids() >> (side.bit_length() - 1)
    bit = 1
    while bit < len(values):
        keep = (ids & bit) == 0
        for n in range(len(values)):
            if n & bit == 0:
                a, b = values[n], values[n + bit]
                values[n] = jnp.where(keep, a, turned(b, side * bit))
                values[n + bit] = jnp.where(keep, turned(a, -side * bit), b)
        bit *= 2
    return values


def edges_kernel(levels, side, table_ref, cell_ref, rows_ref, west_ref, east_ref):
    group = LANES // side
    rounds = cell_ref.shape[1] // levels // group
    level_tiles = levels // SUB

    def body(lt, carry):
        for i in range(rounds):
            row = pl.multiple_of(i * levels + lt * SUB, SUB)
            first, second = [], []
            for g in range(group):
                at = pl.multiple_of((i * group + g) * levels + lt * SUB, SUB)
                first.append(cell_ref[0, pl.ds(at, SUB), 0:LANES])
                second.append(cell_ref[0, pl.ds(at, SUB), LANES : 2 * LANES])
            west, east = pack_columns(first, second, side)
            west_ref[0, pl.ds(row, SUB), :] = west
            east_ref[0, pl.ds(row, SUB), :] = east
            for n, quad in enumerate(pack_quads(first, second, side)):
                at = pl.multiple_of((i * (group // 2) + n) * levels + lt * SUB, SUB)
                rows_ref[0, pl.ds(at, SUB), :] = quad
        return carry

    lax.fori_loop(0, level_tiles, body, 0, unroll=True)


def first_edges(table, tracers, levels, side):
    slot_count, channels, cell_count = tracers.shape
    lon_count = lax.axis_size("lon")
    rows = channels * side // LANES
    f32 = jnp.float32
    by_slot = pl.BlockSpec((1, rows, LANES), lambda s, t: (s, 0, 0))
    return pl.pallas_call(
        functools.partial(edges_kernel, levels, side),
        out_shape=[
            jax.ShapeDtypeStruct((lon_count, 4 * rows, LANES), f32),
            jax.ShapeDtypeStruct((slot_count, rows, LANES), f32),
            jax.ShapeDtypeStruct((slot_count, rows, LANES), f32),
        ],
        grid_spec=pltpu.PrefetchScalarGridSpec(
            num_scalar_prefetch=1,
            grid=(slot_count,),
            in_specs=[pl.BlockSpec((1, channels, cell_count), lambda s, t: (s, 0, 0))],
            out_specs=[
                pl.BlockSpec((1, 4 * rows, LANES), lambda s, t: (t[SLOT_TILE, s], 0, 0)),
                by_slot,
                by_slot,
            ],
        ),
        compiler_params=pltpu.CompilerParams(vmem_limit_bytes=VMEM_LIMIT),
        name="first_edges",
    )(table, tracers)


def react(mixed, par_light, warm_factor):
    (
        carbon_dis,
        alkalinity,
        oxygen,
        nitrate,
        ammonium,
        phosphate,
        silicate,
        iron_free,
        nano_carbon,
        diat_carbon,
        nano_chl,
        diat_chl,
        nano_iron,
        diat_iron,
        diat_silica,
        micro_zoo,
        meso_zoo,
        dissolved_org,
        small_part,
        big_part,
        small_iron,
        big_iron,
        big_silica,
        calcite,
    ) = mixed
    nitrogen = positive(nitrate) + positive(ammonium)
    limit_nitro = nitrogen / (0.5 + nitrogen)
    limit_phos = positive(phosphate) / (0.3 + positive(phosphate))
    limit_iron = positive(iron_free) / (0.2 + positive(iron_free))
    limit_sil = positive(silicate) / (1.0 + positive(silicate))
    nutr_nano = jnp.minimum(jnp.minimum(limit_nitro, limit_phos), limit_iron)
    nutr_diat = jnp.minimum(nutr_nano, limit_sil)
    lit = warm_factor * par_light
    prod_nano = 0.1 * lit / (par_light + 0.5) * nutr_nano * nano_carbon
    prod_diat = 0.12 * lit / (par_light + 1.0) * nutr_diat * diat_carbon
    ammon_share = (positive(ammonium) + 0.01) / (nitrogen + 0.02)
    graze_nano = 0.08 * warm_factor * micro_zoo / (1.0 + positive(nano_carbon))
    graze_diat = 0.06 * warm_factor * meso_zoo / (1.0 + positive(diat_carbon))
    loss_nano = graze_nano + 0.02
    loss_diat = graze_diat + 0.02
    eaten_nano = graze_nano * nano_carbon
    eaten_diat = graze_diat * diat_carbon
    death_micro = 0.03 * micro_zoo * positive(micro_zoo)
    death_meso = 0.03 * meso_zoo * positive(meso_zoo)
    remin_doc = 0.03 * warm_factor * dissolved_org
    remin_poc = 0.02 * warm_factor * small_part
    remin_goc = 0.01 * warm_factor * big_part
    nitrify = 0.05 * ammonium
    melt_si = 0.02 * big_silica
    melt_cal = 0.01 * calcite
    melt_sfe = 0.02 * small_iron
    melt_bfe = 0.01 * big_iron
    uptake = prod_nano + prod_diat
    remin_total = remin_doc + remin_poc + remin_goc
    calcify = 0.02 * prod_nano
    gained = remin_total - uptake
    shell = melt_cal - calcify
    by_ammon = ammon_share * uptake
    by_nitrate = 0.16 * (uptake - by_ammon - nitrify)
    return [
        carbon_dis + gained + shell,
        alkalinity + 2.0 * shell + by_nitrate,
        oxygen - 1.3 * gained - 0.32 * nitrify,
        nitrate - by_nitrate,
        ammonium + 0.16 * (remin_total - by_ammon - nitrify),
        phosphate + 0.01 * gained,
        silicate + melt_si - 0.15 * prod_diat,
        iron_free + melt_sfe + melt_bfe - 0.005 * uptake,
        nano_carbon + prod_nano - loss_nano * nano_carbon,
        diat_carbon + prod_diat - loss_diat * diat_carbon,
        nano_chl + 0.03 * prod_nano - loss_nano * nano_chl,
        diat_chl + 0.03 * prod_diat - loss_diat * diat_chl,
        nano_iron + 0.005 * prod_nano - loss_nano * nano_iron,
        diat_iron + 0.005 * prod_diat - loss_diat * diat_iron,
        diat_silica + 0.15 * prod_diat - loss_diat * diat_silica,
        micro_zoo + 0.3 * eaten_nano - death_micro,
        meso_zoo + 0.3 * eaten_diat - death_meso,
        dissolved_org + 0.3 * eaten_nano + 0.02 * nano_carbon - remin_doc,
        small_part + 0.4 * eaten_nano + death_micro - remin_poc,
        big_part + 0.4 * eaten_diat + 0.02 * diat_carbon + death_meso - remin_goc,
        small_iron + loss_nano * nano_iron - melt_sfe,
        big_iron + loss_diat * diat_iron - melt_bfe,
        big_silica + loss_diat * diat_silica - melt_si,
        calcite + calcify - melt_cal,
    ]


def set_transport(coef_ref, at, span, faces, opens):
    flow_e, flow_n, flow_w, flow_s = (face * is_open for face, is_open in zip(faces, opens))
    open_e, open_n, open_w, open_s = opens
    out_e, in_e = jnp.maximum(flow_e, 0.0), jnp.minimum(flow_e, 0.0)
    out_n, in_n = jnp.maximum(flow_n, 0.0), jnp.minimum(flow_n, 0.0)
    in_w, out_w = jnp.maximum(flow_w, 0.0), jnp.minimum(flow_w, 0.0)
    in_s, out_s = jnp.maximum(flow_s, 0.0), jnp.minimum(flow_s, 0.0)
    drift = diffuse_rate * (open_w + open_e + open_s + open_n)
    coef_ref[0, at, span] = 1.0 - (out_e - out_w) - (out_n - out_s) - drift
    coef_ref[1, at, span] = diffuse_rate * open_e - in_e
    coef_ref[2, at, span] = diffuse_rate * open_w + in_w
    coef_ref[3, at, span] = diffuse_rate * open_n - in_n
    coef_ref[4, at, span] = diffuse_rate * open_s + in_s


def set_mixing(coef_ref, at, span, mix, above, bottom):
    sub = lax.broadcasted_iota(jnp.int32, (SUB, LANES), 0)
    mix_up = pltpu.roll(jnp.where(sub == SUB - 1, above, mix), 1, 0)
    if bottom:
        mix = jnp.where(sub == SUB - 1, 0.0, mix)
    coef_ref[5, at, span] = 1.0 - mix - mix_up
    coef_ref[6, at, span] = mix
    coef_ref[7, at, span] = mix_up


def set_blank(moved_ref, channels):
    blank = jnp.zeros((SUB, moved_ref.shape[1]), jnp.float32)
    moved_ref[0:SUB, :] = blank
    moved_ref[SUB + channels : 2 * SUB + channels, :] = blank


def mix_and_react(levels, tracer_count, spans, moved_ref, coef_ref, light, wet, warm_at, store):
    sub = lax.broadcasted_iota(jnp.int32, (SUB, LANES), 0)

    def reacting(lt, carry):
        at = pl.multiple_of(lt * SUB, SUB)
        depths = []
        halves_new = []
        for h, span in enumerate(spans):
            mix_c, mix_d, mix_u = (coef_ref[n, pl.ds(at, SUB), span] for n in (5, 6, 7))
            mixed = []
            for t in range(tracer_count):
                base = t * levels + lt * SUB
                before = moved_ref[pl.ds(pl.multiple_of(base, SUB), SUB), span]
                now = moved_ref[pl.ds(pl.multiple_of(base + SUB, SUB), SUB), span]
                after = moved_ref[pl.ds(pl.multiple_of(base + 2 * SUB, SUB), SUB), span]
                up = pltpu.roll(jnp.where(sub == SUB - 1, before, now), 1, 0)
                down = pltpu.roll(jnp.where(sub == 0, after, now), SUB - 1, 0)
                mixed.append(mix_c * now + mix_d * down + mix_u * up)
            absorb = 0.04 + 0.02 * (positive(mixed[nano_chl_index]) + positive(mixed[diat_chl_index]))
            total = absorb
            for by in (1, 2, 4):
                total = total + jnp.where(sub >= by, pltpu.roll(total, by, 0), 0.0)
            above = carry[h] + (total - absorb)
            depths.append(carry[h] + total[SUB - 1 : SUB, :])
            par_light = light[h] * jnp.exp(-(above + 0.5 * absorb))
            halves_new.append([value * wet[h] for value in react(mixed, par_light, warm_at(lt, h))])
            for t in range(tracer_count):
                store(t, pl.multiple_of(t * levels + lt * SUB, SUB), h, halves_new[h][t])
        store(None, lt, None, halves_new)
        return tuple(depths)

    start = tuple(jnp.zeros((1, LANES), jnp.float32) for _ in spans)
    lax.fori_loop(0, levels // SUB, reacting, start, unroll=True)


def step_kernel(levels, side, last, table_ref, cell_ref, phys_ref, rim_ref, rim_w_ref, rim_e_ref, *refs):
    if last:
        out_ref, chl_ref, coef_ref, moved_ref, ends_ref = refs
        edge_refs = (chl_ref,)
    else:
        out_ref, west_ref, east_ref, coef_ref, moved_ref, ends_ref = refs
        edge_refs = (west_ref, east_ref)
    channels, cell_count = cell_ref.shape[1:]
    tracer_count = channels // levels
    group = LANES // side
    halves = cell_count // LANES
    rounds = tracer_count // group
    level_tiles = levels // SUB
    rows = rounds * levels
    slot = pl.program_id(0)
    full = table_ref[SLOT_FULL, slot] == 1
    spans = [slice(h * LANES, (h + 1) * LANES) for h in range(halves)]

    @pl.when(jnp.logical_not(full))
    def _():
        out_ref[...] = jnp.zeros_like(out_ref)
        for ref in edge_refs:
            ref[...] = jnp.zeros_like(ref)

    @pl.when(full)
    def _():
        lane = lane_ids()
        col = lane & (side - 1)
        first_col = col == 0
        last_col = col == side - 1
        first_row = lane < side
        last_row = lane >= LANES - side
        odd = (lane & 1) == 1
        flag_row = 4 * levels
        pack_at = flag_row + SUB

        def flag(f, h):
            return phys_ref[0, flag_row + f : flag_row + f + 1, spans[h]]

        def southward(values, edge):
            out = []
            for h in range(halves):
                before = edge if h == 0 else turned(values[h - 1], side)
                out.append(jnp.where(first_row, before, turned(values[h], side)))
            return out

        def northward(values, edge):
            out = []
            for h in range(halves):
                after = edge if h == halves - 1 else turned(values[h + 1], -side)
                out.append(jnp.where(last_row, after, turned(values[h], -side)))
            return out

        above_mix = [jnp.zeros((SUB, LANES), jnp.float32)] * halves
        west_pack = phys_ref[0, pack_at : pack_at + SUB, spans[0]]
        south_pack = phys_ref[0, pack_at : pack_at + SUB, spans[1]]
        for lt in range(level_tiles):
            at = slice(lt * SUB, (lt + 1) * SUB)
            east_face = [phys_ref[0, lt * SUB : (lt + 1) * SUB, spans[h]] for h in range(halves)]
            north_face = [
                phys_ref[0, levels + lt * SUB : levels + (lt + 1) * SUB, spans[h]] for h in range(halves)
            ]
            south_face = southward(north_face, turned(south_pack, -side * lt))
            for h in range(halves):
                west_face = jnp.where(
                    first_col, turned(west_pack, -(h * group + lt)), turned(east_face[h], 1)
                )
                faces = (east_face[h], north_face[h], west_face, south_face[h])
                set_transport(coef_ref, at, spans[h], faces, [flag(f, h) for f in range(4)])
                mix = phys_ref[0, 3 * levels + lt * SUB : 3 * levels + (lt + 1) * SUB, spans[h]]
                set_mixing(coef_ref, at, spans[h], mix, above_mix[h], lt == level_tiles - 1)
                above_mix[h] = mix

        for at in range(0, rows, SUB):
            ends_ref[at : at + SUB, :] = turned(rim_w_ref[0, at : at + SUB, :], 2 - 2 * side)
        set_blank(moved_ref, channels)

        def advect(lt, carry):
            at = pl.multiple_of(lt * SUB, SUB)
            coef = [[coef_ref[n, pl.ds(at, SUB), spans[h]] for n in range(5)] for h in range(halves)]
            for i in range(rounds):
                row = pl.multiple_of(i * levels + lt * SUB, SUB)
                rims = [
                    rim_ref[0, pl.ds(row, SUB), :],
                    rim_ref[0, pl.ds(pl.multiple_of(rows + row, SUB), SUB), :],
                ]
                ends_w = ends_ref[pl.ds(row, SUB), :]
                ends_e = rim_e_ref[0, pl.ds(row, SUB), :]
                sides = [jnp.where(odd, ends_e, ends_w), jnp.where(odd, ends_w, ends_e)]
                for g in range(group):
                    chan = pl.multiple_of((i * group + g) * levels + lt * SUB, SUB)
                    here = [cell_ref[0, pl.ds(chan, SUB), spans[h]] for h in range(halves)]
                    rim = turned(rims[2 * g // group], -side - 2 * side * (g % (group // 2)))
                    south = southward(here, rim)
                    north = northward(here, rim)
                    for h in range(halves):
                        ends = turned(sides[h], side - 2 + h - 2 * g)
                        west = jnp.where(first_col, ends, turned(here[h], 1))
                        east = jnp.where(last_col, ends, turned(here[h], -1))
                        c, e, w, n, s = coef[h]
                        moved_ref[pl.ds(pl.multiple_of(SUB + chan, SUB), SUB), spans[h]] = (
                            c * here[h] + (e * east + w * west) + (n * north[h] + s * south[h])
                        )
            return carry

        lax.fori_loop(0, level_tiles, advect, 0, unroll=True)

        def store(t, at, h, value):
            if t is not None:
                out_ref[0, pl.ds(at, SUB), spans[h]] = value
            elif last:
                for k, new in enumerate(value):
                    chl_ref[0, pl.ds(pl.multiple_of(at * SUB, SUB), SUB), spans[k]] = positive(
                        new[nano_chl_index]
                    ) + positive(new[diat_chl_index])
            else:
                for i in range(rounds):
                    row = pl.multiple_of(i * levels + at * SUB, SUB)
                    first, second = (new[i * group : (i + 1) * group] for new in value)
                    west, east = pack_columns(first, second, side)
                    west_ref[0, pl.ds(row, SUB), :] = west
                    east_ref[0, pl.ds(row, SUB), :] = east

        def warm_at(lt, h):
            return phys_ref[0, pl.ds(pl.multiple_of(2 * levels + lt * SUB, SUB), SUB), spans[h]]

        light = [flag(LIGHT, h) for h in range(halves)]
        wet = [flag(WET, h) for h in range(halves)]
        mix_and_react(levels, tracer_count, spans, moved_ref, coef_ref, light, wet, warm_at, store)


def step(table, cells, phys, rims, rim_w, rim_e, levels, side, last):
    slot_count, channels, cell_count = cells.shape
    lon_count = lax.axis_size("lon")
    rows = channels * side // LANES
    phys_rows = phys.shape[1]
    f32 = jnp.float32
    by_slot = pl.BlockSpec((1, channels, cell_count), lambda s, t: (s, 0, 0))
    shapes = [jax.ShapeDtypeStruct(cells.shape, f32)]
    specs = [by_slot]
    if last:
        shapes.append(jax.ShapeDtypeStruct((lon_count, levels, cell_count), f32))
        specs.append(pl.BlockSpec((1, levels, cell_count), lambda s, t: (t[SLOT_TILE, s], 0, 0)))
    else:
        beside = jax.ShapeDtypeStruct((slot_count, rows, LANES), f32)
        shapes += [beside, beside]
        specs += [pl.BlockSpec((1, rows, LANES), lambda s, t: (s, 0, 0))] * 2
    return pl.pallas_call(
        functools.partial(step_kernel, levels, side, last),
        out_shape=shapes,
        grid_spec=pltpu.PrefetchScalarGridSpec(
            num_scalar_prefetch=1,
            grid=(slot_count,),
            in_specs=[
                by_slot,
                pl.BlockSpec((1, phys_rows, cell_count), lambda s, t: (t[SLOT_TILE, s], 0, 0)),
                pl.BlockSpec((1, 2 * rows, LANES), lambda s, t: (t[SLOT_TILE, s], 0, 0)),
                pl.BlockSpec((1, rows, LANES), lambda s, t: (t[SLOT_WEST, s], 0, 0)),
                pl.BlockSpec((1, rows, LANES), lambda s, t: (t[SLOT_EAST, s], 0, 0)),
            ],
            out_specs=specs,
            scratch_shapes=[
                pltpu.VMEM((8, levels, cell_count), f32),
                pltpu.VMEM((channels + 2 * SUB, cell_count), f32),
                pltpu.VMEM((rows, LANES), f32),
            ],
        ),
        compiler_params=pltpu.CompilerParams(vmem_limit_bytes=VMEM_LIMIT),
        name="step",
    )(table, cells, phys, rims, rim_w, rim_e)


def rows_kernel(levels, factor, fine_ref, mix_ref, pick_ref, rows_ref):
    f32 = jnp.float32
    picks = pick_ref[...]
    east_face = jnp.zeros((levels, LANES), f32)
    temp_mean = jnp.zeros((levels, LANES), f32)
    for r in range(factor):
        got = jnp.dot(fine_ref[r], picks, preferred_element_type=f32)
        east_face += got[0:levels, 0:LANES]
        temp_mean += got[2 * levels : 3 * levels, LANES : 2 * LANES]
        if r == factor - 1:
            north_face = got[levels : 2 * levels, LANES : 2 * LANES]
    rows_ref[0, 0:levels, :] = east_face * (1.0 / factor)
    rows_ref[0, levels : 2 * levels, :] = north_face * (1.0 / factor)
    rows_ref[0, 2 * levels : 3 * levels, :] = jnp.exp(0.0639 * (temp_mean * (1.0 / (factor * factor))))
    rows_ref[0, 3 * levels : 4 * levels, :] = mix_ref[0].astype(f32)


def coarse_rows(fine, mix, picks):
    side, levels, tile_cols = mix.shape
    factor = fine.shape[0] // side
    fine_cols = fine.shape[2]
    return pl.pallas_call(
        functools.partial(rows_kernel, levels, factor),
        out_shape=jax.ShapeDtypeStruct((side, 4 * levels, tile_cols), jnp.float32),
        grid=(side,),
        in_specs=[
            pl.BlockSpec((factor, 3 * levels, fine_cols), lambda i: (i, 0, 0)),
            pl.BlockSpec((1, levels, tile_cols), lambda i: (i, 0, 0)),
            pl.BlockSpec(picks.shape, lambda i: (0, 0)),
        ],
        out_specs=pl.BlockSpec((1, 4 * levels, tile_cols), lambda i: (i, 0, 0)),
        compiler_params=pltpu.CompilerParams(vmem_limit_bytes=VMEM_LIMIT),
        name="coarse_rows",
    )(fine, mix, picks)


def place_kernel(
    levels,
    side,
    factor,
    table_ref,
    rows_ref,
    light_ref,
    land_ref,
    south_ref,
    north_ref,
    west_ref,
    east_ref,
    pick_ref,
    out_ref,
    line_ref,
    flags_ref,
):
    tile_blocks = land_ref.shape[1] // side
    halves = side * side // LANES
    group = LANES // side
    fine_cols = light_ref.shape[1]
    f32 = jnp.float32
    picks = pick_ref[...]
    lane = lane_ids()
    group_id = lane >> (side.bit_length() - 1)
    col_id = lane & (side - 1)
    flag_row = 4 * levels
    pack_at = flag_row + SUB
    wet = land_ref[...].astype(f32)
    sides = wet.shape
    lane2 = lax.broadcasted_iota(jnp.int32, sides, 1)
    sub2 = lax.broadcasted_iota(jnp.int32, sides, 0)
    diagonal = lane2 == sub2
    rim_w = jnp.sum(jnp.where(diagonal, west_ref[SUB : SUB + 1, :], 0.0), axis=1, keepdims=True)
    rim_e = jnp.sum(jnp.where(diagonal, east_ref[0:1, :], 0.0), axis=1, keepdims=True)
    wet_w = jnp.where(lane2 == 0, rim_w, pltpu.roll(wet, 1, 1))
    wet_e = jnp.where(lane2 == LANES - 1, rim_e, pltpu.roll(wet, LANES - 1, 1))
    wet_s = jnp.where(sub2 == 0, south_ref[levels : levels + 1, 0:LANES], pltpu.roll(wet, 1, 0))
    wet_n = jnp.where(sub2 == side - 1, north_ref[0:1, 0:LANES], pltpu.roll(wet, side - 1, 0))
    fold_r = lax.broadcasted_iota(jnp.int32, (side, side * factor), 0)
    fold_c = lax.broadcasted_iota(jnp.int32, (side, side * factor), 1)
    fold_d = fold_c - factor * fold_r
    fold = jnp.where((fold_d >= 0) & (fold_d < factor), 1.0, 0.0)
    narrow = picks[:, LANES : 2 * LANES].astype(f32)
    light_rows = jnp.dot(fold, light_ref[...], precision=lax.Precision.HIGHEST, preferred_element_type=f32)
    light_mean = jnp.dot(
        light_rows, narrow, precision=lax.Precision.HIGHEST, preferred_element_type=f32
    ) * (1.0 / (factor * factor))
    flags = [wet * wet_e, wet * wet_n, wet * wet_w, wet * wet_s, light_mean, wet]
    for r in range(side):
        for f, value in enumerate(flags):
            flags_ref[r, f : f + 1, :] = value[r : r + 1, :]
        flags_ref[r, len(flags) : SUB, :] = jnp.zeros((SUB - len(flags), LANES), f32)

    def place(ref, frm, to):
        for h in range(halves):
            values = [ref[h * group + r, pl.ds(frm, SUB), :] for r in range(group)]
            for b, block in enumerate(regroup(values, side)):
                owner = table_ref[TILE_OWNER, b]
                out_ref[owner, pl.ds(to, SUB), h * LANES : (h + 1) * LANES] = block

    def place_four(q, carry):
        for n in range(4):
            at = pl.multiple_of(n * levels + q * SUB, SUB)
            place(rows_ref, at, at)
        return carry

    lax.fori_loop(0, levels // SUB, place_four, 0)
    place(flags_ref, 0, flag_row)

    fine_v = south_ref[0:levels, 0:fine_cols].astype(jnp.bfloat16)
    north_below = jnp.dot(fine_v, picks, preferred_element_type=f32)[:, LANES : 2 * LANES] * (1.0 / factor)
    for h, r in enumerate((0, side - 1)):
        span = slice(h * LANES, (h + 1) * LANES)
        line_ref[0 : 4 * levels, span] = rows_ref[r, 0 : 4 * levels, :]
        line_ref[6 * levels : 6 * levels + SUB, span] = flags_ref[r]
        line_ref[5 * levels : 6 * levels, span] = (
            north_below if h == 0 else rows_ref[r - 1, levels : 2 * levels, :]
        )
        from_lane = side * (r % group) + group * (r // group)
        for lt in range(levels // SUB):
            face = rows_ref[r, lt * SUB : (lt + 1) * SUB, :]
            line_ref[4 * levels + lt * SUB : 4 * levels + (lt + 1) * SUB, span] = jnp.where(
                lane == 0, turned(west_ref[0:SUB, :], -(from_lane + lt)), turned(face, 1)
            )
    for b in range(tile_blocks):
        owner = table_ref[TILE_OWNER, b]
        south_pack = jnp.zeros((SUB, LANES), f32)
        for lt in range(levels // SUB):
            piece = turned(north_below[lt * SUB : (lt + 1) * SUB, :], side * (lt - b))
            south_pack = jnp.where(group_id == lt, piece, south_pack)
        if b == 0:
            west_pack = west_ref[0:SUB, :]
        else:
            beside = table_ref[TILE_OWNER, b - 1]
            west_pack = jnp.zeros((SUB, LANES), f32)
            for h in range(halves):
                for lt in range(levels // SUB):
                    face = out_ref[beside, lt * SUB : (lt + 1) * SUB, h * LANES : (h + 1) * LANES]
                    piece = turned(face, h * group + lt - (side - 1))
                    west_pack = jnp.where(col_id == h * group + lt, piece, west_pack)
        out_ref[owner, pack_at : pack_at + SUB, 0:LANES] = west_pack
        out_ref[owner, pack_at : pack_at + SUB, LANES : 2 * LANES] = south_pack


def coarsen(table, rows, light, land, from_south, from_north, from_west, from_east, picks):
    lon_count = lax.axis_size("lon")
    side, tile_cols = land.shape
    levels = rows.shape[1] // 4
    factor = light.shape[0] // side
    phys_rows = 4 * levels + 2 * SUB
    f32 = jnp.float32
    vmem = pl.BlockSpec(memory_space=pltpu.VMEM)
    return pl.pallas_call(
        functools.partial(place_kernel, levels, side, factor),
        out_shape=[
            jax.ShapeDtypeStruct((lon_count, phys_rows, side * side), f32),
            jax.ShapeDtypeStruct((6 * levels + SUB, 2 * LANES), f32),
        ],
        in_specs=[pl.BlockSpec(memory_space=pltpu.SMEM)] + [vmem] * 8,
        out_specs=[vmem, vmem],
        scratch_shapes=[pltpu.VMEM((side, SUB, LANES), f32)],
        compiler_params=pltpu.CompilerParams(vmem_limit_bytes=VMEM_LIMIT),
        name="coarsen",
    )(table, rows, light, land, from_south, from_north, from_west, from_east, picks)


def lines_kernel(levels, side, table_ref, quad_ref, low_ref, high_ref, low_in_ref, high_in_ref, ends_ref):
    tile_blocks = LANES // side
    pairs = quad_ref.shape[1] // levels
    lane = lane_ids()
    spot = lane >> 1

    def body(lt, carry):
        packed = jnp.zeros((SUB, LANES), jnp.float32)
        for m in range(pairs):
            at = pl.multiple_of(m * levels + lt * SUB, SUB)
            blocks = []
            for b in range(tile_blocks):
                value = quad_ref[table_ref[TILE_OWNER, b], pl.ds(at, SUB), :]
                blocks.append(jnp.where(table_ref[TILE_WET, b] == 1, value, 0.0))
            parts = regroup(blocks, side)
            for p in range(2):
                t = 2 * m + p
                chan = pl.ds(pl.multiple_of(t * levels + lt * SUB, SUB), SUB)
                high_in, high, low, low_in = parts[4 * p : 4 * p + 4]
                low_ref[chan, :] = low
                high_ref[chan, :] = high
                low_in_ref[chan, :] = low_in
                high_in_ref[chan, :] = high_in
                for k, line in ((2 * t, low), (2 * t + 1, high)):
                    packed = jnp.where(spot == k, turned(line, 1 + 2 * k), packed)
        ends_ref[pl.ds(pl.multiple_of(lt * SUB, SUB), SUB), :] = packed
        return carry

    lax.fori_loop(0, levels // SUB, body, 0)


def tile_lines(table, quads, levels, side):
    channels = quads.shape[1] // levels * 2 * levels
    vmem = pl.BlockSpec(memory_space=pltpu.VMEM)
    line = jax.ShapeDtypeStruct((channels, LANES), jnp.float32)
    return pl.pallas_call(
        functools.partial(lines_kernel, levels, side),
        out_shape=[line] * 4 + [jax.ShapeDtypeStruct((levels, LANES), jnp.float32)],
        in_specs=[pl.BlockSpec(memory_space=pltpu.SMEM), vmem],
        out_specs=[vmem] * 5,
        compiler_params=pltpu.CompilerParams(vmem_limit_bytes=VMEM_LIMIT),
        name="tile_lines",
    )(table, quads)


def line_kernel(
    levels,
    low_ref,
    high_ref,
    low_in_ref,
    high_in_ref,
    below_ref,
    above_ref,
    west_ref,
    east_ref,
    phys_ref,
    low_out_ref,
    high_out_ref,
    coef_ref,
    moved_ref,
    ends_ref,
):
    channels = low_ref.shape[0]
    tracer_count = channels // levels
    level_tiles = levels // SUB
    lane = lane_ids()
    odd = (lane & 1) == 1
    spans = [slice(0, LANES), slice(LANES, 2 * LANES)]
    flag_row = 6 * levels
    lines = (
        (low_ref, low_in_ref, below_ref, low_out_ref),
        (high_ref, above_ref, high_in_ref, high_out_ref),
    )

    def flag(f, h):
        return phys_ref[flag_row + f : flag_row + f + 1, spans[h]]

    above_mix = [jnp.zeros((SUB, LANES), jnp.float32)] * 2
    for lt in range(level_tiles):
        at = slice(lt * SUB, (lt + 1) * SUB)
        from_west = west_ref[lt * SUB : (lt + 1) * SUB, :]
        from_east = east_ref[lt * SUB : (lt + 1) * SUB, :]
        ends_ref[at, :] = jnp.where(odd, turned(from_east, -2), from_west)
        for h in range(2):
            faces = [
                phys_ref[n * levels + lt * SUB : n * levels + (lt + 1) * SUB, spans[h]] for n in (0, 1, 4, 5)
            ]
            set_transport(coef_ref, at, spans[h], faces, [flag(f, h) for f in range(4)])
            mix = phys_ref[3 * levels + lt * SUB : 3 * levels + (lt + 1) * SUB, spans[h]]
            set_mixing(coef_ref, at, spans[h], mix, above_mix[h], lt == level_tiles - 1)
            above_mix[h] = mix
    set_blank(moved_ref, channels)

    def advect(lt, carry):
        at = pl.multiple_of(lt * SUB, SUB)
        ends = ends_ref[pl.ds(at, SUB), :]
        for h in range(2):
            here_ref, north_ref, south_ref, _ = lines[h]
            c, e, w, n, s = (coef_ref[k, pl.ds(at, SUB), spans[h]] for k in range(5))
            for t in range(tracer_count):
                chan = pl.multiple_of(t * levels + lt * SUB, SUB)
                here = here_ref[pl.ds(chan, SUB), :]
                end = turned(ends, -2 * (2 * t + h))
                west = jnp.where(lane == 0, end, turned(here, 1))
                east = jnp.where(lane == LANES - 1, end, turned(here, -1))
                moved_ref[pl.ds(pl.multiple_of(SUB + chan, SUB), SUB), spans[h]] = (
                    c * here
                    + (e * east + w * west)
                    + (n * north_ref[pl.ds(chan, SUB), :] + s * south_ref[pl.ds(chan, SUB), :])
                )
        return carry

    lax.fori_loop(0, level_tiles, advect, 0, unroll=True)

    def store(t, at, h, value):
        if t is not None:
            lines[h][3][pl.ds(at, SUB), :] = value

    def warm_at(lt, h):
        return phys_ref[pl.ds(pl.multiple_of(2 * levels + lt * SUB, SUB), SUB), spans[h]]

    light = [flag(LIGHT, h) for h in range(2)]
    wet = [flag(WET, h) for h in range(2)]
    mix_and_react(levels, tracer_count, spans, moved_ref, coef_ref, light, wet, warm_at, store)


def line_step(low, high, low_in, high_in, below, above, from_west, from_east, phys, levels):
    channels = low.shape[0]
    vmem = pl.BlockSpec(memory_space=pltpu.VMEM)
    f32 = jnp.float32
    line = jax.ShapeDtypeStruct((channels, LANES), f32)
    return pl.pallas_call(
        functools.partial(line_kernel, levels),
        out_shape=[line, line],
        in_specs=[vmem] * 9,
        out_specs=[vmem, vmem],
        scratch_shapes=[
            pltpu.VMEM((8, levels, 2 * LANES), f32),
            pltpu.VMEM((channels + 2 * SUB, 2 * LANES), f32),
            pltpu.VMEM((levels, LANES), f32),
        ],
        compiler_params=pltpu.CompilerParams(vmem_limit_bytes=VMEM_LIMIT),
        name="line_step",
    )(low, high, low_in, high_in, below, above, from_west, from_east, phys)


def hand_kernel(levels, side, table_ref, below_ref, above_ref, *refs):
    out_ref = refs[-1]
    group = LANES // side
    rounds = below_ref.shape[0] // levels // group
    half = group // 2

    def body(lt, carry):
        for i in range(rounds):
            for part in range(2):
                lines = []
                for g in range(half):
                    t = i * group + part * half + g
                    chan = pl.ds(pl.multiple_of(t * levels + lt * SUB, SUB), SUB)
                    lines += [above_ref[chan, :], below_ref[chan, :]]
                row = pl.multiple_of((part * rounds + i) * levels + lt * SUB, SUB)
                for b, value in enumerate(regroup(lines, side)):
                    out_ref[table_ref[TILE_OWNER, b], pl.ds(row, SUB), :] = value
        return carry

    lax.fori_loop(0, levels // SUB, body, 0)


def hand_on(table, below, above, levels, side, *after):
    lon_count = lax.axis_size("lon")
    rows = 2 * below.shape[0] * side // LANES
    vmem = pl.BlockSpec(memory_space=pltpu.VMEM)
    return pl.pallas_call(
        functools.partial(hand_kernel, levels, side),
        out_shape=jax.ShapeDtypeStruct((lon_count, rows, LANES), jnp.float32),
        in_specs=[pl.BlockSpec(memory_space=pltpu.SMEM), vmem, vmem]
        + [pl.BlockSpec(memory_space=pl.ANY)] * len(after),
        out_specs=vmem,
        compiler_params=pltpu.CompilerParams(vmem_limit_bytes=VMEM_LIMIT),
        name="hand_on",
    )(table, below, above, *after)


def gate_kernel(*refs):
    pass


def gate(values, *others):
    anywhere = pl.BlockSpec(memory_space=pl.ANY)
    count = len(values)
    return pl.pallas_call(
        gate_kernel,
        out_shape=[jax.ShapeDtypeStruct(x.shape, x.dtype) for x in values],
        in_specs=[anywhere] * (count + len(others)),
        out_specs=[anywhere] * count,
        input_output_aliases={i: i for i in range(count)},
        name="gate",
    )(*values, *others)


def heat_kernel(levels, side, factor, table_ref, chl_ref, light_ref, land_ref, widen_ref, out_ref, rows_ref, wide_ref):
    tile_blocks = land_ref.shape[1] // side
    halves = side * side // LANES
    group = LANES // side
    fine_cols = light_ref.shape[1]
    fine_rows = light_ref.shape[0]
    f32 = jnp.float32
    group_id = lane_ids() >> (side.bit_length() - 1)

    def place(lt, carry):
        at = pl.multiple_of(lt * SUB, SUB)
        for h in range(halves):
            blocks = []
            for b in range(tile_blocks):
                owner = table_ref[TILE_OWNER, b]
                values = chl_ref[owner, pl.ds(at, SUB), h * LANES : (h + 1) * LANES]
                blocks.append(jnp.where(table_ref[TILE_WET, b] == 1, values, 0.0))
            for r in range(group):
                line = None
                for b in range(tile_blocks):
                    piece = turned(blocks[b], side * (b - r))
                    line = piece if line is None else jnp.where(group_id == b, piece, line)
                rows_ref[pl.ds(pl.multiple_of((h * group + r) * levels + lt * SUB, SUB), SUB), :] = line
        return carry

    lax.fori_loop(0, levels // SUB, place, 0)
    wet = land_ref[...].astype(f32)
    widen = widen_ref[...]
    above = jnp.zeros_like(wet)
    passing = jnp.ones_like(wet)
    for l in range(levels):
        chl = rows_ref[pl.ds(l, side, stride=levels), :]
        above = above + (0.04 + 0.02 * chl)
        through = jnp.exp(-above)
        kept = (passing - through) * wet
        passing = through
        high = kept.astype(jnp.bfloat16)
        low = (kept - high.astype(f32)).astype(jnp.bfloat16)
        wide_ref[l * side : (l + 1) * side, :] = jnp.dot(
            high, widen, preferred_element_type=f32
        ) + jnp.dot(low, widen, preferred_element_type=f32)

    sub = lax.broadcasted_iota(jnp.int32, (SUB, LANES), 0)
    sources = []
    for m in range(fine_rows // SUB):
        start = (m * SUB // factor) // SUB * SUB
        index = jnp.zeros_like(sub)
        for r in range(1, side):
            index = index + jnp.where(sub + m * SUB >= r * factor, 1, 0)
        sources.append((start, index - start))

    def spread(l, carry):
        for c in range(fine_cols // LANES):
            span = slice(c * LANES, (c + 1) * LANES)
            for m in range(0, fine_rows // SUB, 2):
                both = []
                for n in (m, m + 1):
                    start, index = sources[n]
                    lines = wide_ref[pl.ds(pl.multiple_of(l * side + start, SUB), SUB), span]
                    lines = jnp.take_along_axis(lines, index, axis=0)
                    both.append(lines * light_ref[n * SUB : (n + 1) * SUB, span])
                out_ref[l, m * SUB : (m + 2) * SUB, span] = jnp.concatenate(both, axis=0).astype(jnp.bfloat16)
        return carry

    lax.fori_loop(0, levels, spread, 0)


def heat(table, chl, light, land, levels, widen):
    side = land.shape[0]
    factor = light.shape[0] // side
    vmem = pl.BlockSpec(memory_space=pltpu.VMEM)
    return pl.pallas_call(
        functools.partial(heat_kernel, levels, side, factor),
        out_shape=jax.ShapeDtypeStruct((levels,) + light.shape, jnp.bfloat16),
        in_specs=[pl.BlockSpec(memory_space=pltpu.SMEM), vmem, vmem, vmem, vmem],
        out_specs=vmem,
        scratch_shapes=[
            pltpu.VMEM((side * levels, LANES), jnp.float32),
            pltpu.VMEM((side * levels, light.shape[1]), jnp.float32),
        ],
        compiler_params=pltpu.CompilerParams(vmem_limit_bytes=VMEM_LIMIT),
        name="heat",
    )(table, chl, light, land, widen)


def widened(x, rows, width):
    return jnp.pad(x, ((0, rows - x.shape[0]), (0, width - x.shape[1])))


def on_device(tracers, phys_fine, mix_coarse, surf_light, land_mask, owner_map):
    f32 = jnp.float32
    slot_count = tracers.shape[0]
    side = land_mask.shape[0]
    levels = mix_coarse.shape[2]
    tile_blocks = land_mask.shape[1] // side
    factor = phys_fine.shape[0] // side
    fine_cols = phys_fine.shape[1]
    group = LANES // side

    fine = jnp.transpose(phys_fine, (0, 2, 1))
    mix = jnp.transpose(mix_coarse, (0, 2, 1))
    wet = land_mask.astype(f32)
    width = fine_cols

    northward = jnp.concatenate(
        [
            widened(fine[-1, levels : 2 * levels, :].astype(f32), levels, width),
            widened(wet[-1:], 1, width),
        ],
        axis=0,
    )
    southward = widened(wet[:1], 1, width)
    last_face = jnp.mean(
        fine[:, :levels, fine_cols - 1].astype(f32).reshape(side, factor, levels), axis=1
    )
    face_pack = jnp.pad(
        last_face.reshape(side // group, group, levels // SUB, SUB).transpose(3, 1, 0, 2),
        ((0, 0), (0, 0), (0, 0), (0, group - levels // SUB)),
    ).reshape(SUB, LANES)
    eastward = jnp.concatenate([face_pack, widened(wet[:, -1][None], 1, LANES)], axis=0)
    westward = widened(wet[:, 0][None], 1, LANES)

    from_south = lax.ppermute(northward, "lat", along("lat", 1, False))
    from_north = lax.ppermute(southward, "lat", along("lat", -1, False))
    from_west = lax.ppermute(eastward, "lon", along("lon", 1, True))
    from_east = lax.ppermute(westward, "lon", along("lon", -1, True))

    fine_id = jnp.arange(fine_cols)[:, None]
    coarse_id = jnp.arange(land_mask.shape[1])[None, :]
    member = (fine_id // factor == coarse_id).astype(jnp.bfloat16)
    final = (fine_id == factor * coarse_id + factor - 1).astype(jnp.bfloat16)
    picks = jnp.concatenate([final, member], axis=1)

    table = routing(owner_map, slot_count, tile_blocks)
    def to_north(x):
        return lax.ppermute(x, "lat", along("lat", 1, False))

    def to_south(x):
        return lax.ppermute(x, "lat", along("lat", -1, False))

    def to_east(x):
        return lax.ppermute(x, "lon", along("lon", 1, True))

    def to_west(x):
        return lax.ppermute(x, "lon", along("lon", -1, True))

    def across(x):
        return lax.all_to_all(x, "lon", 0, 0, tiled=True)

    quads, west, east = first_edges(table, tracers, levels, side)
    quads = across(quads)
    rows = coarse_rows(fine, mix, picks)
    phys, line_phys = coarsen(
        table, rows, surf_light, land_mask, from_south, from_north, from_west, from_east, picks
    )
    phys = across(phys)
    low, high, low_in, high_in, ends = tile_lines(table, quads, levels, side)
    below, above = to_north(high), to_south(low)
    west, east = gate((west, east), phys)
    rim_w, rim_e = to_east(east), to_west(west)
    ends_w, ends_e = to_east(ends), to_west(ends)
    rims = across(hand_on(table, below, above, levels, side, phys, ends_w, ends_e))
    new_low, new_high = line_step(
        low, high, low_in, high_in, below, above, ends_w, ends_e, line_phys, levels
    )
    below, above = to_north(new_high), to_south(new_low)
    new_rims = across(hand_on(table, below, above, levels, side, rims, rim_w, rim_e))
    current, west, east = step(table, tracers, phys, rims, rim_w, rim_e, levels, side, False)
    current, chl = step(table, current, phys, new_rims, to_east(east), to_west(west), levels, side, True)
    chl = lax.all_to_all(chl, "lon", 0, 0, tiled=True)
    heating = heat(table, chl, surf_light, land_mask, levels, jnp.transpose(member))
    return current, heating


def solution(mesh):
    in_specs = (
        P(("lat", "lon"), None, None),
        P("lat", "lon", None),
        P("lat", "lon", None),
        P("lat", "lon"),
        P("lat", "lon"),
        P("lat", None),
    )
    out_specs = (P(("lat", "lon"), None, None), P(None, "lat", "lon"))
    return jax.shard_map(
        on_device, mesh=mesh, in_specs=in_specs, out_specs=out_specs, check_vma=False
    )
```

time: 312 us -> 276 us (0.88)
  blocking collectives: 109 us -> 0 us
  waiting for transfers between devices: 70.4 us -> 112 us
  starting transfers between devices: 38.9 us -> 55.5 us
  local copies, waits for them, and re-layouts: 7.16 us -> 19.5 us
  Pallas kernels: 77.3 us -> 83.3 us
    all_to_all x3 -> x0, blocking collectives: 109 us -> none  [the longest x2 64.8 us: hand(): return lax.all_to_all(handed, 'lon', 0, 0, tiled=True)]
    all_to_all x2 -> x4, waiting for transfers between devices: 0.01 us -> 27.5 us  [across(): return lax.all_to_all(x, 'lon', 0, 0, tiled=True)]
    ppermute x1, waiting for transfers between devices: 0.01 us -> 17.5 us  [on_device(): from_east = lax.ppermute(westward, 'lon', along('lon', -1, True))]
    all_to_all x2 -> x4, starting transfers between devices: 7.94 us -> 24.1 us  [across(): return lax.all_to_all(x, 'lon', 0, 0, tiled=True)]
    unnamed x31 -> x59, local copies, waits for them, and re-layouts: 6.64 us -> 19.1 us
    pallas_call x6 -> x8, Pallas kernels: 29.8 us -> 37.2 us  [the longest x1 10.6 us: coarse_rows(): pl.pallas_call(functools.partial(rows_kernel, levels, factor), out_shape=...]
    ppermute x2, waiting for transfers between devices: 4.93 us -> 0.01 us  [to_south(): return lax.ppermute(x, 'lat', along('lat', -1, False))]
    ppermute x4 -> x6, starting transfers between devices: 9.53 us -> 14.3 us  [the longest x3 8.18 us: to_west(): return lax.ppermute(x, 'lon', along('lon', -1, True))]
  transfers between devices with their start and end apart: 15 -> 19, of which waited for: 9 -> 9; matrix products, arithmetic and copies ran while one was open for 1% -> 1% of each run, Pallas kernels for 6% -> 16%
where the time goes in v2:
time: 276 us; the launch traced here: 274 us
  waiting for transfers between devices  112 us (41%)
  Pallas kernels  83.3 us (30%)
  starting transfers between devices  55.5 us (20%)
  local copies, waits for them, and re-layouts  19.5 us (7%)
    ppermute x3, waiting for transfers between devices, to_east(): return lax.ppermute(x, 'lon', along('lon', 1, True))  47.5 us
    pallas_call x2, Pallas kernels, step(): pl.pallas_call(functools.partial(step_kernel, levels, side, last), out_sh...  37.6 us
    all_to_all x4, waiting for transfers between devices, across(): return lax.all_to_all(x, 'lon', 0, 0, tiled=True)  27.5 us
    all_to_all x4, starting transfers between devices, across(): return lax.all_to_all(x, 'lon', 0, 0, tiled=True)  24.1 us
    unnamed x59, local copies, waits for them, and re-layouts  19.1 us
    ppermute x1, waiting for transfers between devices, on_device(): from_east = lax.ppermute(westward, 'lon', along('lon', -1, True))  17.5 us
    all_to_all x1, waiting for transfers between devices, on_device(): chl = lax.all_to_all(chl, 'lon', 0, 0, tiled=True)  12 us
    pallas_call x1, Pallas kernels, coarse_rows(): pl.pallas_call(functools.partial(rows_kernel, levels, factor), out_shape=...  10.6 us
  transfers between devices with their start and end apart: 19, of which 9 were waited for; matrix products, arithmetic and copies ran while one was open for 1% of the time, Pallas kernels for 16%

profile of v2, /device:TPU:0, one launch (start us, length us, event | category | flops | bytes accessed | tf_op | source)
XLA Modules:
  0.0 274.0 jit_solution(12613661625869954683)
XLA Ops:
  0.6 3.1 %routing.1.table_ref = s32[8,8]{1,0:T(8,128)} custom-call(s32[1,64]{1,0:T(1,128)} %row_ref.1), custom_call_target="tpu_custom_call" | custom-call | tf_op jit(solution)/shard_map/routing/pallas_call | solution.py:131
  4.4 8.5 %first_edges.1 = (f32[8,576,128]{2,1,0:T(8,128)S(1)}, f32[8,144,128]{2,1,0:T(8,128)S(1)}, f32[8,144,128]{2,1,0:T(8,128)S(1)}) custom-call(s32[8,8]{1,0:T(8,128)S(1)} %copy-done.17, f32[8,1152,256]{2,1,0:T(8,128)} %cell_ref.3), custom_call_target="tpu_custom_call" | custom-call | tf_op jit(solution)/shard_map/first_edges/pallas_call | solution.py:210
  16.0 7.4 %all-to-all-start.1 = ((f32[8,576,128]{2,1,0:T(8,128)}), f32[8,576,128]{2,1,0:T(8,128)S(1)}, u32[]{:S(2)}, u32[]{:S(2)}) async-start(f32[8,576,128]{2,1,0:T(8,128)} %copy-done.7), calls=%async_computation.1 | async-start | bytes 4718592 | tf_op jit(solution)/shard_map/all_to_all | solution.py:1069
  25.8 2.1 collective-permute-start.2
  31.3 2.8 %collective-permute-start.3 = (f32[1,128]{1,0:T(1,128)S(1)}, f32[1,128]{1,0:T(1,128)S(1)}, u32[]{:S(2)}, u32[]{:S(2)}) collective-permute-start(f32[1,128]{1,0:T(1,128)S(1)} %pad.22), channel_id=1, source_target_pairs={{0,7},{1,0},{2,1},{3,2},{4,3},{5,4},{6,5},{7,6},{8,15},{9,8},{10,9... | collective-permute-start | bytes 1544 | tf_op jit(solution)/shard_map/ppermute | solution.py:1047
  34.3 10.6 %coarse_rows.1.rows_ref = f32[16,192,128]{2,1,0:T(8,128)S(1)} custom-call(bf16[48,144,384]{2,1,0:T(8,128)(2,1)} %bitcast.13, bf16[16,48,128]{2,1,0:T(8,128)(2,1)S(1)} %bitcast.10, bf16[384,256]{1,0:T(8,128)(2,1)S(1)} %add_convert_fusion.pick_ref), custom_call_target="tpu_custom_call" | custom-call | tf_op jit(solution)/shard_map/coarse_rows/pallas_call | solution.py:580
  44.8 17.5 %collective-permute-done.3.east_ref = f32[1,128]{1,0:T(1,128)S(1)} collective-permute-done((f32[1,128]{1,0:T(1,128)S(1)}, f32[1,128]{1,0:T(1,128)S(1)}, u32[]{:S(2)}, u32[]{:S(2)}) %collective-permute-start.3) | collective-permute-done | bytes 544 | tf_op jit(solution)/shard_map/ppermute | solution.py:1047
  62.3 4.2 %collective-permute-done.2.west_ref = f32[9,128]{1,0:T(8,128)S(1)} collective-permute-done((f32[9,128]{1,0:T(8,128)S(1)}, f32[9,128]{1,0:T(8,128)S(1)}, u32[]{:S(2)}, u32[]{:S(2)}) %collective-permute-start.2) | collective-permute-done | bytes 4640 | tf_op jit(solution)/shard_map/ppermute | solution.py:1046
  66.5 3.6 %coarsen.1 = (f32[8,208,256]{2,1,0:T(8,128)S(1)}, f32[296,256]{1,0:T(8,128)S(1)}) custom-call(s32[8,8]{1,0:T(8,128)S(1)} %copy-done.18, f32[16,192,128]{2,1,0:T(8,128)S(1)} %coarse_rows.1.rows_ref, f32[48,384]{1,0:T(8,128)S(1)} %copy-done.21, s32[16,128]{1,0:T(8,128)S(1)} %copy-done.28, f32[49,384]{1,0:T(8,128)S(1)} %collective-permute-done.south_ref, ...), custom_call_target="tpu_custom_call" | custom-call | tf_op jit(solution)/shard_map/coarsen/pallas_call | solution.py:708
  72.0 5.0 %all-to-all-done.1.quad_ref = f32[8,576,128]{2,1,0:T(8,128)S(1)} async-done(((f32[8,576,128]{2,1,0:T(8,128)}), f32[8,576,128]{2,1,0:T(8,128)S(1)}, u32[]{:S(2)}, u32[]{:S(2)}) %all-to-all-start.1) | async-done | bytes 2359328 | tf_op jit(solution)/shard_map/all_to_all | solution.py:1069
  78.4 8.4 %all-to-all-start = ((f32[8,208,256]{2,1,0:T(8,128)}), f32[8,208,256]{2,1,0:T(8,128)S(1)}, u32[]{:S(2)}, u32[]{:S(2)}) async-start(f32[8,208,256]{2,1,0:T(8,128)} %copy-done.8), calls=%async_computation | async-start | bytes 3407872 | tf_op jit(solution)/shard_map/all_to_all | solution.py:1069
  88.5 6.8 %tile_lines.1 = (f32[1152,128]{1,0:T(8,128)S(1)}, f32[1152,128]{1,0:T(8,128)}, f32[1152,128]{1,0:T(8,128)S(1)}, f32[1152,128]{1,0:T(8,128)S(1)}, f32[48,128]{1,0:T(8,128)}) custom-call(s32[8,8]{1,0:T(8,128)S(1)} %copy-done.18, f32[8,576,128]{2,1,0:T(8,128)S(1)} %copy-done.3), custom_call_target="tpu_custom_call" | custom-call | tf_op jit(solution)/shard_map/tile_lines/pallas_call | solution.py:757
  99.6 2.0 collective-permute-start.6
  101.6 2.8 %collective-permute-start.7 = (f32[48,128]{1,0:T(8,128)}, f32[48,128]{1,0:T(8,128)S(1)}, u32[]{:S(2)}, u32[]{:S(2)}) collective-permute-start(f32[48,128]{1,0:T(8,128)} %get-tuple-element.25), channel_id=1, source_target_pairs={{0,7},{1,0},{2,1},{3,2},{4,3},{5,4},{6,5},{7,6},{8,15},{9,8},{10,9... | collective-permute-start | bytes 73736 | tf_op jit(solution)/shard_map/ppermute | solution.py:1066
  104.4 22.4 %all-to-all-done.refs_0_.refs_2_.phys_ref = f32[8,208,256]{2,1,0:T(8,128)S(1)} async-done(((f32[8,208,256]{2,1,0:T(8,128)}), f32[8,208,256]{2,1,0:T(8,128)S(1)}, u32[]{:S(2)}, u32[]{:S(2)}) %all-to-all-start) | async-done | bytes 1703968 | tf_op jit(solution)/shard_map/all_to_all | solution.py:1069
  126.8 3.2 %hand_on.2 = f32[8,288,128]{2,1,0:T(8,128)} custom-call(s32[8,8]{1,0:T(8,128)S(1)} %copy-done.18, f32[1152,128]{1,0:T(8,128)S(1)} %collective-permute-done.4.below_ref, f32[1152,128]{1,0:T(8,128)S(1)} %collective-permute-done.5.above_ref, f32[8,208,256]{2,1,0:T(8,128)S(1)} %all-to-all-done.refs_0_.refs_2_.phys_ref, ...), custom_call_target="tpu_custom_call" | custom-call | tf_op jit(solution)/shard_map/hand_on/pallas_call | solution.py:894
  130.0 3.6 %all-to-all-start.2 = ((f32[8,288,128]{2,1,0:T(8,128)}), f32[8,288,128]{2,1,0:T(8,128)S(1)}, u32[]{:S(2)}, u32[]{:S(2)}) async-start(f32[8,288,128]{2,1,0:T(8,128)} %hand_on.2), calls=%async_computation.2 | async-start | bytes 2359296 | tf_op jit(solution)/shard_map/all_to_all | solution.py:1069
  133.6 2.0 collective-permute-start.8
  135.6 2.8 %collective-permute-start.9 = (f32[8,144,128]{2,1,0:T(8,128)}, f32[8,144,128]{2,1,0:T(8,128)S(1)}, u32[]{:S(2)}, u32[]{:S(2)}) collective-permute-start(f32[8,144,128]{2,1,0:T(8,128)} %get-tuple-element.29), channel_id=1, source_target_pairs={{0,7},{1,0},{2,1},{3,2},{4,3},{5,4},{6,5},{7,6},{8,15},{9,8},{10,9... | collective-permute-start | bytes 1769480 | tf_op jit(solution)/shard_map/ppermute | solution.py:1066
  144.0 2.4 line_step.1
  149.1 22.9 %collective-permute-done.8.rim_w_ref.refs_1_ = f32[8,144,128]{2,1,0:T(8,128)S(1)} collective-permute-done((f32[8,144,128]{2,1,0:T(8,128)}, f32[8,144,128]{2,1,0:T(8,128)S(1)}, u32[]{:S(2)}, u32[]{:S(2)}) %collective-permute-start.8) | collective-permute-done | bytes 589856 | tf_op jit(solution)/shard_map/ppermute | solution.py:1063
  172.0 2.1 collective-permute-done.9.rim_e_ref.refs_2_
  174.1 2.2 hand_on.3
  178.1 4.7 %all-to-all-start.3 = ((f32[8,288,128]{2,1,0:T(8,128)}), f32[8,288,128]{2,1,0:T(8,128)}, u32[]{:S(2)}, u32[]{:S(2)}) async-start(f32[8,288,128]{2,1,0:T(8,128)} %copy-done.4), calls=%async_computation.3 | async-start | bytes 2359296 | tf_op jit(solution)/shard_map/all_to_all | solution.py:1069
  183.8 19.2 %step.2 = (f32[8,1152,256]{2,1,0:T(8,128)}, f32[8,144,128]{2,1,0:T(8,128)S(1)}, f32[8,144,128]{2,1,0:T(8,128)S(1)}) custom-call(s32[8,8]{1,0:T(8,128)S(1)} %copy-done.18, f32[8,1152,256]{2,1,0:T(8,128)} %cell_ref.3, f32[8,208,256]{2,1,0:T(8,128)S(1)} %copy-done.1, f32[8,288,128]{2,1,0:T(8,128)S(1)} %all-to-all-done.2.rim_ref.refs_0_, ...), custom_call_target="tpu_custom_call" | custom-call | tf_op jit(solution)/shard_map/step/pallas_call | solution.py:534
  203.1 2.1 collective-permute-start.12
  205.1 2.7 collective-permute-start.13
  207.8 24.6 %collective-permute-done.12.rim_w_ref = f32[8,144,128]{2,1,0:T(8,128)S(1)} collective-permute-done((f32[8,144,128]{2,1,0:T(8,128)S(1)}, f32[8,144,128]{2,1,0:T(8,128)S(1)}, u32[]{:S(2)}, u32[]{:S(2)}) %collective-permute-start.12) | collective-permute-done | bytes 589856 | tf_op jit(solution)/shard_map/ppermute | solution.py:1063
  233.7 18.4 %step.3 = (f32[8,1152,256]{2,1,0:T(8,128)}, f32[8,48,256]{2,1,0:T(8,128)}) custom-call(s32[8,8]{1,0:T(8,128)S(1)} %copy-done.18, f32[8,1152,256]{2,1,0:T(8,128)} %get-tuple-element.30.cell_ref, f32[8,208,256]{2,1,0:T(8,128)S(1)} %copy-done.1, f32[8,288,128]{2,1,0:T(8,128)} %all-to-all-done.3.rim_ref, f32[8,144,128]{2,1,0:T(8,128)S(1)} %collective-permute-done.12.rim_w_ref, ...), custom_call_target="tpu_custom_call" | custom-call | tf_op jit(solution)/shard_map/step/pallas_call | solution.py:534
  252.1 4.4 %all-to-all-start.4 = ((f32[8,48,256]{2,1,0:T(8,128)}), f32[8,48,256]{2,1,0:T(8,128)S(1)}, u32[]{:S(2)}, u32[]{:S(2)}) async-start(f32[8,48,256]{2,1,0:T(8,128)} %get-tuple-element.39), calls=%async_computation.4 | async-start | bytes 786432 | tf_op jit(solution)/shard_map/all_to_all | solution.py:1091
  256.5 12.0 %all-to-all-done.4.chl_ref = f32[8,48,256]{2,1,0:T(8,128)S(1)} async-done(((f32[8,48,256]{2,1,0:T(8,128)}), f32[8,48,256]{2,1,0:T(8,128)S(1)}, u32[]{:S(2)}, u32[]{:S(2)}) %all-to-all-start.4) | async-done | bytes 393248 | tf_op jit(solution)/shard_map/all_to_all | solution.py:1091
  268.5 5.4 %heat.1 = bf16[48,48,384]{2,1,0:T(8,128)(2,1)} custom-call(s32[8,8]{1,0:T(8,128)S(1)} %copy-done.18, f32[8,48,256]{2,1,0:T(8,128)S(1)} %all-to-all-done.4.chl_ref, f32[48,384]{1,0:T(8,128)S(1)} %copy-done.22, s32[16,128]{1,0:T(8,128)S(1)} %copy-done.28, bf16[128,384]{1,0:T(8,128)(2,1)S(1)} %fusion.widen_ref), custom_call_target="tpu_custom_call" | custom-call | tf_op jit(solution)/shard_map/heat/pallas_call | solution.py:993
  (97 shorter events, 31.4 us)
Async XLA Ops:
  12.9 1.4 copy-start.7
  16.0 9.6 %copy-start.28 = (s32[16,128]{1,0:T(8,128)S(1)}, s32[16,128]{1,0:T(8,128)}, u32[]{:S(2)}) copy-start(s32[16,128]{1,0:T(8,128)} %land_ref.3) | copy-start | bytes 24580
  16.0 61.0 %all-to-all-start.1 = ((f32[8,576,128]{2,1,0:T(8,128)}), f32[8,576,128]{2,1,0:T(8,128)S(1)}, u32[]{:S(2)}, u32[]{:S(2)}) async-start(f32[8,576,128]{2,1,0:T(8,128)} %copy-done.7), calls=%async_computation.1 | async-start | bytes 4718592 | tf_op jit(solution)/shard_map/all_to_all | solution.py:1069
  23.4 10.8 %copy-start.23 = (bf16[16,128,48]{1,2,0:T(8,128)(2,1)S(1)}, bf16[16,128,48]{1,2,0:T(8,128)(2,1)}, u32[]{:S(2)}) copy-start(bf16[16,128,48]{1,2,0:T(8,128)(2,1)} %param.8) | copy-start | bytes 589828
  25.8 40.7 %collective-permute-start.2 = (f32[9,128]{1,0:T(8,128)S(1)}, f32[9,128]{1,0:T(8,128)S(1)}, u32[]{:S(2)}, u32[]{:S(2)}) collective-permute-start(f32[9,128]{1,0:T(8,128)S(1)} %select_maximum_fusion.1), channel_id=1, source_target_pairs={{0,1},{1,2},{2,3},{3,4},{4,5},{5,6},{6,7},{7,0},{8,9},{9,10},{10,1... | collective-permute-start | bytes 13832 | tf_op jit(solution)/shard_map/ppermute | solution.py:1046
  28.6 37.8 %collective-permute-start = (f32[49,384]{1,0:T(8,128)S(1)}, f32[49,384]{1,0:T(8,128)S(1)}, u32[]{:S(2)}, u32[]{:S(2)}) collective-permute-start(f32[49,384]{1,0:T(8,128)S(1)} %select_maximum_fusion), channel_id=1, source_target_pairs={{0,8},{8,16},{16,24},{1,9},{9,17},{17,25},{2,10},{10,18},{18,26},{... | collective-permute-start | bytes 225800 | tf_op jit(solution)/shard_map/ppermute | solution.py:1044
  30.0 32.3 %collective-permute-start.1 = (f32[1,384]{1,0:T(1,128)S(1)}, f32[1,384]{1,0:T(1,128)S(1)}, u32[]{:S(2)}, u32[]{:S(2)}) collective-permute-start(f32[1,384]{1,0:T(1,128)S(1)} %pad.19), channel_id=1, source_target_pairs={{8,0},{16,8},{24,16},{9,1},{17,9},{25,17},{10,2},{18,10},{26,18},{... | collective-permute-start | bytes 4616 | tf_op jit(solution)/shard_map/ppermute | solution.py:1045
  31.3 31.0 %collective-permute-start.3 = (f32[1,128]{1,0:T(1,128)S(1)}, f32[1,128]{1,0:T(1,128)S(1)}, u32[]{:S(2)}, u32[]{:S(2)}) collective-permute-start(f32[1,128]{1,0:T(1,128)S(1)} %pad.22), channel_id=1, source_target_pairs={{0,7},{1,0},{2,1},{3,2},{4,3},{5,4},{6,5},{7,6},{8,15},{9,8},{10,9... | collective-permute-start | bytes 1544 | tf_op jit(solution)/shard_map/ppermute | solution.py:1047
  34.2 32.2 %copy-start.18 = (s32[8,8]{1,0:T(8,128)S(1)}, s32[8,8]{1,0:T(8,128)}, u32[]{:S(2)}) copy-start(s32[8,8]{1,0:T(8,128)} %routing.1.table_ref) | copy-start | bytes 772
  34.3 32.2 %copy-start.21 = (f32[48,384]{1,0:T(8,128)S(1)}, f32[48,384]{1,0:T(8,128)}, u32[]{:S(2)}) copy-start(f32[48,384]{1,0:T(8,128)} %light_ref.3) | copy-start | bytes 221188
  77.0 1.4 copy-start.2
  78.4 48.4 %all-to-all-start = ((f32[8,208,256]{2,1,0:T(8,128)}), f32[8,208,256]{2,1,0:T(8,128)S(1)}, u32[]{:S(2)}, u32[]{:S(2)}) async-start(f32[8,208,256]{2,1,0:T(8,128)} %copy-done.8), calls=%async_computation | async-start | bytes 3407872 | tf_op jit(solution)/shard_map/all_to_all | solution.py:1069
  86.8 1.7 copy-start.3
  96.9 33.1 %copy-start.11 = (f32[1152,128]{1,0:T(8,128)}, f32[1152,128]{1,0:T(8,128)S(1)}, u32[]{:S(2)}) copy-start(f32[1152,128]{1,0:T(8,128)S(1)} %get-tuple-element.24.low_ref) | copy-start | bytes 1769476
  96.9 29.9 %collective-permute-start.4 = (f32[1152,128]{1,0:T(8,128)}, f32[1152,128]{1,0:T(8,128)S(1)}, u32[]{:S(2)}, u32[]{:S(2)}) collective-permute-start(f32[1152,128]{1,0:T(8,128)} %get-tuple-element.23.high_ref), channel_id=1, source_target_pairs={{0,8},{8,16},{16,24},{1,9},{9,17},{17,25},{2,10},{10,18},{18,26},{... | collective-permute-start | bytes 1769480 | tf_op jit(solution)/shard_map/ppermute | solution.py:1057
  98.3 28.5 %collective-permute-start.5 = (f32[1152,128]{1,0:T(8,128)S(1)}, f32[1152,128]{1,0:T(8,128)S(1)}, u32[]{:S(2)}, u32[]{:S(2)}) collective-permute-start(f32[1152,128]{1,0:T(8,128)S(1)} %get-tuple-element.24.low_ref), channel_id=1, source_target_pairs={{8,0},{16,8},{24,16},{9,1},{17,9},{25,17},{10,2},{18,10},{26,18},{... | collective-permute-start | bytes 1769480 | tf_op jit(solution)/shard_map/ppermute | solution.py:1060
  99.6 27.2 %collective-permute-start.6 = (f32[48,128]{1,0:T(8,128)}, f32[48,128]{1,0:T(8,128)S(1)}, u32[]{:S(2)}, u32[]{:S(2)}) collective-permute-start(f32[48,128]{1,0:T(8,128)} %get-tuple-element.25), channel_id=1, source_target_pairs={{0,1},{1,2},{2,3},{3,4},{4,5},{5,6},{6,7},{7,0},{8,9},{9,10},{10,1... | collective-permute-start | bytes 73736 | tf_op jit(solution)/shard_map/ppermute | solution.py:1063
  101.6 25.2 %collective-permute-start.7 = (f32[48,128]{1,0:T(8,128)}, f32[48,128]{1,0:T(8,128)S(1)}, u32[]{:S(2)}, u32[]{:S(2)}) collective-permute-start(f32[48,128]{1,0:T(8,128)} %get-tuple-element.25), channel_id=1, source_target_pairs={{0,7},{1,0},{2,1},{3,2},{4,3},{5,4},{6,5},{7,6},{8,15},{9,8},{10,9... | collective-permute-start | bytes 73736 | tf_op jit(solution)/shard_map/ppermute | solution.py:1066
  126.8 3.2 %copy-start = (f32[8,208,256]{2,1,0:T(8,128)}, f32[8,208,256]{2,1,0:T(8,128)S(1)}, u32[]{:S(2)}) copy-start(f32[8,208,256]{2,1,0:T(8,128)S(1)} %all-to-all-done.refs_0_.refs_2_.phys_ref) | copy-start | bytes 5111812
  126.8 3.2 %copy-start.24 = (f32[48,128]{1,0:T(8,128)}, f32[48,128]{1,0:T(8,128)S(1)}, u32[]{:S(2)}) copy-start(f32[48,128]{1,0:T(8,128)S(1)} %collective-permute-done.6.refs_1_.west_ref) | copy-start | bytes 73732
  126.8 3.2 %copy-start.26 = (f32[48,128]{1,0:T(8,128)}, f32[48,128]{1,0:T(8,128)S(1)}, u32[]{:S(2)}) copy-start(f32[48,128]{1,0:T(8,128)S(1)} %collective-permute-done.7.refs_2_.east_ref) | copy-start | bytes 73732
  130.0 44.1 %all-to-all-start.2 = ((f32[8,288,128]{2,1,0:T(8,128)}), f32[8,288,128]{2,1,0:T(8,128)S(1)}, u32[]{:S(2)}, u32[]{:S(2)}) async-start(f32[8,288,128]{2,1,0:T(8,128)} %hand_on.2), calls=%async_computation.2 | async-start | bytes 2359296 | tf_op jit(solution)/shard_map/all_to_all | solution.py:1069
  133.6 38.4 %collective-permute-start.8 = (f32[8,144,128]{2,1,0:T(8,128)}, f32[8,144,128]{2,1,0:T(8,128)S(1)}, u32[]{:S(2)}, u32[]{:S(2)}) collective-permute-start(f32[8,144,128]{2,1,0:T(8,128)} %get-tuple-element.28), channel_id=1, source_target_pairs={{0,1},{1,2},{2,3},{3,4},{4,5},{5,6},{6,7},{7,0},{8,9},{9,10},{10,1... | collective-permute-start | bytes 1769480 | tf_op jit(solution)/shard_map/ppermute | solution.py:1063
  135.6 38.4 %collective-permute-start.9 = (f32[8,144,128]{2,1,0:T(8,128)}, f32[8,144,128]{2,1,0:T(8,128)S(1)}, u32[]{:S(2)}, u32[]{:S(2)}) collective-permute-start(f32[8,144,128]{2,1,0:T(8,128)} %get-tuple-element.29), channel_id=1, source_target_pairs={{0,7},{1,0},{2,1},{3,2},{4,3},{5,4},{6,5},{7,6},{8,15},{9,8},{10,9... | collective-permute-start | bytes 1769480 | tf_op jit(solution)/shard_map/ppermute | solution.py:1066
  146.5 27.6 %collective-permute-start.10 = (f32[1152,128]{1,0:T(8,128)S(1)}, f32[1152,128]{1,0:T(8,128)S(1)}, u32[]{:S(2)}, u32[]{:S(2)}) collective-permute-start(f32[1152,128]{1,0:T(8,128)S(1)} %get-tuple-element.34), channel_id=1, source_target_pairs={{0,8},{8,16},{16,24},{1,9},{9,17},{17,25},{2,10},{10,18},{18,26},{... | collective-permute-start | bytes 1769480 | tf_op jit(solution)/shard_map/ppermute | solution.py:1057
  147.8 26.3 %collective-permute-start.11 = (f32[1152,128]{1,0:T(8,128)S(1)}, f32[1152,128]{1,0:T(8,128)S(1)}, u32[]{:S(2)}, u32[]{:S(2)}) collective-permute-start(f32[1152,128]{1,0:T(8,128)S(1)} %get-tuple-element.35), channel_id=1, source_target_pairs={{8,0},{16,8},{24,16},{9,1},{17,9},{25,17},{10,2},{18,10},{26,18},{... | collective-permute-start | bytes 1769480 | tf_op jit(solution)/shard_map/ppermute | solution.py:1060
  178.1 4.7 %copy-start.1 = (f32[8,208,256]{2,1,0:T(8,128)S(1)}, f32[8,208,256]{2,1,0:T(8,128)}, u32[]{:S(2)}) copy-start(f32[8,208,256]{2,1,0:T(8,128)} %copy-done) | copy-start | bytes 5111812
  178.1 55.6 %all-to-all-start.3 = ((f32[8,288,128]{2,1,0:T(8,128)}), f32[8,288,128]{2,1,0:T(8,128)}, u32[]{:S(2)}, u32[]{:S(2)}) async-start(f32[8,288,128]{2,1,0:T(8,128)} %copy-done.4), calls=%async_computation.3 | async-start | bytes 2359296 | tf_op jit(solution)/shard_map/all_to_all | solution.py:1069
  203.1 29.3 %collective-permute-start.12 = (f32[8,144,128]{2,1,0:T(8,128)S(1)}, f32[8,144,128]{2,1,0:T(8,128)S(1)}, u32[]{:S(2)}, u32[]{:S(2)}) collective-permute-start(f32[8,144,128]{2,1,0:T(8,128)S(1)} %get-tuple-element.36), channel_id=1, source_target_pairs={{0,1},{1,2},{2,3},{3,4},{4,5},{5,6},{6,7},{7,0},{8,9},{9,10},{10,1... | collective-permute-start | bytes 1769480 | tf_op jit(solution)/shard_map/ppermute | solution.py:1063
  205.1 28.6 %collective-permute-start.13 = (f32[8,144,128]{2,1,0:T(8,128)S(1)}, f32[8,144,128]{2,1,0:T(8,128)S(1)}, u32[]{:S(2)}, u32[]{:S(2)}) collective-permute-start(f32[8,144,128]{2,1,0:T(8,128)S(1)} %get-tuple-element.37), channel_id=1, source_target_pairs={{0,7},{1,0},{2,1},{3,2},{4,3},{5,4},{6,5},{7,6},{8,15},{9,8},{10,9... | collective-permute-start | bytes 1769480 | tf_op jit(solution)/shard_map/ppermute | solution.py:1066
  233.7 34.8 %copy-start.22 = (f32[48,384]{1,0:T(8,128)S(1)}, f32[48,384]{1,0:T(8,128)}, u32[]{:S(2)}) copy-start(f32[48,384]{1,0:T(8,128)} %light_ref.3) | copy-start | bytes 221188
  252.1 16.5 %all-to-all-start.4 = ((f32[8,48,256]{2,1,0:T(8,128)}), f32[8,48,256]{2,1,0:T(8,128)S(1)}, u32[]{:S(2)}, u32[]{:S(2)}) async-start(f32[8,48,256]{2,1,0:T(8,128)} %get-tuple-element.39), calls=%async_computation.4 | async-start | bytes 786432 | tf_op jit(solution)/shard_map/all_to_all | solution.py:1091
  (16 other events, 14.4 us)

commit v3 on v2

--- a/solution.py
+++ b/solution.py
@@ -318,7 +318,7 @@
     ]
 
 
-def set_transport(coef_ref, at, span, faces, opens):
+def transport(faces, opens):
     flow_e, flow_n, flow_w, flow_s = (face * is_open for face, is_open in zip(faces, opens))
     open_e, open_n, open_w, open_s = opens
     out_e, in_e = jnp.maximum(flow_e, 0.0), jnp.minimum(flow_e, 0.0)
@@ -326,11 +326,13 @@
     in_w, out_w = jnp.maximum(flow_w, 0.0), jnp.minimum(flow_w, 0.0)
     in_s, out_s = jnp.maximum(flow_s, 0.0), jnp.minimum(flow_s, 0.0)
     drift = diffuse_rate * (open_w + open_e + open_s + open_n)
-    coef_ref[0, at, span] = 1.0 - (out_e - out_w) - (out_n - out_s) - drift
-    coef_ref[1, at, span] = diffuse_rate * open_e - in_e
-    coef_ref[2, at, span] = diffuse_rate * open_w + in_w
-    coef_ref[3, at, span] = diffuse_rate * open_n - in_n
-    coef_ref[4, at, span] = diffuse_rate * open_s + in_s
+    return (
+        1.0 - (out_e - out_w) - (out_n - out_s) - drift,
+        diffuse_rate * open_e - in_e,
+        diffuse_rate * open_w + in_w,
+        diffuse_rate * open_n - in_n,
+        diffuse_rate * open_s + in_s,
+    )
 
 
 def set_mixing(coef_ref, at, span, mix, above, bottom):
@@ -384,14 +386,113 @@
     lax.fori_loop(0, levels // SUB, reacting, start, unroll=True)
 
 
-def step_kernel(levels, side, last, table_ref, cell_ref, phys_ref, rim_ref, rim_w_ref, rim_e_ref, *refs):
+def block_faces(phys_ref, spans, levels, side, lt):
+    group = LANES // side
+    pack_at = 4 * levels + SUB
+    lane = lane_ids()
+    first_col = (lane & (side - 1)) == 0
+    first_row = lane < side
+    west_pack = phys_ref[0, pack_at : pack_at + SUB, spans[0]]
+    south_pack = phys_ref[0, pack_at : pack_at + SUB, spans[1]]
+    east = [phys_ref[0, lt * SUB : (lt + 1) * SUB, span] for span in spans]
+    north = [phys_ref[0, levels + lt * SUB : levels + (lt + 1) * SUB, span] for span in spans]
+    faces = []
+    for h in range(len(spans)):
+        west = jnp.where(first_col, turned(west_pack, -(h * group + lt)), turned(east[h], 1))
+        before = turned(south_pack, -side * lt) if h == 0 else turned(north[h - 1], side)
+        south = jnp.where(first_row, before, turned(north[h], side))
+        faces.append((east[h], north[h], west, south))
+    return faces
+
+
+def inner_kernel(levels, side, table_ref, cell_ref, phys_ref, out_ref, coef_ref):
+    channels, cell_count = cell_ref.shape[1:]
+    tracer_count = channels // levels
+    halves = cell_count // LANES
+    level_tiles = levels // SUB
+    spans = [slice(h * LANES, (h + 1) * LANES) for h in range(halves)]
+    full = table_ref[SLOT_FULL, pl.program_id(0)] == 1
+
+    @pl.when(jnp.logical_not(full))
+    def _():
+        out_ref[...] = jnp.zeros_like(out_ref)
+
+    @pl.when(full)
+    def _():
+        lane = lane_ids()
+        col = lane & (side - 1)
+        first_row = lane < side
+        last_row = lane >= LANES - side
+        flag_row = 4 * levels
+
+        def flag(f, h):
+            return phys_ref[0, flag_row + f : flag_row + f + 1, spans[h]]
+
+        for lt in range(level_tiles):
+            at = slice(lt * SUB, (lt + 1) * SUB)
+            for h, faces in enumerate(block_faces(phys_ref, spans, levels, side, lt)):
+                c, e, w, n, s = transport(faces, [flag(f, h) for f in range(4)])
+                e = jnp.where(col == side - 1, 0.0, e)
+                w = jnp.where(col == 0, 0.0, w)
+                if h == halves - 1:
+                    n = jnp.where(last_row, 0.0, n)
+                if h == 0:
+                    s = jnp.where(first_row, 0.0, s)
+                for k, value in enumerate((c, e, w, n, s)):
+                    coef_ref[k, at, spans[h]] = value
+
+        def advect(lt, carry):
+            at = pl.multiple_of(lt * SUB, SUB)
+            coef = [[coef_ref[n, pl.ds(at, SUB), span] for n in range(5)] for span in spans]
+            for t in range(tracer_count):
+                chan = pl.multiple_of(t * levels + lt * SUB, SUB)
+                here = [cell_ref[0, pl.ds(chan, SUB), span] for span in spans]
+                up = [turned(value, side) for value in here]
+                down = [turned(value, -side) for value in here]
+                for h in range(halves):
+                    south = up[h] if h == 0 else jnp.where(first_row, up[h - 1], up[h])
+                    north = down[h] if h == halves - 1 else jnp.where(last_row, down[h + 1], down[h])
+                    c, e, w, n, s = coef[h]
+                    out_ref[0, pl.ds(chan, SUB), spans[h]] = (
+                        c * here[h]
+                        + (e * turned(here[h], -1) + w * turned(here[h], 1))
+                        + (n * north + s * south)
+                    )
+            return carry
+
+        lax.fori_loop(0, level_tiles, advect, 0, unroll=True)
+
+
+def inner(table, cells, phys, levels, side):
+    slot_count, channels, cell_count = cells.shape
+    phys_rows = phys.shape[1]
+    by_slot = pl.BlockSpec((1, channels, cell_count), lambda s, t: (s, 0, 0))
+    return pl.pallas_call(
+        functools.partial(inner_kernel, levels, side),
+        out_shape=jax.ShapeDtypeStruct(cells.shape, jnp.float32),
+        grid_spec=pltpu.PrefetchScalarGridSpec(
+            num_scalar_prefetch=1,
+            grid=(slot_count,),
+            in_specs=[
+                by_slot,
+                pl.BlockSpec((1, phys_rows, cell_count), lambda s, t: (t[SLOT_TILE, s], 0, 0)),
+            ],
+            out_specs=by_slot,
+            scratch_shapes=[pltpu.VMEM((5, levels, cell_count), jnp.float32)],
+        ),
+        compiler_params=pltpu.CompilerParams(vmem_limit_bytes=VMEM_LIMIT),
+        name="inner",
+    )(table, cells, phys)
+
+
+def step_kernel(levels, side, last, table_ref, part_ref, phys_ref, rim_ref, rim_w_ref, rim_e_ref, *refs):
     if last:
         out_ref, chl_ref, coef_ref, moved_ref, ends_ref = refs
         edge_refs = (chl_ref,)
     else:
         out_ref, west_ref, east_ref, coef_ref, moved_ref, ends_ref = refs
         edge_refs = (west_ref, east_ref)
-    channels, cell_count = cell_ref.shape[1:]
+    channels, cell_count = part_ref.shape[1:]
     tracer_count = channels // levels
     group = LANES // side
     halves = cell_count // LANES
@@ -412,47 +513,24 @@
     def _():
         lane = lane_ids()
         col = lane & (side - 1)
-        first_col = col == 0
-        last_col = col == side - 1
         first_row = lane < side
         last_row = lane >= LANES - side
         odd = (lane & 1) == 1
         flag_row = 4 * levels
-        pack_at = flag_row + SUB
 
         def flag(f, h):
             return phys_ref[0, flag_row + f : flag_row + f + 1, spans[h]]
 
-        def southward(values, edge):
-            out = []
-            for h in range(halves):
-                before = edge if h == 0 else turned(values[h - 1], side)
-                out.append(jnp.where(first_row, before, turned(values[h], side)))
-            return out
-
-        def northward(values, edge):
-            out = []
-            for h in range(halves):
-                after = edge if h == halves - 1 else turned(values[h + 1], -side)
-                out.append(jnp.where(last_row, after, turned(values[h], -side)))
-            return out
-
         above_mix = [jnp.zeros((SUB, LANES), jnp.float32)] * halves
-        west_pack = phys_ref[0, pack_at : pack_at + SUB, spans[0]]
-        south_pack = phys_ref[0, pack_at : pack_at + SUB, spans[1]]
         for lt in range(level_tiles):
             at = slice(lt * SUB, (lt + 1) * SUB)
-            east_face = [phys_ref[0, lt * SUB : (lt + 1) * SUB, spans[h]] for h in range(halves)]
-            north_face = [
-                phys_ref[0, levels + lt * SUB : levels + (lt + 1) * SUB, spans[h]] for h in range(halves)
-            ]
-            south_face = southward(north_face, turned(south_pack, -side * lt))
-            for h in range(halves):
-                west_face = jnp.where(
-                    first_col, turned(west_pack, -(h * group + lt)), turned(east_face[h], 1)
-                )
-                faces = (east_face[h], north_face[h], west_face, south_face[h])
-                set_transport(coef_ref, at, spans[h], faces, [flag(f, h) for f in range(4)])
+            for h, faces in enumerate(block_faces(phys_ref, spans, levels, side, lt)):
+                _, e, w, n, s = transport(faces, [flag(f, h) for f in range(4)])
+                coef_ref[0, at, spans[h]] = jnp.where(col == 0, w, jnp.where(col == side - 1, e, 0.0))
+                if h == 0:
+                    coef_ref[1, at, spans[h]] = jnp.where(first_row, s, 0.0)
+                if h == halves - 1:
+                    coef_ref[1, at, spans[h]] = jnp.where(last_row, n, 0.0)
                 mix = phys_ref[0, 3 * levels + lt * SUB : 3 * levels + (lt + 1) * SUB, spans[h]]
                 set_mixing(coef_ref, at, spans[h], mix, above_mix[h], lt == level_tiles - 1)
                 above_mix[h] = mix
@@ -461,9 +539,8 @@
             ends_ref[at : at + SUB, :] = turned(rim_w_ref[0, at : at + SUB, :], 2 - 2 * side)
         set_blank(moved_ref, channels)
 
-        def advect(lt, carry):
+        def gather(lt, carry):
             at = pl.multiple_of(lt * SUB, SUB)
-            coef = [[coef_ref[n, pl.ds(at, SUB), spans[h]] for n in range(5)] for h in range(halves)]
             for i in range(rounds):
                 row = pl.multiple_of(i * levels + lt * SUB, SUB)
                 rims = [
@@ -475,21 +552,17 @@
                 sides = [jnp.where(odd, ends_e, ends_w), jnp.where(odd, ends_w, ends_e)]
                 for g in range(group):
                     chan = pl.multiple_of((i * group + g) * levels + lt * SUB, SUB)
-                    here = [cell_ref[0, pl.ds(chan, SUB), spans[h]] for h in range(halves)]
                     rim = turned(rims[2 * g // group], -side - 2 * side * (g % (group // 2)))
-                    south = southward(here, rim)
-                    north = northward(here, rim)
                     for h in range(halves):
                         ends = turned(sides[h], side - 2 + h - 2 * g)
-                        west = jnp.where(first_col, ends, turned(here[h], 1))
-                        east = jnp.where(last_col, ends, turned(here[h], -1))
-                        c, e, w, n, s = coef[h]
-                        moved_ref[pl.ds(pl.multiple_of(SUB + chan, SUB), SUB), spans[h]] = (
-                            c * here[h] + (e * east + w * west) + (n * north[h] + s * south[h])
-                        )
+                        moved = part_ref[0, pl.ds(chan, SUB), spans[h]]
+                        moved = moved + coef_ref[0, pl.ds(at, SUB), spans[h]] * ends
+                        if h in (0, halves - 1):
+                            moved = moved + coef_ref[1, pl.ds(at, SUB), spans[h]] * rim
+                        moved_ref[pl.ds(pl.multiple_of(SUB + chan, SUB), SUB), spans[h]] = moved
             return carry
 
-        lax.fori_loop(0, level_tiles, advect, 0, unroll=True)
+        lax.fori_loop(0, level_tiles, gather, 0, unroll=True)
 
         def store(t, at, h, value):
             if t is not None:
@@ -806,7 +879,8 @@
             faces = [
                 phys_ref[n * levels + lt * SUB : n * levels + (lt + 1) * SUB, spans[h]] for n in (0, 1, 4, 5)
             ]
-            set_transport(coef_ref, at, spans[h], faces, [flag(f, h) for f in range(4)])
+            for n, value in enumerate(transport(faces, [flag(f, h) for f in range(4)])):
+                coef_ref[n, at, spans[h]] = value
             mix = phys_ref[3 * levels + lt * SUB : 3 * levels + (lt + 1) * SUB, spans[h]]
             set_mixing(coef_ref, at, spans[h], mix, above_mix[h], lt == level_tiles - 1)
             above_mix[h] = mix
@@ -1085,9 +1159,13 @@
         low, high, low_in, high_in, below, above, ends_w, ends_e, line_phys, levels
     )
     below, above = to_north(new_high), to_south(new_low)
-    new_rims = across(hand_on(table, below, above, levels, side, rims, rim_w, rim_e))
-    current, west, east = step(table, tracers, phys, rims, rim_w, rim_e, levels, side, False)
-    current, chl = step(table, current, phys, new_rims, to_east(east), to_west(west), levels, side, True)
+    partial = inner(table, tracers, phys, levels, side)
+    (handed,) = gate((hand_on(table, below, above, levels, side),), rims, rim_w, rim_e, partial)
+    new_rims = across(handed)
+    current, west, east = step(table, partial, phys, rims, rim_w, rim_e, levels, side, False)
+    rim_w, rim_e = to_east(east), to_west(west)
+    partial = inner(table, current, phys, levels, side)
+    current, chl = step(table, partial, phys, new_rims, rim_w, rim_e, levels, side, True)
     chl = lax.all_to_all(chl, "lon", 0, 0, tiled=True)
     heating = heat(table, chl, surf_light, land_mask, levels, jnp.transpose(member))
     return current, heating

time: 276 us -> 268 us (0.971)
  waiting for transfers between devices: 112 us -> 82.4 us
  Pallas kernels: 83.3 us -> 103 us
    ppermute x3, waiting for transfers between devices: 47.5 us -> 15.3 us  [to_east(): return lax.ppermute(x, 'lon', along('lon', 1, True))]
    pallas_call x0 -> x2, Pallas kernels: none -> 29.8 us  [inner(): pl.pallas_call(functools.partial(inner_kernel, levels, side), out_shape=j...]
    pallas_call x2, Pallas kernels: 37.6 us -> 28.4 us  [step(): pl.pallas_call(functools.partial(step_kernel, levels, side, last), out_sh...]
    ppermute x3, waiting for transfers between devices: 3.4 us -> 7.63 us  [to_west(): return lax.ppermute(x, 'lon', along('lon', -1, True))]
    unnamed x59 -> x65, local copies, waits for them, and re-layouts: 19.1 us -> 19.8 us
  transfers between devices with their start and end apart: 19 -> 19, of which waited for: 9 -> 9; matrix products, arithmetic and copies ran while one was open for 1% -> 1% of each run, Pallas kernels for 16% -> 26%
where the time goes in v3:
time: 268 us; the launch traced here: 265 us
  Pallas kernels  103 us (38%)
  waiting for transfers between devices  82.4 us (31%)
  starting transfers between devices  56 us (21%)
  local copies, waits for them, and re-layouts  20.3 us (8%)
    pallas_call x2, Pallas kernels, inner(): pl.pallas_call(functools.partial(inner_kernel, levels, side), out_shape=j...  29.8 us
    pallas_call x2, Pallas kernels, step(): pl.pallas_call(functools.partial(step_kernel, levels, side, last), out_sh...  28.4 us
    all_to_all x4, waiting for transfers between devices, across(): return lax.all_to_all(x, 'lon', 0, 0, tiled=True)  26.7 us
    all_to_all x4, starting transfers between devices, across(): return lax.all_to_all(x, 'lon', 0, 0, tiled=True)  24.4 us
    unnamed x65, local copies, waits for them, and re-layouts  19.8 us
    ppermute x1, waiting for transfers between devices, on_device(): from_east = lax.ppermute(westward, 'lon', along('lon', -1, True))  18.2 us
    ppermute x3, waiting for transfers between devices, to_east(): return lax.ppermute(x, 'lon', along('lon', 1, True))  15.3 us
    all_to_all x1, waiting for transfers between devices, on_device(): chl = lax.all_to_all(chl, 'lon', 0, 0, tiled=True)  10.8 us
  transfers between devices with their start and end apart: 19, of which 9 were waited for; matrix products, arithmetic and copies ran while one was open for 1% of the time, Pallas kernels for 26%

profile of v3, /device:TPU:0, one launch (start us, length us, event | category | flops | bytes accessed | tf_op | source)
XLA Modules:
  0.0 265.1 jit_solution(12855556196774922282)
XLA Ops:
  0.6 2.8 %routing.1.table_ref = s32[8,8]{1,0:T(8,128)} custom-call(s32[1,64]{1,0:T(1,128)} %row_ref.1), custom_call_target="tpu_custom_call" | custom-call | tf_op jit(solution)/shard_map/routing/pallas_call | solution.py:131
  4.1 8.5 %first_edges.1 = (f32[8,576,128]{2,1,0:T(8,128)S(1)}, f32[8,144,128]{2,1,0:T(8,128)S(1)}, f32[8,144,128]{2,1,0:T(8,128)S(1)}) custom-call(s32[8,8]{1,0:T(8,128)S(1)} %copy-done.24, f32[8,1152,256]{2,1,0:T(8,128)} %cell_ref.3), custom_call_target="tpu_custom_call" | custom-call | tf_op jit(solution)/shard_map/first_edges/pallas_call | solution.py:210
  15.7 7.4 %all-to-all-start.1 = ((f32[8,576,128]{2,1,0:T(8,128)}), f32[8,576,128]{2,1,0:T(8,128)S(1)}, u32[]{:S(2)}, u32[]{:S(2)}) async-start(f32[8,576,128]{2,1,0:T(8,128)} %copy-done.10), calls=%async_computation.1 | async-start | bytes 4718592 | tf_op jit(solution)/shard_map/all_to_all | solution.py:1143
  25.5 2.1 collective-permute-start.2
  31.1 3.1 %collective-permute-start.3 = (f32[1,128]{1,0:T(1,128)S(1)}, f32[1,128]{1,0:T(1,128)S(1)}, u32[]{:S(2)}, u32[]{:S(2)}) collective-permute-start(f32[1,128]{1,0:T(1,128)S(1)} %pad.22), channel_id=1, source_target_pairs={{0,7},{1,0},{2,1},{3,2},{4,3},{5,4},{6,5},{7,6},{8,15},{9,8},{10,9... | collective-permute-start | bytes 1544 | tf_op jit(solution)/shard_map/ppermute | solution.py:1121
  34.4 10.6 %coarse_rows.1.rows_ref = f32[16,192,128]{2,1,0:T(8,128)S(1)} custom-call(bf16[48,144,384]{2,1,0:T(8,128)(2,1)} %bitcast.13, bf16[16,48,128]{2,1,0:T(8,128)(2,1)S(1)} %bitcast.10, bf16[384,256]{1,0:T(8,128)(2,1)S(1)} %add_convert_fusion.pick_ref), custom_call_target="tpu_custom_call" | custom-call | tf_op jit(solution)/shard_map/coarse_rows/pallas_call | solution.py:653
  44.9 18.2 %collective-permute-done.3.east_ref = f32[1,128]{1,0:T(1,128)S(1)} collective-permute-done((f32[1,128]{1,0:T(1,128)S(1)}, f32[1,128]{1,0:T(1,128)S(1)}, u32[]{:S(2)}, u32[]{:S(2)}) %collective-permute-start.3) | collective-permute-done | bytes 544 | tf_op jit(solution)/shard_map/ppermute | solution.py:1121
  63.2 3.8 %collective-permute-done.2.west_ref = f32[9,128]{1,0:T(8,128)S(1)} collective-permute-done((f32[9,128]{1,0:T(8,128)S(1)}, f32[9,128]{1,0:T(8,128)S(1)}, u32[]{:S(2)}, u32[]{:S(2)}) %collective-permute-start.2) | collective-permute-done | bytes 4640 | tf_op jit(solution)/shard_map/ppermute | solution.py:1120
  67.0 3.6 %coarsen.1 = (f32[8,208,256]{2,1,0:T(8,128)S(1)}, f32[296,256]{1,0:T(8,128)S(1)}) custom-call(s32[8,8]{1,0:T(8,128)S(1)} %copy-done.25, f32[16,192,128]{2,1,0:T(8,128)S(1)} %coarse_rows.1.rows_ref, f32[48,384]{1,0:T(8,128)S(1)} %copy-done.28, s32[16,128]{1,0:T(8,128)S(1)} %copy-done.30, f32[49,384]{1,0:T(8,128)S(1)} %collective-permute-done.south_ref, ...), custom_call_target="tpu_custom_call" | custom-call | tf_op jit(solution)/shard_map/coarsen/pallas_call | solution.py:781
  72.5 5.0 %all-to-all-done.1.quad_ref = f32[8,576,128]{2,1,0:T(8,128)S(1)} async-done(((f32[8,576,128]{2,1,0:T(8,128)}), f32[8,576,128]{2,1,0:T(8,128)S(1)}, u32[]{:S(2)}, u32[]{:S(2)}) %all-to-all-start.1) | async-done | bytes 2359328 | tf_op jit(solution)/shard_map/all_to_all | solution.py:1143
  78.9 8.4 %all-to-all-start = ((f32[8,208,256]{2,1,0:T(8,128)}), f32[8,208,256]{2,1,0:T(8,128)S(1)}, u32[]{:S(2)}, u32[]{:S(2)}) async-start(f32[8,208,256]{2,1,0:T(8,128)} %copy-done.13), calls=%async_computation | async-start | bytes 3407872 | tf_op jit(solution)/shard_map/all_to_all | solution.py:1143
  89.0 6.8 %tile_lines.1 = (f32[1152,128]{1,0:T(8,128)S(1)}, f32[1152,128]{1,0:T(8,128)}, f32[1152,128]{1,0:T(8,128)S(1)}, f32[1152,128]{1,0:T(8,128)S(1)}, f32[48,128]{1,0:T(8,128)}) custom-call(s32[8,8]{1,0:T(8,128)S(1)} %copy-done.25, f32[8,576,128]{2,1,0:T(8,128)S(1)} %copy-done.6), custom_call_target="tpu_custom_call" | custom-call | tf_op jit(solution)/shard_map/tile_lines/pallas_call | solution.py:830
  102.9 2.8 %collective-permute-start.7 = (f32[48,128]{1,0:T(8,128)}, f32[48,128]{1,0:T(8,128)}, u32[]{:S(2)}, u32[]{:S(2)}) collective-permute-start(f32[48,128]{1,0:T(8,128)} %get-tuple-element.25), channel_id=1, source_target_pairs={{0,7},{1,0},{2,1},{3,2},{4,3},{5,4},{6,5},{7,6},{8,15},{9,8},{10,9... | collective-permute-start | bytes 73736 | tf_op jit(solution)/shard_map/ppermute | solution.py:1140
  105.7 21.6 %all-to-all-done.phys_ref.refs_0_.refs_2_ = f32[8,208,256]{2,1,0:T(8,128)S(1)} async-done(((f32[8,208,256]{2,1,0:T(8,128)}), f32[8,208,256]{2,1,0:T(8,128)S(1)}, u32[]{:S(2)}, u32[]{:S(2)}) %all-to-all-start) | async-done | bytes 1703968 | tf_op jit(solution)/shard_map/all_to_all | solution.py:1143
  127.3 2.2 hand_on.2
  130.6 3.6 %all-to-all-start.2 = ((f32[8,288,128]{2,1,0:T(8,128)}), f32[8,288,128]{2,1,0:T(8,128)S(1)}, u32[]{:S(2)}, u32[]{:S(2)}) async-start(f32[8,288,128]{2,1,0:T(8,128)} %copy-done.7), calls=%async_computation.2 | async-start | bytes 2359296 | tf_op jit(solution)/shard_map/all_to_all | solution.py:1143
  139.6 2.5 line_step.1
  146.9 3.0 %collective-permute-start.9 = (f32[8,144,128]{2,1,0:T(8,128)S(1)}, f32[8,144,128]{2,1,0:T(8,128)}, u32[]{:S(2)}, u32[]{:S(2)}) collective-permute-start(f32[8,144,128]{2,1,0:T(8,128)S(1)} %copy-done.15), channel_id=1, source_target_pairs={{0,7},{1,0},{2,1},{3,2},{4,3},{5,4},{6,5},{7,6},{8,15},{9,8},{10,9... | collective-permute-start | bytes 1769480 | tf_op jit(solution)/shard_map/ppermute | solution.py:1140
  149.9 14.9 %inner.2.part_ref.refs_4_ = f32[8,1152,256]{2,1,0:T(8,128)} custom-call(s32[8,8]{1,0:T(8,128)S(1)} %copy-done.25, f32[8,1152,256]{2,1,0:T(8,128)} %cell_ref.3, f32[8,208,256]{2,1,0:T(8,128)S(1)} %copy-done.1), custom_call_target="tpu_custom_call" | custom-call | tf_op jit(solution)/shard_map/inner/pallas_call | solution.py:470
  164.8 2.2 hand_on.3.refs_0_
  168.0 6.3 %collective-permute-done.8.rim_w_ref.refs_2_ = f32[8,144,128]{2,1,0:T(8,128)S(1)} collective-permute-done((f32[8,144,128]{2,1,0:T(8,128)S(1)}, f32[8,144,128]{2,1,0:T(8,128)S(1)}, u32[]{:S(2)}, u32[]{:S(2)}) %collective-permute-start.8) | collective-permute-done | bytes 589856 | tf_op jit(solution)/shard_map/ppermute | solution.py:1137
  174.3 4.0 %collective-permute-done.9.rim_e_ref.refs_3_ = f32[8,144,128]{2,1,0:T(8,128)} collective-permute-done((f32[8,144,128]{2,1,0:T(8,128)S(1)}, f32[8,144,128]{2,1,0:T(8,128)}, u32[]{:S(2)}, u32[]{:S(2)}) %collective-permute-start.9) | collective-permute-done | bytes 589856 | tf_op jit(solution)/shard_map/ppermute | solution.py:1140
  179.4 4.9 %all-to-all-start.3 = ((f32[8,288,128]{2,1,0:T(8,128)}), f32[8,288,128]{2,1,0:T(8,128)}, u32[]{:S(2)}, u32[]{:S(2)}) async-start(f32[8,288,128]{2,1,0:T(8,128)} %gate.3), calls=%async_computation.3 | async-start | bytes 2359296 | tf_op jit(solution)/shard_map/all_to_all | solution.py:1143
  184.3 14.5 %step.2 = (f32[8,1152,256]{2,1,0:T(8,128)}, f32[8,144,128]{2,1,0:T(8,128)S(1)}, f32[8,144,128]{2,1,0:T(8,128)S(1)}) custom-call(s32[8,8]{1,0:T(8,128)S(1)} %copy-done.25, f32[8,1152,256]{2,1,0:T(8,128)} %inner.2.part_ref.refs_4_, f32[8,208,256]{2,1,0:T(8,128)S(1)} %copy-done.1, f32[8,288,128]{2,1,0:T(8,128)S(1)} %copy-done.3, f32[8,144,128]{2,1,0:T(8,128)S(1)} %copy-done.9, ...), custom_call_target="tpu_custom_call" | custom-call | tf_op jit(solution)/shard_map/step/pallas_call | solution.py:607
  200.8 2.7 %collective-permute-start.13 = (f32[8,144,128]{2,1,0:T(8,128)S(1)}, f32[8,144,128]{2,1,0:T(8,128)S(1)}, u32[]{:S(2)}, u32[]{:S(2)}) collective-permute-start(f32[8,144,128]{2,1,0:T(8,128)S(1)} %get-tuple-element.37), channel_id=1, source_target_pairs={{0,7},{1,0},{2,1},{3,2},{4,3},{5,4},{6,5},{7,6},{8,15},{9,8},{10,9... | collective-permute-start | bytes 1769480 | tf_op jit(solution)/shard_map/ppermute | solution.py:1140
  203.5 14.9 %inner.3.part_ref = f32[8,1152,256]{2,1,0:T(8,128)} custom-call(s32[8,8]{1,0:T(8,128)S(1)} %copy-done.25, f32[8,1152,256]{2,1,0:T(8,128)} %get-tuple-element.30.cell_ref, f32[8,208,256]{2,1,0:T(8,128)S(1)} %copy-done.1), custom_call_target="tpu_custom_call" | custom-call | tf_op jit(solution)/shard_map/inner/pallas_call | solution.py:470
  218.4 8.9 %collective-permute-done.12.rim_w_ref = f32[8,144,128]{2,1,0:T(8,128)S(1)} collective-permute-done((f32[8,144,128]{2,1,0:T(8,128)S(1)}, f32[8,144,128]{2,1,0:T(8,128)S(1)}, u32[]{:S(2)}, u32[]{:S(2)}) %collective-permute-start.12) | collective-permute-done | bytes 589856 | tf_op jit(solution)/shard_map/ppermute | solution.py:1137
  227.3 3.6 %collective-permute-done.13.rim_e_ref = f32[8,144,128]{2,1,0:T(8,128)S(1)} collective-permute-done((f32[8,144,128]{2,1,0:T(8,128)S(1)}, f32[8,144,128]{2,1,0:T(8,128)S(1)}, u32[]{:S(2)}, u32[]{:S(2)}) %collective-permute-start.13) | collective-permute-done | bytes 589856 | tf_op jit(solution)/shard_map/ppermute | solution.py:1140
  230.9 14.0 %step.3 = (f32[8,1152,256]{2,1,0:T(8,128)}, f32[8,48,256]{2,1,0:T(8,128)}) custom-call(s32[8,8]{1,0:T(8,128)S(1)} %copy-done.25, f32[8,1152,256]{2,1,0:T(8,128)} %inner.3.part_ref, f32[8,208,256]{2,1,0:T(8,128)S(1)} %copy-done.1, f32[8,288,128]{2,1,0:T(8,128)} %all-to-all-done.3.rim_ref, f32[8,144,128]{2,1,0:T(8,128)S(1)} %collective-permute-done.12.rim_w_ref, ...), custom_call_target="tpu_custom_call" | custom-call | tf_op jit(solution)/shard_map/step/pallas_call | solution.py:607
  244.9 3.9 %all-to-all-start.4 = ((f32[8,48,256]{2,1,0:T(8,128)}), f32[8,48,256]{2,1,0:T(8,128)S(1)}, u32[]{:S(2)}, u32[]{:S(2)}) async-start(f32[8,48,256]{2,1,0:T(8,128)} %get-tuple-element.39), calls=%async_computation.4 | async-start | bytes 786432 | tf_op jit(solution)/shard_map/all_to_all | solution.py:1169
  248.9 10.8 %all-to-all-done.4.chl_ref = f32[8,48,256]{2,1,0:T(8,128)S(1)} async-done(((f32[8,48,256]{2,1,0:T(8,128)}), f32[8,48,256]{2,1,0:T(8,128)S(1)}, u32[]{:S(2)}, u32[]{:S(2)}) %all-to-all-start.4) | async-done | bytes 393248 | tf_op jit(solution)/shard_map/all_to_all | solution.py:1169
  259.6 5.4 %heat.1 = bf16[48,48,384]{2,1,0:T(8,128)(2,1)} custom-call(s32[8,8]{1,0:T(8,128)S(1)} %copy-done.25, f32[8,48,256]{2,1,0:T(8,128)S(1)} %all-to-all-done.4.chl_ref, f32[48,384]{1,0:T(8,128)S(1)} %copy-done.28, s32[16,128]{1,0:T(8,128)S(1)} %copy-done.31, bf16[128,384]{1,0:T(8,128)(2,1)S(1)} %fusion.widen_ref), custom_call_target="tpu_custom_call" | custom-call | tf_op jit(solution)/shard_map/heat/pallas_call | solution.py:1067
  (106 shorter events, 37.1 us)
Async XLA Ops:
  15.7 9.6 %copy-start.30 = (s32[16,128]{1,0:T(8,128)S(1)}, s32[16,128]{1,0:T(8,128)}, u32[]{:S(2)}) copy-start(s32[16,128]{1,0:T(8,128)} %land_ref.3) | copy-start | bytes 24580
  15.7 18.6 %copy-start.29 = (bf16[16,128,48]{1,2,0:T(8,128)(2,1)S(1)}, bf16[16,128,48]{1,2,0:T(8,128)(2,1)}, u32[]{:S(2)}) copy-start(bf16[16,128,48]{1,2,0:T(8,128)(2,1)} %param.8) | copy-start | bytes 589828
  15.7 61.8 %all-to-all-start.1 = ((f32[8,576,128]{2,1,0:T(8,128)}), f32[8,576,128]{2,1,0:T(8,128)S(1)}, u32[]{:S(2)}, u32[]{:S(2)}) async-start(f32[8,576,128]{2,1,0:T(8,128)} %copy-done.10), calls=%async_computation.1 | async-start | bytes 4718592 | tf_op jit(solution)/shard_map/all_to_all | solution.py:1143
  25.5 41.5 %collective-permute-start.2 = (f32[9,128]{1,0:T(8,128)S(1)}, f32[9,128]{1,0:T(8,128)S(1)}, u32[]{:S(2)}, u32[]{:S(2)}) collective-permute-start(f32[9,128]{1,0:T(8,128)S(1)} %select_maximum_fusion.1), channel_id=1, source_target_pairs={{0,1},{1,2},{2,3},{3,4},{4,5},{5,6},{6,7},{7,0},{8,9},{9,10},{10,1... | collective-permute-start | bytes 13832 | tf_op jit(solution)/shard_map/ppermute | solution.py:1120
  28.3 38.7 %collective-permute-start = (f32[49,384]{1,0:T(8,128)S(1)}, f32[49,384]{1,0:T(8,128)S(1)}, u32[]{:S(2)}, u32[]{:S(2)}) collective-permute-start(f32[49,384]{1,0:T(8,128)S(1)} %select_maximum_fusion), channel_id=1, source_target_pairs={{0,8},{8,16},{16,24},{1,9},{9,17},{17,25},{2,10},{10,18},{18,26},{... | collective-permute-start | bytes 225800 | tf_op jit(solution)/shard_map/ppermute | solution.py:1118
  29.8 33.4 %collective-permute-start.1 = (f32[1,384]{1,0:T(1,128)S(1)}, f32[1,384]{1,0:T(1,128)S(1)}, u32[]{:S(2)}, u32[]{:S(2)}) collective-permute-start(f32[1,384]{1,0:T(1,128)S(1)} %pad.19), channel_id=1, source_target_pairs={{8,0},{16,8},{24,16},{9,1},{17,9},{25,17},{10,2},{18,10},{26,18},{... | collective-permute-start | bytes 4616 | tf_op jit(solution)/shard_map/ppermute | solution.py:1119
  31.1 32.1 %collective-permute-start.3 = (f32[1,128]{1,0:T(1,128)S(1)}, f32[1,128]{1,0:T(1,128)S(1)}, u32[]{:S(2)}, u32[]{:S(2)}) collective-permute-start(f32[1,128]{1,0:T(1,128)S(1)} %pad.22), channel_id=1, source_target_pairs={{0,7},{1,0},{2,1},{3,2},{4,3},{5,4},{6,5},{7,6},{8,15},{9,8},{10,9... | collective-permute-start | bytes 1544 | tf_op jit(solution)/shard_map/ppermute | solution.py:1121
  34.4 32.6 %copy-start.25 = (s32[8,8]{1,0:T(8,128)S(1)}, s32[8,8]{1,0:T(8,128)}, u32[]{:S(2)}) copy-start(s32[8,8]{1,0:T(8,128)} %routing.1.table_ref) | copy-start | bytes 772
  34.4 32.6 %copy-start.28 = (f32[48,384]{1,0:T(8,128)S(1)}, f32[48,384]{1,0:T(8,128)}, u32[]{:S(2)}) copy-start(f32[48,384]{1,0:T(8,128)} %light_ref.3) | copy-start | bytes 221188
  78.9 48.4 %all-to-all-start = ((f32[8,208,256]{2,1,0:T(8,128)}), f32[8,208,256]{2,1,0:T(8,128)S(1)}, u32[]{:S(2)}, u32[]{:S(2)}) async-start(f32[8,208,256]{2,1,0:T(8,128)} %copy-done.13), calls=%async_computation | async-start | bytes 3407872 | tf_op jit(solution)/shard_map/all_to_all | solution.py:1143
  97.4 29.9 %collective-permute-start.4 = (f32[1152,128]{1,0:T(8,128)}, f32[1152,128]{1,0:T(8,128)S(1)}, u32[]{:S(2)}, u32[]{:S(2)}) collective-permute-start(f32[1152,128]{1,0:T(8,128)} %get-tuple-element.23.high_ref), channel_id=1, source_target_pairs={{0,8},{8,16},{16,24},{1,9},{9,17},{17,25},{2,10},{10,18},{18,26},{... | collective-permute-start | bytes 1769480 | tf_op jit(solution)/shard_map/ppermute | solution.py:1131
  98.8 28.5 %collective-permute-start.5 = (f32[1152,128]{1,0:T(8,128)S(1)}, f32[1152,128]{1,0:T(8,128)S(1)}, u32[]{:S(2)}, u32[]{:S(2)}) collective-permute-start(f32[1152,128]{1,0:T(8,128)S(1)} %get-tuple-element.24.low_ref), channel_id=1, source_target_pairs={{8,0},{16,8},{24,16},{9,1},{17,9},{25,17},{10,2},{18,10},{26,18},{... | collective-permute-start | bytes 1769480 | tf_op jit(solution)/shard_map/ppermute | solution.py:1134
  100.9 26.4 %collective-permute-start.6 = (f32[48,128]{1,0:T(8,128)}, f32[48,128]{1,0:T(8,128)}, u32[]{:S(2)}, u32[]{:S(2)}) collective-permute-start(f32[48,128]{1,0:T(8,128)} %get-tuple-element.25), channel_id=1, source_target_pairs={{0,1},{1,2},{2,3},{3,4},{4,5},{5,6},{6,7},{7,0},{8,9},{9,10},{10,1... | collective-permute-start | bytes 73736 | tf_op jit(solution)/shard_map/ppermute | solution.py:1137
  102.9 24.4 %collective-permute-start.7 = (f32[48,128]{1,0:T(8,128)}, f32[48,128]{1,0:T(8,128)}, u32[]{:S(2)}, u32[]{:S(2)}) collective-permute-start(f32[48,128]{1,0:T(8,128)} %get-tuple-element.25), channel_id=1, source_target_pairs={{0,7},{1,0},{2,1},{3,2},{4,3},{5,4},{6,5},{7,6},{8,15},{9,8},{10,9... | collective-permute-start | bytes 73736 | tf_op jit(solution)/shard_map/ppermute | solution.py:1140
  127.3 3.3 %copy-start = (f32[8,208,256]{2,1,0:T(8,128)}, f32[8,208,256]{2,1,0:T(8,128)S(1)}, u32[]{:S(2)}) copy-start(f32[8,208,256]{2,1,0:T(8,128)S(1)} %all-to-all-done.phys_ref.refs_0_.refs_2_) | copy-start | bytes 5111812
  127.3 3.3 %copy-start.11 = (f32[1152,128]{1,0:T(8,128)}, f32[1152,128]{1,0:T(8,128)S(1)}, u32[]{:S(2)}) copy-start(f32[1152,128]{1,0:T(8,128)S(1)} %collective-permute-done.5.above_ref) | copy-start | bytes 1769476
  130.6 47.7 %all-to-all-start.2 = ((f32[8,288,128]{2,1,0:T(8,128)}), f32[8,288,128]{2,1,0:T(8,128)S(1)}, u32[]{:S(2)}, u32[]{:S(2)}) async-start(f32[8,288,128]{2,1,0:T(8,128)} %copy-done.7), calls=%async_computation.2 | async-start | bytes 2359296 | tf_op jit(solution)/shard_map/all_to_all | solution.py:1143
  134.2 15.7 %copy-start.1 = (f32[8,208,256]{2,1,0:T(8,128)S(1)}, f32[8,208,256]{2,1,0:T(8,128)}, u32[]{:S(2)}) copy-start(f32[8,208,256]{2,1,0:T(8,128)} %copy-done) | copy-start | bytes 5111812
  139.6 5.5 %copy-start.17 = (f32[8,144,128]{2,1,0:T(8,128)S(1)}, f32[8,144,128]{2,1,0:T(8,128)}, u32[]{:S(2)}) copy-start(f32[8,144,128]{2,1,0:T(8,128)} %get-tuple-element.28) | copy-start | bytes 1769476
  139.6 7.3 %copy-start.15 = (f32[8,144,128]{2,1,0:T(8,128)S(1)}, f32[8,144,128]{2,1,0:T(8,128)}, u32[]{:S(2)}) copy-start(f32[8,144,128]{2,1,0:T(8,128)} %get-tuple-element.29) | copy-start | bytes 1769476
  142.1 22.7 %collective-permute-start.10 = (f32[1152,128]{1,0:T(8,128)S(1)}, f32[1152,128]{1,0:T(8,128)S(1)}, u32[]{:S(2)}, u32[]{:S(2)}) collective-permute-start(f32[1152,128]{1,0:T(8,128)S(1)} %get-tuple-element.34), channel_id=1, source_target_pairs={{0,8},{8,16},{16,24},{1,9},{9,17},{17,25},{2,10},{10,18},{18,26},{... | collective-permute-start | bytes 1769480 | tf_op jit(solution)/shard_map/ppermute | solution.py:1131
  143.8 21.0 %collective-permute-start.11 = (f32[1152,128]{1,0:T(8,128)S(1)}, f32[1152,128]{1,0:T(8,128)S(1)}, u32[]{:S(2)}, u32[]{:S(2)}) collective-permute-start(f32[1152,128]{1,0:T(8,128)S(1)} %get-tuple-element.35), channel_id=1, source_target_pairs={{8,0},{16,8},{24,16},{9,1},{17,9},{25,17},{10,2},{18,10},{26,18},{... | collective-permute-start | bytes 1769480 | tf_op jit(solution)/shard_map/ppermute | solution.py:1134
  145.1 29.2 %collective-permute-start.8 = (f32[8,144,128]{2,1,0:T(8,128)S(1)}, f32[8,144,128]{2,1,0:T(8,128)S(1)}, u32[]{:S(2)}, u32[]{:S(2)}) collective-permute-start(f32[8,144,128]{2,1,0:T(8,128)S(1)} %copy-done.17), channel_id=1, source_target_pairs={{0,1},{1,2},{2,3},{3,4},{4,5},{5,6},{6,7},{7,0},{8,9},{9,10},{10,1... | collective-permute-start | bytes 1769480 | tf_op jit(solution)/shard_map/ppermute | solution.py:1137
  146.9 31.4 %collective-permute-start.9 = (f32[8,144,128]{2,1,0:T(8,128)S(1)}, f32[8,144,128]{2,1,0:T(8,128)}, u32[]{:S(2)}, u32[]{:S(2)}) collective-permute-start(f32[8,144,128]{2,1,0:T(8,128)S(1)} %copy-done.15), channel_id=1, source_target_pairs={{0,7},{1,0},{2,1},{3,2},{4,3},{5,4},{6,5},{7,6},{8,15},{9,8},{10,9... | collective-permute-start | bytes 1769480 | tf_op jit(solution)/shard_map/ppermute | solution.py:1140
  174.3 4.0 %copy-start.8 = (f32[8,144,128]{2,1,0:T(8,128)}, f32[8,144,128]{2,1,0:T(8,128)S(1)}, u32[]{:S(2)}) copy-start(f32[8,144,128]{2,1,0:T(8,128)S(1)} %collective-permute-done.8.rim_w_ref.refs_2_) | copy-start | bytes 1769476
  179.4 4.9 %copy-start.3 = (f32[8,288,128]{2,1,0:T(8,128)S(1)}, f32[8,288,128]{2,1,0:T(8,128)}, u32[]{:S(2)}) copy-start(f32[8,288,128]{2,1,0:T(8,128)} %copy-done.2) | copy-start | bytes 3538948
  179.4 5.0 %copy-start.9 = (f32[8,144,128]{2,1,0:T(8,128)S(1)}, f32[8,144,128]{2,1,0:T(8,128)}, u32[]{:S(2)}) copy-start(f32[8,144,128]{2,1,0:T(8,128)} %copy-done.8) | copy-start | bytes 1769476
  179.4 51.5 %all-to-all-start.3 = ((f32[8,288,128]{2,1,0:T(8,128)}), f32[8,288,128]{2,1,0:T(8,128)}, u32[]{:S(2)}, u32[]{:S(2)}) async-start(f32[8,288,128]{2,1,0:T(8,128)} %gate.3), calls=%async_computation.3 | async-start | bytes 2359296 | tf_op jit(solution)/shard_map/all_to_all | solution.py:1143
  198.8 28.5 %collective-permute-start.12 = (f32[8,144,128]{2,1,0:T(8,128)S(1)}, f32[8,144,128]{2,1,0:T(8,128)S(1)}, u32[]{:S(2)}, u32[]{:S(2)}) collective-permute-start(f32[8,144,128]{2,1,0:T(8,128)S(1)} %get-tuple-element.36), channel_id=1, source_target_pairs={{0,1},{1,2},{2,3},{3,4},{4,5},{5,6},{6,7},{7,0},{8,9},{9,10},{10,1... | collective-permute-start | bytes 1769480 | tf_op jit(solution)/shard_map/ppermute | solution.py:1137
  200.8 30.1 %collective-permute-start.13 = (f32[8,144,128]{2,1,0:T(8,128)S(1)}, f32[8,144,128]{2,1,0:T(8,128)S(1)}, u32[]{:S(2)}, u32[]{:S(2)}) collective-permute-start(f32[8,144,128]{2,1,0:T(8,128)S(1)} %get-tuple-element.37), channel_id=1, source_target_pairs={{0,7},{1,0},{2,1},{3,2},{4,3},{5,4},{6,5},{7,6},{8,15},{9,8},{10,9... | collective-permute-start | bytes 1769480 | tf_op jit(solution)/shard_map/ppermute | solution.py:1140
  218.4 41.2 %copy-start.31 = (s32[16,128]{1,0:T(8,128)S(1)}, s32[16,128]{1,0:T(8,128)}, u32[]{:S(2)}) copy-start(s32[16,128]{1,0:T(8,128)} %land_ref.3) | copy-start | bytes 24580
  244.9 14.7 %all-to-all-start.4 = ((f32[8,48,256]{2,1,0:T(8,128)}), f32[8,48,256]{2,1,0:T(8,128)S(1)}, u32[]{:S(2)}, u32[]{:S(2)}) async-start(f32[8,48,256]{2,1,0:T(8,128)} %get-tuple-element.39), calls=%async_computation.4 | async-start | bytes 786432 | tf_op jit(solution)/shard_map/all_to_all | solution.py:1169
  (19 other events, 19.6 us)

commit v4 on v3

--- a/solution.py
+++ b/solution.py
@@ -227,6 +227,68 @@
         compiler_params=pltpu.CompilerParams(vmem_limit_bytes=VMEM_LIMIT),
         name="first_edges",
     )(table, tracers)
+
+
+def growth(
+    nitrogen,
+    phosphate,
+    silicate,
+    iron_free,
+    nano_carbon,
+    diat_carbon,
+    micro_zoo,
+    meso_zoo,
+    par_light,
+    warm_factor,
+):
+    limit_nitro = nitrogen / (0.5 + nitrogen)
+    limit_phos = positive(phosphate) / (0.3 + positive(phosphate))
+    limit_iron = positive(iron_free) / (0.2 + positive(iron_free))
+    limit_sil = positive(silicate) / (1.0 + positive(silicate))
+    nutr_nano = jnp.minimum(jnp.minimum(limit_nitro, limit_phos), limit_iron)
+    nutr_diat = jnp.minimum(nutr_nano, limit_sil)
+    lit = warm_factor * par_light
+    prod_nano = 0.1 * lit / (par_light + 0.5) * nutr_nano * nano_carbon
+    prod_diat = 0.12 * lit / (par_light + 1.0) * nutr_diat * diat_carbon
+    graze_nano = 0.08 * warm_factor * micro_zoo / (1.0 + positive(nano_carbon))
+    graze_diat = 0.06 * warm_factor * meso_zoo / (1.0 + positive(diat_carbon))
+    return prod_nano, prod_diat, graze_nano, graze_diat
+
+
+CHL_TRACERS = (3, 4, 5, 6, 7, 8, 9, 10, 11, 15, 16)
+CHL_RUN = 3
+CHL_BLOCKS = sorted({tracer // CHL_RUN for tracer in CHL_TRACERS})
+
+
+def chl_after(mixed, par_light, warm_factor):
+    (
+        nitrate,
+        ammonium,
+        phosphate,
+        silicate,
+        iron_free,
+        nano_carbon,
+        diat_carbon,
+        nano_chl,
+        diat_chl,
+        micro_zoo,
+        meso_zoo,
+    ) = mixed
+    prod_nano, prod_diat, graze_nano, graze_diat = growth(
+        positive(nitrate) + positive(ammonium),
+        phosphate,
+        silicate,
+        iron_free,
+        nano_carbon,
+        diat_carbon,
+        micro_zoo,
+        meso_zoo,
+        par_light,
+        warm_factor,
+    )
+    nano_chl = nano_chl + 0.03 * prod_nano - (graze_nano + 0.02) * nano_chl
+    diat_chl = diat_chl + 0.03 * prod_diat - (graze_diat + 0.02) * diat_chl
+    return nano_chl, diat_chl
 
 
 def react(mixed, par_light, warm_factor):
@@ -257,18 +319,19 @@
         calcite,
     ) = mixed
     nitrogen = positive(nitrate) + positive(ammonium)
-    limit_nitro = nitrogen / (0.5 + nitrogen)
-    limit_phos = positive(phosphate) / (0.3 + positive(phosphate))
-    limit_iron = positive(iron_free) / (0.2 + positive(iron_free))
-    limit_sil = positive(silicate) / (1.0 + positive(silicate))
-    nutr_nano = jnp.minimum(jnp.minimum(limit_nitro, limit_phos), limit_iron)
-    nutr_diat = jnp.minimum(nutr_nano, limit_sil)
-    lit = warm_factor * par_light
-    prod_nano = 0.1 * lit / (par_light + 0.5) * nutr_nano * nano_carbon
-    prod_diat = 0.12 * lit / (par_light + 1.0) * nutr_diat * diat_carbon
     ammon_share = (positive(ammonium) + 0.01) / (nitrogen + 0.02)
-    graze_nano = 0.08 * warm_factor * micro_zoo / (1.0 + positive(nano_carbon))
-    graze_diat = 0.06 * warm_factor * meso_zoo / (1.0 + positive(diat_carbon))
+    prod_nano, prod_diat, graze_nano, graze_diat = growth(
+        nitrogen,
+        phosphate,
+        silicate,
+        iron_free,
+        nano_carbon,
+        diat_carbon,
+        micro_zoo,
+        meso_zoo,
+        par_light,
+        warm_factor,
+    )
     loss_nano = graze_nano + 0.02
     loss_diat = graze_diat + 0.02
     eaten_nano = graze_nano * nano_carbon
@@ -351,31 +414,40 @@
     moved_ref[SUB + channels : 2 * SUB + channels, :] = blank
 
 
+def mixed_at(levels, count, span, moved_ref, coef_ref, lt):
+    sub = lax.broadcasted_iota(jnp.int32, (SUB, LANES), 0)
+    at = pl.multiple_of(lt * SUB, SUB)
+    mix_c, mix_d, mix_u = (coef_ref[n, pl.ds(at, SUB), span] for n in (5, 6, 7))
+    mixed = []
+    for t in range(count):
+        base = t * levels + lt * SUB
+        before = moved_ref[pl.ds(pl.multiple_of(base, SUB), SUB), span]
+        now = moved_ref[pl.ds(pl.multiple_of(base + SUB, SUB), SUB), span]
+        after = moved_ref[pl.ds(pl.multiple_of(base + 2 * SUB, SUB), SUB), span]
+        up = pltpu.roll(jnp.where(sub == SUB - 1, before, now), 1, 0)
+        down = pltpu.roll(jnp.where(sub == 0, after, now), SUB - 1, 0)
+        mixed.append(mix_c * now + mix_d * down + mix_u * up)
+    return mixed
+
+
+def lit_at(nano_chl, diat_chl, light, depth):
+    sub = lax.broadcasted_iota(jnp.int32, (SUB, LANES), 0)
+    absorb = 0.04 + 0.02 * (positive(nano_chl) + positive(diat_chl))
+    total = absorb
+    for by in (1, 2, 4):
+        total = total + jnp.where(sub >= by, pltpu.roll(total, by, 0), 0.0)
+    above = depth + (total - absorb)
+    return light * jnp.exp(-(above + 0.5 * absorb)), depth + total[SUB - 1 : SUB, :]
+
+
 def mix_and_react(levels, tracer_count, spans, moved_ref, coef_ref, light, wet, warm_at, store):
-    sub = lax.broadcasted_iota(jnp.int32, (SUB, LANES), 0)
-
     def reacting(lt, carry):
-        at = pl.multiple_of(lt * SUB, SUB)
         depths = []
         halves_new = []
         for h, span in enumerate(spans):
-            mix_c, mix_d, mix_u = (coef_ref[n, pl.ds(at, SUB), span] for n in (5, 6, 7))
-            mixed = []
-            for t in range(tracer_count):
-                base = t * levels + lt * SUB
-                before = moved_ref[pl.ds(pl.multiple_of(base, SUB), SUB), span]
-                now = moved_ref[pl.ds(pl.multiple_of(base + SUB, SUB), SUB), span]
-                after = moved_ref[pl.ds(pl.multiple_of(base + 2 * SUB, SUB), SUB), span]
-                up = pltpu.roll(jnp.where(sub == SUB - 1, before, now), 1, 0)
-                down = pltpu.roll(jnp.where(sub == 0, after, now), SUB - 1, 0)
-                mixed.append(mix_c * now + mix_d * down + mix_u * up)
-            absorb = 0.04 + 0.02 * (positive(mixed[nano_chl_index]) + positive(mixed[diat_chl_index]))
-            total = absorb
-            for by in (1, 2, 4):
-                total = total + jnp.where(sub >= by, pltpu.roll(total, by, 0), 0.0)
-            above = carry[h] + (total - absorb)
-            depths.append(carry[h] + total[SUB - 1 : SUB, :])
-            par_light = light[h] * jnp.exp(-(above + 0.5 * absorb))
+            mixed = mixed_at(levels, tracer_count, span, moved_ref, coef_ref, lt)
+            par_light, depth = lit_at(mixed[nano_chl_index], mixed[diat_chl_index], light[h], carry[h])
+            depths.append(depth)
             halves_new.append([value * wet[h] for value in react(mixed, par_light, warm_at(lt, h))])
             for t in range(tracer_count):
                 store(t, pl.multiple_of(t * levels + lt * SUB, SUB), h, halves_new[h][t])
@@ -485,10 +557,75 @@
     )(table, cells, phys)
 
 
+def add_rims(
+    levels, side, spans, tracers, part_at, phys_ref, rim_ref, rim_w_ref, rim_e_ref, coef_ref, moved_ref, ends_ref
+):
+    group = LANES // side
+    halves = len(spans)
+    rows = rim_w_ref.shape[1]
+    rounds = rows // levels
+    level_tiles = levels // SUB
+    lane = lane_ids()
+    col = lane & (side - 1)
+    first_row = lane < side
+    last_row = lane >= LANES - side
+    odd = (lane & 1) == 1
+    flag_row = 4 * levels
+
+    def flag(f, h):
+        return phys_ref[0, flag_row + f : flag_row + f + 1, spans[h]]
+
+    above_mix = [jnp.zeros((SUB, LANES), jnp.float32)] * halves
+    for lt in range(level_tiles):
+        at = slice(lt * SUB, (lt + 1) * SUB)
+        for h, faces in enumerate(block_faces(phys_ref, spans, levels, side, lt)):
+            _, e, w, n, s = transport(faces, [flag(f, h) for f in range(4)])
+            coef_ref[0, at, spans[h]] = jnp.where(col == 0, w, jnp.where(col == side - 1, e, 0.0))
+            if h == 0:
+                coef_ref[1, at, spans[h]] = jnp.where(first_row, s, 0.0)
+            if h == halves - 1:
+                coef_ref[1, at, spans[h]] = jnp.where(last_row, n, 0.0)
+            mix = phys_ref[0, 3 * levels + lt * SUB : 3 * levels + (lt + 1) * SUB, spans[h]]
+            set_mixing(coef_ref, at, spans[h], mix, above_mix[h], lt == level_tiles - 1)
+            above_mix[h] = mix
+
+    for at in range(0, rows, SUB):
+        ends_ref[at : at + SUB, :] = turned(rim_w_ref[0, at : at + SUB, :], 2 - 2 * side)
+    set_blank(moved_ref, len(tracers) * levels)
+
+    def gather(lt, carry):
+        at = pl.multiple_of(lt * SUB, SUB)
+        for i in range(rounds):
+            row = pl.multiple_of(i * levels + lt * SUB, SUB)
+            rims = [
+                rim_ref[0, pl.ds(row, SUB), :],
+                rim_ref[0, pl.ds(pl.multiple_of(rows + row, SUB), SUB), :],
+            ]
+            ends_w = ends_ref[pl.ds(row, SUB), :]
+            ends_e = rim_e_ref[0, pl.ds(row, SUB), :]
+            sides = [jnp.where(odd, ends_e, ends_w), jnp.where(odd, ends_w, ends_e)]
+            for g in range(group):
+                if i * group + g not in tracers:
+                    continue
+                place = tracers.index(i * group + g)
+                chan = pl.multiple_of(place * levels + lt * SUB, SUB)
+                rim = turned(rims[2 * g // group], -side - 2 * side * (g % (group // 2)))
+                for h in range(halves):
+                    ends = turned(sides[h], side - 2 + h - 2 * g)
+                    moved = part_at(place, lt, spans[h])
+                    moved = moved + coef_ref[0, pl.ds(at, SUB), spans[h]] * ends
+                    if h in (0, halves - 1):
+                        moved = moved + coef_ref[1, pl.ds(at, SUB), spans[h]] * rim
+                    moved_ref[pl.ds(pl.multiple_of(SUB + chan, SUB), SUB), spans[h]] = moved
+        return carry
+
+    lax.fori_loop(0, level_tiles, gather, 0, unroll=True)
+
+
 def step_kernel(levels, side, last, table_ref, part_ref, phys_ref, rim_ref, rim_w_ref, rim_e_ref, *refs):
     if last:
-        out_ref, chl_ref, coef_ref, moved_ref, ends_ref = refs
-        edge_refs = (chl_ref,)
+        out_ref, coef_ref, moved_ref, ends_ref = refs
+        edge_refs = ()
     else:
         out_ref, west_ref, east_ref, coef_ref, moved_ref, ends_ref = refs
         edge_refs = (west_ref, east_ref)
@@ -497,8 +634,6 @@
     group = LANES // side
     halves = cell_count // LANES
     rounds = tracer_count // group
-    level_tiles = levels // SUB
-    rows = rounds * levels
     slot = pl.program_id(0)
     full = table_ref[SLOT_FULL, slot] == 1
     spans = [slice(h * LANES, (h + 1) * LANES) for h in range(halves)]
@@ -511,68 +646,33 @@
 
     @pl.when(full)
     def _():
-        lane = lane_ids()
-        col = lane & (side - 1)
-        first_row = lane < side
-        last_row = lane >= LANES - side
-        odd = (lane & 1) == 1
         flag_row = 4 * levels
 
         def flag(f, h):
             return phys_ref[0, flag_row + f : flag_row + f + 1, spans[h]]
 
-        above_mix = [jnp.zeros((SUB, LANES), jnp.float32)] * halves
-        for lt in range(level_tiles):
-            at = slice(lt * SUB, (lt + 1) * SUB)
-            for h, faces in enumerate(block_faces(phys_ref, spans, levels, side, lt)):
-                _, e, w, n, s = transport(faces, [flag(f, h) for f in range(4)])
-                coef_ref[0, at, spans[h]] = jnp.where(col == 0, w, jnp.where(col == side - 1, e, 0.0))
-                if h == 0:
-                    coef_ref[1, at, spans[h]] = jnp.where(first_row, s, 0.0)
-                if h == halves - 1:
-                    coef_ref[1, at, spans[h]] = jnp.where(last_row, n, 0.0)
-                mix = phys_ref[0, 3 * levels + lt * SUB : 3 * levels + (lt + 1) * SUB, spans[h]]
-                set_mixing(coef_ref, at, spans[h], mix, above_mix[h], lt == level_tiles - 1)
-                above_mix[h] = mix
-
-        for at in range(0, rows, SUB):
-            ends_ref[at : at + SUB, :] = turned(rim_w_ref[0, at : at + SUB, :], 2 - 2 * side)
-        set_blank(moved_ref, channels)
-
-        def gather(lt, carry):
-            at = pl.multiple_of(lt * SUB, SUB)
-            for i in range(rounds):
-                row = pl.multiple_of(i * levels + lt * SUB, SUB)
-                rims = [
-                    rim_ref[0, pl.ds(row, SUB), :],
-                    rim_ref[0, pl.ds(pl.multiple_of(rows + row, SUB), SUB), :],
-                ]
-                ends_w = ends_ref[pl.ds(row, SUB), :]
-                ends_e = rim_e_ref[0, pl.ds(row, SUB), :]
-                sides = [jnp.where(odd, ends_e, ends_w), jnp.where(odd, ends_w, ends_e)]
-                for g in range(group):
-                    chan = pl.multiple_of((i * group + g) * levels + lt * SUB, SUB)
-                    rim = turned(rims[2 * g // group], -side - 2 * side * (g % (group // 2)))
-                    for h in range(halves):
-                        ends = turned(sides[h], side - 2 + h - 2 * g)
-                        moved = part_ref[0, pl.ds(chan, SUB), spans[h]]
-                        moved = moved + coef_ref[0, pl.ds(at, SUB), spans[h]] * ends
-                        if h in (0, halves - 1):
-                            moved = moved + coef_ref[1, pl.ds(at, SUB), spans[h]] * rim
-                        moved_ref[pl.ds(pl.multiple_of(SUB + chan, SUB), SUB), spans[h]] = moved
-            return carry
-
-        lax.fori_loop(0, level_tiles, gather, 0, unroll=True)
+        def part_at(t, lt, span):
+            return part_ref[0, pl.ds(pl.multiple_of(t * levels + lt * SUB, SUB), SUB), span]
+
+        add_rims(
+            levels,
+            side,
+            spans,
+            list(range(tracer_count)),
+            part_at,
+            phys_ref,
+            rim_ref,
+            rim_w_ref,
+            rim_e_ref,
+            coef_ref,
+            moved_ref,
+            ends_ref,
+        )
 
         def store(t, at, h, value):
             if t is not None:
                 out_ref[0, pl.ds(at, SUB), spans[h]] = value
-            elif last:
-                for k, new in enumerate(value):
-                    chl_ref[0, pl.ds(pl.multiple_of(at * SUB, SUB), SUB), spans[k]] = positive(
-                        new[nano_chl_index]
-                    ) + positive(new[diat_chl_index])
-            else:
+            elif not last:
                 for i in range(rounds):
                     row = pl.multiple_of(i * levels + at * SUB, SUB)
                     first, second = (new[i * group : (i + 1) * group] for new in value)
@@ -597,10 +697,7 @@
     by_slot = pl.BlockSpec((1, channels, cell_count), lambda s, t: (s, 0, 0))
     shapes = [jax.ShapeDtypeStruct(cells.shape, f32)]
     specs = [by_slot]
-    if last:
-        shapes.append(jax.ShapeDtypeStruct((lon_count, levels, cell_count), f32))
-        specs.append(pl.BlockSpec((1, levels, cell_count), lambda s, t: (t[SLOT_TILE, s], 0, 0)))
-    else:
+    if not last:
         beside = jax.ShapeDtypeStruct((slot_count, rows, LANES), f32)
         shapes += [beside, beside]
         specs += [pl.BlockSpec((1, rows, LANES), lambda s, t: (s, 0, 0))] * 2
@@ -627,6 +724,96 @@
         compiler_params=pltpu.CompilerParams(vmem_limit_bytes=VMEM_LIMIT),
         name="step",
     )(table, cells, phys, rims, rim_w, rim_e)
+
+
+def chl_kernel(levels, side, table_ref, *refs):
+    count = len(CHL_TRACERS)
+    part_refs = refs[: len(CHL_BLOCKS)]
+    phys_ref, rim_ref, rim_w_ref, rim_e_ref, chl_ref, coef_ref, moved_ref, ends_ref = refs[len(CHL_BLOCKS) :]
+    halves = chl_ref.shape[2] // LANES
+    spans = [slice(h * LANES, (h + 1) * LANES) for h in range(halves)]
+    full = table_ref[SLOT_FULL, pl.program_id(0)] == 1
+    flag_row = 4 * levels
+
+    @pl.when(jnp.logical_not(full))
+    def _():
+        chl_ref[...] = jnp.zeros_like(chl_ref)
+
+    @pl.when(full)
+    def _():
+        def part_at(place, lt, span):
+            tracer = CHL_TRACERS[place]
+            at = (tracer % CHL_RUN) * levels + lt * SUB
+            return part_refs[CHL_BLOCKS.index(tracer // CHL_RUN)][0, pl.ds(pl.multiple_of(at, SUB), SUB), span]
+
+        add_rims(
+            levels,
+            side,
+            spans,
+            list(CHL_TRACERS),
+            part_at,
+            phys_ref,
+            rim_ref,
+            rim_w_ref,
+            rim_e_ref,
+            coef_ref,
+            moved_ref,
+            ends_ref,
+        )
+        nano = CHL_TRACERS.index(nano_chl_index)
+        diat = CHL_TRACERS.index(diat_chl_index)
+
+        def greening(lt, carry):
+            at = pl.multiple_of(lt * SUB, SUB)
+            depths = []
+            for h, span in enumerate(spans):
+                mixed = mixed_at(levels, count, span, moved_ref, coef_ref, lt)
+                light = phys_ref[0, flag_row + LIGHT : flag_row + LIGHT + 1, span]
+                wet = phys_ref[0, flag_row + WET : flag_row + WET + 1, span]
+                warm = phys_ref[0, pl.ds(pl.multiple_of(2 * levels + lt * SUB, SUB), SUB), span]
+                par_light, depth = lit_at(mixed[nano], mixed[diat], light, carry[h])
+                depths.append(depth)
+                nano_chl, diat_chl = chl_after(mixed, par_light, warm)
+                chl_ref[0, pl.ds(at, SUB), span] = positive(nano_chl * wet) + positive(diat_chl * wet)
+            return tuple(depths)
+
+        start = tuple(jnp.zeros((1, LANES), jnp.float32) for _ in spans)
+        lax.fori_loop(0, levels // SUB, greening, start, unroll=True)
+
+
+def last_chl(table, cells, phys, rims, rim_w, rim_e, levels, side):
+    slot_count, channels, cell_count = cells.shape
+    lon_count = lax.axis_size("lon")
+    rows = channels * side // LANES
+    count = len(CHL_TRACERS)
+    f32 = jnp.float32
+
+    def level_block(number):
+        return pl.BlockSpec((1, CHL_RUN * levels, cell_count), lambda s, t: (s, number, 0))
+
+    return pl.pallas_call(
+        functools.partial(chl_kernel, levels, side),
+        out_shape=jax.ShapeDtypeStruct((lon_count, levels, cell_count), f32),
+        grid_spec=pltpu.PrefetchScalarGridSpec(
+            num_scalar_prefetch=1,
+            grid=(slot_count,),
+            in_specs=[level_block(n) for n in CHL_BLOCKS]
+            + [
+                pl.BlockSpec((1, phys.shape[1], cell_count), lambda s, t: (t[SLOT_TILE, s], 0, 0)),
+                pl.BlockSpec((1, 2 * rows, LANES), lambda s, t: (t[SLOT_TILE, s], 0, 0)),
+                pl.BlockSpec((1, rows, LANES), lambda s, t: (t[SLOT_WEST, s], 0, 0)),
+                pl.BlockSpec((1, rows, LANES), lambda s, t: (t[SLOT_EAST, s], 0, 0)),
+            ],
+            out_specs=pl.BlockSpec((1, levels, cell_count), lambda s, t: (t[SLOT_TILE, s], 0, 0)),
+            scratch_shapes=[
+                pltpu.VMEM((8, levels, cell_count), f32),
+                pltpu.VMEM((count * levels + 2 * SUB, cell_count), f32),
+                pltpu.VMEM((rows, LANES), f32),
+            ],
+        ),
+        compiler_params=pltpu.CompilerParams(vmem_limit_bytes=VMEM_LIMIT),
+        name="last_chl",
+    )(table, *([cells] * len(CHL_BLOCKS)), phys, rims, rim_w, rim_e)
 
 
 def rows_kernel(levels, factor, fine_ref, mix_ref, pick_ref, rows_ref):
@@ -993,7 +1180,20 @@
     )(*values, *others)
 
 
-def heat_kernel(levels, side, factor, table_ref, chl_ref, light_ref, land_ref, widen_ref, out_ref, rows_ref, wide_ref):
+def heat_kernel(
+    levels,
+    side,
+    factor,
+    table_ref,
+    chl_ref,
+    light_ref,
+    land_ref,
+    widen_ref,
+    after_ref,
+    out_ref,
+    rows_ref,
+    wide_ref,
+):
     tile_blocks = land_ref.shape[1] // side
     halves = side * side // LANES
     group = LANES // side
@@ -1018,7 +1218,7 @@
                 rows_ref[pl.ds(pl.multiple_of((h * group + r) * levels + lt * SUB, SUB), SUB), :] = line
         return carry
 
-    lax.fori_loop(0, levels // SUB, place, 0)
+    lax.fori_loop(0, levels // SUB, place, 0, unroll=True)
     wet = land_ref[...].astype(f32)
     widen = widen_ref[...]
     above = jnp.zeros_like(wet)
@@ -1057,17 +1257,18 @@
                 out_ref[l, m * SUB : (m + 2) * SUB, span] = jnp.concatenate(both, axis=0).astype(jnp.bfloat16)
         return carry
 
-    lax.fori_loop(0, levels, spread, 0)
-
-
-def heat(table, chl, light, land, levels, widen):
+    lax.fori_loop(0, levels, spread, 0, unroll=4)
+
+
+def heat(table, chl, light, land, levels, widen, after):
     side = land.shape[0]
     factor = light.shape[0] // side
     vmem = pl.BlockSpec(memory_space=pltpu.VMEM)
     return pl.pallas_call(
         functools.partial(heat_kernel, levels, side, factor),
         out_shape=jax.ShapeDtypeStruct((levels,) + light.shape, jnp.bfloat16),
-        in_specs=[pl.BlockSpec(memory_space=pltpu.SMEM), vmem, vmem, vmem, vmem],
+        in_specs=[pl.BlockSpec(memory_space=pltpu.SMEM), vmem, vmem, vmem, vmem]
+        + [pl.BlockSpec(memory_space=pl.ANY)],
         out_specs=vmem,
         scratch_shapes=[
             pltpu.VMEM((side * levels, LANES), jnp.float32),
@@ -1075,7 +1276,7 @@
         ],
         compiler_params=pltpu.CompilerParams(vmem_limit_bytes=VMEM_LIMIT),
         name="heat",
-    )(table, chl, light, land, widen)
+    )(table, chl, light, land, widen, after)
 
 
 def widened(x, rows, width):
@@ -1165,9 +1366,9 @@
     current, west, east = step(table, partial, phys, rims, rim_w, rim_e, levels, side, False)
     rim_w, rim_e = to_east(east), to_west(west)
     partial = inner(table, current, phys, levels, side)
-    current, chl = step(table, partial, phys, new_rims, rim_w, rim_e, levels, side, True)
-    chl = lax.all_to_all(chl, "lon", 0, 0, tiled=True)
-    heating = heat(table, chl, surf_light, land_mask, levels, jnp.transpose(member))
+    chl = across(last_chl(table, partial, phys, new_rims, rim_w, rim_e, levels, side))
+    (current,) = step(table, partial, phys, new_rims, rim_w, rim_e, levels, side, True)
+    heating = heat(table, chl, surf_light, land_mask, levels, jnp.transpose(member), current)
     return current, heating
 
 

time: 268 us -> 264 us (0.985)
  waiting for transfers between devices: 82.4 us -> 73.9 us
  Pallas kernels: 103 us -> 106 us
    all_to_all x1 -> x0, waiting for transfers between devices: 10.8 us -> none  [on_device(): chl = lax.all_to_all(chl, 'lon', 0, 0, tiled=True)]
    pallas_call x0 -> x1, Pallas kernels: none -> 8.46 us  [last_chl(): pl.pallas_call(functools.partial(chl_kernel, levels, side), out_shape=jax...]
    all_to_all x4 -> x5, starting transfers between devices: 24.4 us -> 29.1 us  [across(): return lax.all_to_all(x, 'lon', 0, 0, tiled=True)]
    all_to_all x1 -> x0, starting transfers between devices: 3.94 us -> none  [on_device(): chl = lax.all_to_all(chl, 'lon', 0, 0, tiled=True)]
    all_to_all x4 -> x5, waiting for transfers between devices: 26.7 us -> 26.7 us  [across(): return lax.all_to_all(x, 'lon', 0, 0, tiled=True)]
  transfers between devices with their start and end apart: 19 -> 19, of which waited for: 9 -> 8; matrix products, arithmetic and copies ran while one was open for 1% -> 1% of each run, Pallas kernels for 26% -> 31%
where the time goes in v4:
time: 264 us; the launch traced here: 260 us
  Pallas kernels  106 us (40%)
  waiting for transfers between devices  73.9 us (28%)
  starting transfers between devices  56.3 us (21%)
  local copies, waits for them, and re-layouts  20.2 us (8%)
  other arithmetic  2.66 us (1%)
    all_to_all x5, starting transfers between devices, across(): return lax.all_to_all(x, 'lon', 0, 0, tiled=True)  29.1 us
    pallas_call x2, Pallas kernels, inner(): pl.pallas_call(functools.partial(inner_kernel, levels, side), out_shape=j...  27.6 us
    all_to_all x5, waiting for transfers between devices, across(): return lax.all_to_all(x, 'lon', 0, 0, tiled=True)  26.7 us
    pallas_call x2, Pallas kernels, step(): pl.pallas_call(functools.partial(step_kernel, levels, side, last), out_sh...  26.3 us
    unnamed x65, local copies, waits for them, and re-layouts  19.8 us
    ppermute x1, waiting for transfers between devices, on_device(): from_east = lax.ppermute(westward, 'lon', along('lon', -1, True))  17.5 us
    ppermute x3, waiting for transfers between devices, to_east(): return lax.ppermute(x, 'lon', along('lon', 1, True))  17.4 us
    pallas_call x1, Pallas kernels, coarse_rows(): pl.pallas_call(functools.partial(rows_kernel, levels, factor), out_shape=...  10.6 us
  transfers between devices with their start and end apart: 19, of which 8 were waited for; matrix products, arithmetic and copies ran while one was open for 1% of the time, Pallas kernels for 31%

profile of v4, /device:TPU:0, one launch (start us, length us, event | category | flops | bytes accessed | tf_op | source)
XLA Modules:
  0.0 259.9 jit_solution(1428291210286674454)
XLA Ops:
  0.6 2.9 %routing.1.table_ref = s32[8,8]{1,0:T(8,128)} custom-call(s32[1,64]{1,0:T(1,128)} %row_ref.1), custom_call_target="tpu_custom_call" | custom-call | tf_op jit(solution)/shard_map/routing/pallas_call | solution.py:131
  4.2 8.5 %first_edges.1 = (f32[8,576,128]{2,1,0:T(8,128)S(1)}, f32[8,144,128]{2,1,0:T(8,128)S(1)}, f32[8,144,128]{2,1,0:T(8,128)S(1)}) custom-call(s32[8,8]{1,0:T(8,128)S(1)} %copy-done.24, f32[8,1152,256]{2,1,0:T(8,128)} %cell_ref.3), custom_call_target="tpu_custom_call" | custom-call | tf_op jit(solution)/shard_map/first_edges/pallas_call | solution.py:210
  15.8 7.8 %all-to-all-start.1 = ((f32[8,576,128]{2,1,0:T(8,128)}), f32[8,576,128]{2,1,0:T(8,128)S(1)}, u32[]{:S(2)}, u32[]{:S(2)}) async-start(f32[8,576,128]{2,1,0:T(8,128)} %copy-done.10), calls=%async_computation.1 | async-start | bytes 4718592 | tf_op jit(solution)/shard_map/all_to_all | solution.py:1344
  25.9 2.1 collective-permute-start.2
  31.4 2.8 %collective-permute-start.3 = (f32[1,128]{1,0:T(1,128)S(1)}, f32[1,128]{1,0:T(1,128)S(1)}, u32[]{:S(2)}, u32[]{:S(2)}) collective-permute-start(f32[1,128]{1,0:T(1,128)S(1)} %pad.22), channel_id=1, source_target_pairs={{0,7},{1,0},{2,1},{3,2},{4,3},{5,4},{6,5},{7,6},{8,15},{9,8},{10,9... | collective-permute-start | bytes 1544 | tf_op jit(solution)/shard_map/ppermute | solution.py:1322
  34.4 10.6 %coarse_rows.1.rows_ref = f32[16,192,128]{2,1,0:T(8,128)S(1)} custom-call(bf16[48,144,384]{2,1,0:T(8,128)(2,1)} %bitcast.13, bf16[16,48,128]{2,1,0:T(8,128)(2,1)S(1)} %bitcast.10, bf16[384,256]{1,0:T(8,128)(2,1)S(1)} %add_convert_fusion.pick_ref), custom_call_target="tpu_custom_call" | custom-call | tf_op jit(solution)/shard_map/coarse_rows/pallas_call | solution.py:840
  45.0 17.5 %collective-permute-done.3.east_ref = f32[1,128]{1,0:T(1,128)S(1)} collective-permute-done((f32[1,128]{1,0:T(1,128)S(1)}, f32[1,128]{1,0:T(1,128)S(1)}, u32[]{:S(2)}, u32[]{:S(2)}) %collective-permute-start.3) | collective-permute-done | bytes 544 | tf_op jit(solution)/shard_map/ppermute | solution.py:1322
  62.4 4.2 %collective-permute-done.2.west_ref = f32[9,128]{1,0:T(8,128)S(1)} collective-permute-done((f32[9,128]{1,0:T(8,128)S(1)}, f32[9,128]{1,0:T(8,128)S(1)}, u32[]{:S(2)}, u32[]{:S(2)}) %collective-permute-start.2) | collective-permute-done | bytes 4640 | tf_op jit(solution)/shard_map/ppermute | solution.py:1321
  66.6 3.6 %coarsen.1 = (f32[8,208,256]{2,1,0:T(8,128)S(1)}, f32[296,256]{1,0:T(8,128)S(1)}) custom-call(s32[8,8]{1,0:T(8,128)S(1)} %copy-done.25, f32[16,192,128]{2,1,0:T(8,128)S(1)} %coarse_rows.1.rows_ref, f32[48,384]{1,0:T(8,128)S(1)} %copy-done.28, s32[16,128]{1,0:T(8,128)S(1)} %copy-done.30, f32[49,384]{1,0:T(8,128)S(1)} %collective-permute-done.south_ref, ...), custom_call_target="tpu_custom_call" | custom-call | tf_op jit(solution)/shard_map/coarsen/pallas_call | solution.py:968
  72.1 5.0 %all-to-all-done.1.quad_ref = f32[8,576,128]{2,1,0:T(8,128)S(1)} async-done(((f32[8,576,128]{2,1,0:T(8,128)}), f32[8,576,128]{2,1,0:T(8,128)S(1)}, u32[]{:S(2)}, u32[]{:S(2)}) %all-to-all-start.1) | async-done | bytes 2359328 | tf_op jit(solution)/shard_map/all_to_all | solution.py:1344
  78.6 8.4 %all-to-all-start = ((f32[8,208,256]{2,1,0:T(8,128)}), f32[8,208,256]{2,1,0:T(8,128)S(1)}, u32[]{:S(2)}, u32[]{:S(2)}) async-start(f32[8,208,256]{2,1,0:T(8,128)} %copy-done.13), calls=%async_computation | async-start | bytes 3407872 | tf_op jit(solution)/shard_map/all_to_all | solution.py:1344
  88.6 6.8 %tile_lines.1 = (f32[1152,128]{1,0:T(8,128)S(1)}, f32[1152,128]{1,0:T(8,128)}, f32[1152,128]{1,0:T(8,128)S(1)}, f32[1152,128]{1,0:T(8,128)S(1)}, f32[48,128]{1,0:T(8,128)}) custom-call(s32[8,8]{1,0:T(8,128)S(1)} %copy-done.25, f32[8,576,128]{2,1,0:T(8,128)S(1)} %copy-done.6), custom_call_target="tpu_custom_call" | custom-call | tf_op jit(solution)/shard_map/tile_lines/pallas_call | solution.py:1017
  102.5 2.8 %collective-permute-start.7 = (f32[48,128]{1,0:T(8,128)}, f32[48,128]{1,0:T(8,128)}, u32[]{:S(2)}, u32[]{:S(2)}) collective-permute-start(f32[48,128]{1,0:T(8,128)} %get-tuple-element.23), channel_id=1, source_target_pairs={{0,7},{1,0},{2,1},{3,2},{4,3},{5,4},{6,5},{7,6},{8,15},{9,8},{10,9... | collective-permute-start | bytes 73736 | tf_op jit(solution)/shard_map/ppermute | solution.py:1341
  105.3 21.7 %all-to-all-done.phys_ref.refs_0_.refs_2_.refs_4_ = f32[8,208,256]{2,1,0:T(8,128)S(1)} async-done(((f32[8,208,256]{2,1,0:T(8,128)}), f32[8,208,256]{2,1,0:T(8,128)S(1)}, u32[]{:S(2)}, u32[]{:S(2)}) %all-to-all-start) | async-done | bytes 1703968 | tf_op jit(solution)/shard_map/all_to_all | solution.py:1344
  127.0 2.2 hand_on.2
  130.2 3.6 %all-to-all-start.2 = ((f32[8,288,128]{2,1,0:T(8,128)}), f32[8,288,128]{2,1,0:T(8,128)S(1)}, u32[]{:S(2)}, u32[]{:S(2)}) async-start(f32[8,288,128]{2,1,0:T(8,128)} %copy-done.7), calls=%async_computation.2 | async-start | bytes 2359296 | tf_op jit(solution)/shard_map/all_to_all | solution.py:1344
  139.2 2.5 line_step.1
  146.5 3.0 %collective-permute-start.9 = (f32[8,144,128]{2,1,0:T(8,128)S(1)}, f32[8,144,128]{2,1,0:T(8,128)}, u32[]{:S(2)}, u32[]{:S(2)}) collective-permute-start(f32[8,144,128]{2,1,0:T(8,128)S(1)} %copy-done.15), channel_id=1, source_target_pairs={{0,7},{1,0},{2,1},{3,2},{4,3},{5,4},{6,5},{7,6},{8,15},{9,8},{10,9... | collective-permute-start | bytes 1769480 | tf_op jit(solution)/shard_map/ppermute | solution.py:1341
  149.5 13.8 %inner.2.part_ref.refs_4_ = f32[8,1152,256]{2,1,0:T(8,128)} custom-call(s32[8,8]{1,0:T(8,128)S(1)} %copy-done.25, f32[8,1152,256]{2,1,0:T(8,128)} %cell_ref.3, f32[8,208,256]{2,1,0:T(8,128)S(1)} %copy-done.1), custom_call_target="tpu_custom_call" | custom-call | tf_op jit(solution)/shard_map/inner/pallas_call | solution.py:542
  163.3 2.2 hand_on.3.refs_0_
  166.4 6.8 %collective-permute-done.8.rim_w_ref.refs_2_ = f32[8,144,128]{2,1,0:T(8,128)S(1)} collective-permute-done((f32[8,144,128]{2,1,0:T(8,128)S(1)}, f32[8,144,128]{2,1,0:T(8,128)S(1)}, u32[]{:S(2)}, u32[]{:S(2)}) %collective-permute-start.8) | collective-permute-done | bytes 589856 | tf_op jit(solution)/shard_map/ppermute | solution.py:1338
  173.2 4.3 %collective-permute-done.9.rim_e_ref.refs_3_ = f32[8,144,128]{2,1,0:T(8,128)} collective-permute-done((f32[8,144,128]{2,1,0:T(8,128)S(1)}, f32[8,144,128]{2,1,0:T(8,128)}, u32[]{:S(2)}, u32[]{:S(2)}) %collective-permute-start.9) | collective-permute-done | bytes 589856 | tf_op jit(solution)/shard_map/ppermute | solution.py:1341
  178.6 5.3 %all-to-all-start.3 = ((f32[8,288,128]{2,1,0:T(8,128)}), f32[8,288,128]{2,1,0:T(8,128)}, u32[]{:S(2)}, u32[]{:S(2)}) async-start(f32[8,288,128]{2,1,0:T(8,128)} %gate.3), calls=%async_computation.3 | async-start | bytes 2359296 | tf_op jit(solution)/shard_map/all_to_all | solution.py:1344
  183.9 13.4 %step.2 = (f32[8,1152,256]{2,1,0:T(8,128)}, f32[8,144,128]{2,1,0:T(8,128)S(1)}, f32[8,144,128]{2,1,0:T(8,128)S(1)}) custom-call(s32[8,8]{1,0:T(8,128)S(1)} %copy-done.25, f32[8,1152,256]{2,1,0:T(8,128)} %inner.2.part_ref.refs_4_, f32[8,208,256]{2,1,0:T(8,128)S(1)} %copy-done.1, f32[8,288,128]{2,1,0:T(8,128)S(1)} %copy-done.3, f32[8,144,128]{2,1,0:T(8,128)S(1)} %copy-done.9, ...), custom_call_target="tpu_custom_call" | custom-call | tf_op jit(solution)/shard_map/step/pallas_call | solution.py:704
  199.3 2.7 %collective-permute-start.13 = (f32[8,144,128]{2,1,0:T(8,128)S(1)}, f32[8,144,128]{2,1,0:T(8,128)S(1)}, u32[]{:S(2)}, u32[]{:S(2)}) collective-permute-start(f32[8,144,128]{2,1,0:T(8,128)S(1)} %get-tuple-element.35), channel_id=1, source_target_pairs={{0,7},{1,0},{2,1},{3,2},{4,3},{5,4},{6,5},{7,6},{8,15},{9,8},{10,9... | collective-permute-start | bytes 1769480 | tf_op jit(solution)/shard_map/ppermute | solution.py:1341
  202.0 13.8 %inner.3.part_ref.refs_0_.refs_1_.refs_2_.refs_3_ = f32[8,1152,256]{2,1,0:T(8,128)} custom-call(s32[8,8]{1,0:T(8,128)S(1)} %copy-done.25, f32[8,1152,256]{2,1,0:T(8,128)} %get-tuple-element.28.cell_ref, f32[8,208,256]{2,1,0:T(8,128)S(1)} %copy-done.1), custom_call_target="tpu_custom_call" | custom-call | tf_op jit(solution)/shard_map/inner/pallas_call | solution.py:542
  215.9 10.7 %collective-permute-done.12.rim_w_ref.refs_6_ = f32[8,144,128]{2,1,0:T(8,128)S(1)} collective-permute-done((f32[8,144,128]{2,1,0:T(8,128)S(1)}, f32[8,144,128]{2,1,0:T(8,128)S(1)}, u32[]{:S(2)}, u32[]{:S(2)}) %collective-permute-start.12) | collective-permute-done | bytes 589856 | tf_op jit(solution)/shard_map/ppermute | solution.py:1338
  226.5 3.8 %collective-permute-done.13.rim_e_ref.refs_7_ = f32[8,144,128]{2,1,0:T(8,128)S(1)} collective-permute-done((f32[8,144,128]{2,1,0:T(8,128)S(1)}, f32[8,144,128]{2,1,0:T(8,128)S(1)}, u32[]{:S(2)}, u32[]{:S(2)}) %collective-permute-start.13) | collective-permute-done | bytes 589856 | tf_op jit(solution)/shard_map/ppermute | solution.py:1341
  230.3 8.5 %last_chl.1 = f32[8,48,256]{2,1,0:T(8,128)} custom-call(s32[8,8]{1,0:T(8,128)S(1)} %copy-done.25, f32[8,1152,256]{2,1,0:T(8,128)} %inner.3.part_ref.refs_0_.refs_1_.refs_2_.refs_3_, f32[8,1152,256]{2,1,0:T(8,128)} %inner.3.part_ref.refs_0_.refs_1_.refs_2_.refs_3_, f32[8,1152,256]{2,1,0:T(8,128)} %inner.3.part_ref.refs_0_.refs_1_.refs_2_.refs_3_, ...), custom_call_target="tpu_custom_call" | custom-call | tf_op jit(solution)/shard_map/last_chl/pallas_call | solution.py:794
  238.8 3.9 %all-to-all-start.4 = ((f32[8,48,256]{2,1,0:T(8,128)}), f32[8,48,256]{2,1,0:T(8,128)S(1)}, u32[]{:S(2)}, u32[]{:S(2)}) async-start(f32[8,48,256]{2,1,0:T(8,128)} %last_chl.1), calls=%async_computation.4 | async-start | bytes 786432 | tf_op jit(solution)/shard_map/all_to_all | solution.py:1344
  242.8 12.9 %step.3.after_ref = f32[8,1152,256]{2,1,0:T(8,128)} custom-call(s32[8,8]{1,0:T(8,128)S(1)} %copy-done.25, f32[8,1152,256]{2,1,0:T(8,128)} %inner.3.part_ref.refs_0_.refs_1_.refs_2_.refs_3_, f32[8,208,256]{2,1,0:T(8,128)S(1)} %copy-done.1, f32[8,288,128]{2,1,0:T(8,128)} %all-to-all-done.3.rim_ref.refs_5_, ...), custom_call_target="tpu_custom_call" | custom-call | tf_op jit(solution)/shard_map/step/pallas_call | solution.py:704
  255.7 4.3 %heat.1 = bf16[48,48,384]{2,1,0:T(8,128)(2,1)} custom-call(s32[8,8]{1,0:T(8,128)S(1)} %copy-done.25, f32[8,48,256]{2,1,0:T(8,128)S(1)} %all-to-all-done.4.chl_ref, f32[48,384]{1,0:T(8,128)S(1)} %copy-done.28, s32[16,128]{1,0:T(8,128)S(1)} %copy-done.31, bf16[128,384]{1,0:T(8,128)(2,1)S(1)} %fusion.widen_ref, f32[8,1152,256]{2,1,0:T(8,128)} %step.3.after_ref), custom_call_target="tpu_custom_call" | custom-call | tf_op jit(solution)/shard_map/heat/pallas_call | solution.py:1267
  (107 shorter events, 36.9 us)
Async XLA Ops:
  15.8 9.9 %copy-start.30 = (s32[16,128]{1,0:T(8,128)S(1)}, s32[16,128]{1,0:T(8,128)}, u32[]{:S(2)}) copy-start(s32[16,128]{1,0:T(8,128)} %land_ref.3) | copy-start | bytes 24580
  15.8 18.6 %copy-start.29 = (bf16[16,128,48]{1,2,0:T(8,128)(2,1)S(1)}, bf16[16,128,48]{1,2,0:T(8,128)(2,1)}, u32[]{:S(2)}) copy-start(bf16[16,128,48]{1,2,0:T(8,128)(2,1)} %param.8) | copy-start | bytes 589828
  15.8 61.4 %all-to-all-start.1 = ((f32[8,576,128]{2,1,0:T(8,128)}), f32[8,576,128]{2,1,0:T(8,128)S(1)}, u32[]{:S(2)}, u32[]{:S(2)}) async-start(f32[8,576,128]{2,1,0:T(8,128)} %copy-done.10), calls=%async_computation.1 | async-start | bytes 4718592 | tf_op jit(solution)/shard_map/all_to_all | solution.py:1344
  25.9 40.7 %collective-permute-start.2 = (f32[9,128]{1,0:T(8,128)S(1)}, f32[9,128]{1,0:T(8,128)S(1)}, u32[]{:S(2)}, u32[]{:S(2)}) collective-permute-start(f32[9,128]{1,0:T(8,128)S(1)} %select_maximum_fusion.1), channel_id=1, source_target_pairs={{0,1},{1,2},{2,3},{3,4},{4,5},{5,6},{6,7},{7,0},{8,9},{9,10},{10,1... | collective-permute-start | bytes 13832 | tf_op jit(solution)/shard_map/ppermute | solution.py:1321
  28.8 37.8 %collective-permute-start = (f32[49,384]{1,0:T(8,128)S(1)}, f32[49,384]{1,0:T(8,128)S(1)}, u32[]{:S(2)}, u32[]{:S(2)}) collective-permute-start(f32[49,384]{1,0:T(8,128)S(1)} %select_maximum_fusion), channel_id=1, source_target_pairs={{0,8},{8,16},{16,24},{1,9},{9,17},{17,25},{2,10},{10,18},{18,26},{... | collective-permute-start | bytes 225800 | tf_op jit(solution)/shard_map/ppermute | solution.py:1319
  30.1 32.3 %collective-permute-start.1 = (f32[1,384]{1,0:T(1,128)S(1)}, f32[1,384]{1,0:T(1,128)S(1)}, u32[]{:S(2)}, u32[]{:S(2)}) collective-permute-start(f32[1,384]{1,0:T(1,128)S(1)} %pad.19), channel_id=1, source_target_pairs={{8,0},{16,8},{24,16},{9,1},{17,9},{25,17},{10,2},{18,10},{26,18},{... | collective-permute-start | bytes 4616 | tf_op jit(solution)/shard_map/ppermute | solution.py:1320
  31.4 31.0 %collective-permute-start.3 = (f32[1,128]{1,0:T(1,128)S(1)}, f32[1,128]{1,0:T(1,128)S(1)}, u32[]{:S(2)}, u32[]{:S(2)}) collective-permute-start(f32[1,128]{1,0:T(1,128)S(1)} %pad.22), channel_id=1, source_target_pairs={{0,7},{1,0},{2,1},{3,2},{4,3},{5,4},{6,5},{7,6},{8,15},{9,8},{10,9... | collective-permute-start | bytes 1544 | tf_op jit(solution)/shard_map/ppermute | solution.py:1322
  34.4 32.2 %copy-start.25 = (s32[8,8]{1,0:T(8,128)S(1)}, s32[8,8]{1,0:T(8,128)}, u32[]{:S(2)}) copy-start(s32[8,8]{1,0:T(8,128)} %routing.1.table_ref) | copy-start | bytes 772
  34.4 32.2 %copy-start.28 = (f32[48,384]{1,0:T(8,128)S(1)}, f32[48,384]{1,0:T(8,128)}, u32[]{:S(2)}) copy-start(f32[48,384]{1,0:T(8,128)} %light_ref.3) | copy-start | bytes 221188
  78.6 48.4 %all-to-all-start = ((f32[8,208,256]{2,1,0:T(8,128)}), f32[8,208,256]{2,1,0:T(8,128)S(1)}, u32[]{:S(2)}, u32[]{:S(2)}) async-start(f32[8,208,256]{2,1,0:T(8,128)} %copy-done.13), calls=%async_computation | async-start | bytes 3407872 | tf_op jit(solution)/shard_map/all_to_all | solution.py:1344
  97.0 29.9 %collective-permute-start.4 = (f32[1152,128]{1,0:T(8,128)}, f32[1152,128]{1,0:T(8,128)S(1)}, u32[]{:S(2)}, u32[]{:S(2)}) collective-permute-start(f32[1152,128]{1,0:T(8,128)} %get-tuple-element.21.high_ref), channel_id=1, source_target_pairs={{0,8},{8,16},{16,24},{1,9},{9,17},{17,25},{2,10},{10,18},{18,26},{... | collective-permute-start | bytes 1769480 | tf_op jit(solution)/shard_map/ppermute | solution.py:1332
  98.4 28.5 %collective-permute-start.5 = (f32[1152,128]{1,0:T(8,128)S(1)}, f32[1152,128]{1,0:T(8,128)S(1)}, u32[]{:S(2)}, u32[]{:S(2)}) collective-permute-start(f32[1152,128]{1,0:T(8,128)S(1)} %get-tuple-element.22.low_ref), channel_id=1, source_target_pairs={{8,0},{16,8},{24,16},{9,1},{17,9},{25,17},{10,2},{18,10},{26,18},{... | collective-permute-start | bytes 1769480 | tf_op jit(solution)/shard_map/ppermute | solution.py:1335
  100.5 26.4 %collective-permute-start.6 = (f32[48,128]{1,0:T(8,128)}, f32[48,128]{1,0:T(8,128)}, u32[]{:S(2)}, u32[]{:S(2)}) collective-permute-start(f32[48,128]{1,0:T(8,128)} %get-tuple-element.23), channel_id=1, source_target_pairs={{0,1},{1,2},{2,3},{3,4},{4,5},{5,6},{6,7},{7,0},{8,9},{9,10},{10,1... | collective-permute-start | bytes 73736 | tf_op jit(solution)/shard_map/ppermute | solution.py:1338
  102.5 24.4 %collective-permute-start.7 = (f32[48,128]{1,0:T(8,128)}, f32[48,128]{1,0:T(8,128)}, u32[]{:S(2)}, u32[]{:S(2)}) collective-permute-start(f32[48,128]{1,0:T(8,128)} %get-tuple-element.23), channel_id=1, source_target_pairs={{0,7},{1,0},{2,1},{3,2},{4,3},{5,4},{6,5},{7,6},{8,15},{9,8},{10,9... | collective-permute-start | bytes 73736 | tf_op jit(solution)/shard_map/ppermute | solution.py:1341
  126.9 3.3 %copy-start = (f32[8,208,256]{2,1,0:T(8,128)}, f32[8,208,256]{2,1,0:T(8,128)S(1)}, u32[]{:S(2)}) copy-start(f32[8,208,256]{2,1,0:T(8,128)S(1)} %all-to-all-done.phys_ref.refs_0_.refs_2_.refs_4_) | copy-start | bytes 5111812
  127.0 3.3 %copy-start.11 = (f32[1152,128]{1,0:T(8,128)}, f32[1152,128]{1,0:T(8,128)S(1)}, u32[]{:S(2)}) copy-start(f32[1152,128]{1,0:T(8,128)S(1)} %collective-permute-done.5.above_ref) | copy-start | bytes 1769476
  130.2 47.3 %all-to-all-start.2 = ((f32[8,288,128]{2,1,0:T(8,128)}), f32[8,288,128]{2,1,0:T(8,128)S(1)}, u32[]{:S(2)}, u32[]{:S(2)}) async-start(f32[8,288,128]{2,1,0:T(8,128)} %copy-done.7), calls=%async_computation.2 | async-start | bytes 2359296 | tf_op jit(solution)/shard_map/all_to_all | solution.py:1344
  133.8 15.7 %copy-start.1 = (f32[8,208,256]{2,1,0:T(8,128)S(1)}, f32[8,208,256]{2,1,0:T(8,128)}, u32[]{:S(2)}) copy-start(f32[8,208,256]{2,1,0:T(8,128)} %copy-done) | copy-start | bytes 5111812
  139.2 5.5 %copy-start.17 = (f32[8,144,128]{2,1,0:T(8,128)S(1)}, f32[8,144,128]{2,1,0:T(8,128)}, u32[]{:S(2)}) copy-start(f32[8,144,128]{2,1,0:T(8,128)} %get-tuple-element.26) | copy-start | bytes 1769476
  139.2 7.3 %copy-start.15 = (f32[8,144,128]{2,1,0:T(8,128)S(1)}, f32[8,144,128]{2,1,0:T(8,128)}, u32[]{:S(2)}) copy-start(f32[8,144,128]{2,1,0:T(8,128)} %get-tuple-element.27) | copy-start | bytes 1769476
  141.7 21.5 %collective-permute-start.10 = (f32[1152,128]{1,0:T(8,128)S(1)}, f32[1152,128]{1,0:T(8,128)S(1)}, u32[]{:S(2)}, u32[]{:S(2)}) collective-permute-start(f32[1152,128]{1,0:T(8,128)S(1)} %get-tuple-element.32), channel_id=1, source_target_pairs={{0,8},{8,16},{16,24},{1,9},{9,17},{17,25},{2,10},{10,18},{18,26},{... | collective-permute-start | bytes 1769480 | tf_op jit(solution)/shard_map/ppermute | solution.py:1332
  143.4 19.9 %collective-permute-start.11 = (f32[1152,128]{1,0:T(8,128)S(1)}, f32[1152,128]{1,0:T(8,128)S(1)}, u32[]{:S(2)}, u32[]{:S(2)}) collective-permute-start(f32[1152,128]{1,0:T(8,128)S(1)} %get-tuple-element.33), channel_id=1, source_target_pairs={{8,0},{16,8},{24,16},{9,1},{17,9},{25,17},{10,2},{18,10},{26,18},{... | collective-permute-start | bytes 1769480 | tf_op jit(solution)/shard_map/ppermute | solution.py:1335
  144.7 28.5 %collective-permute-start.8 = (f32[8,144,128]{2,1,0:T(8,128)S(1)}, f32[8,144,128]{2,1,0:T(8,128)S(1)}, u32[]{:S(2)}, u32[]{:S(2)}) collective-permute-start(f32[8,144,128]{2,1,0:T(8,128)S(1)} %copy-done.17), channel_id=1, source_target_pairs={{0,1},{1,2},{2,3},{3,4},{4,5},{5,6},{6,7},{7,0},{8,9},{9,10},{10,1... | collective-permute-start | bytes 1769480 | tf_op jit(solution)/shard_map/ppermute | solution.py:1338
  146.5 31.0 %collective-permute-start.9 = (f32[8,144,128]{2,1,0:T(8,128)S(1)}, f32[8,144,128]{2,1,0:T(8,128)}, u32[]{:S(2)}, u32[]{:S(2)}) collective-permute-start(f32[8,144,128]{2,1,0:T(8,128)S(1)} %copy-done.15), channel_id=1, source_target_pairs={{0,7},{1,0},{2,1},{3,2},{4,3},{5,4},{6,5},{7,6},{8,15},{9,8},{10,9... | collective-permute-start | bytes 1769480 | tf_op jit(solution)/shard_map/ppermute | solution.py:1341
  173.2 4.3 %copy-start.8 = (f32[8,144,128]{2,1,0:T(8,128)}, f32[8,144,128]{2,1,0:T(8,128)S(1)}, u32[]{:S(2)}) copy-start(f32[8,144,128]{2,1,0:T(8,128)S(1)} %collective-permute-done.8.rim_w_ref.refs_2_) | copy-start | bytes 1769476
  178.6 5.3 %copy-start.3 = (f32[8,288,128]{2,1,0:T(8,128)S(1)}, f32[8,288,128]{2,1,0:T(8,128)}, u32[]{:S(2)}) copy-start(f32[8,288,128]{2,1,0:T(8,128)} %copy-done.2) | copy-start | bytes 3538948
  178.6 5.4 %copy-start.9 = (f32[8,144,128]{2,1,0:T(8,128)S(1)}, f32[8,144,128]{2,1,0:T(8,128)}, u32[]{:S(2)}) copy-start(f32[8,144,128]{2,1,0:T(8,128)} %copy-done.8) | copy-start | bytes 1769476
  178.6 51.7 %all-to-all-start.3 = ((f32[8,288,128]{2,1,0:T(8,128)}), f32[8,288,128]{2,1,0:T(8,128)}, u32[]{:S(2)}, u32[]{:S(2)}) async-start(f32[8,288,128]{2,1,0:T(8,128)} %gate.3), calls=%async_computation.3 | async-start | bytes 2359296 | tf_op jit(solution)/shard_map/all_to_all | solution.py:1344
  197.3 29.2 %collective-permute-start.12 = (f32[8,144,128]{2,1,0:T(8,128)S(1)}, f32[8,144,128]{2,1,0:T(8,128)S(1)}, u32[]{:S(2)}, u32[]{:S(2)}) collective-permute-start(f32[8,144,128]{2,1,0:T(8,128)S(1)} %get-tuple-element.34), channel_id=1, source_target_pairs={{0,1},{1,2},{2,3},{3,4},{4,5},{5,6},{6,7},{7,0},{8,9},{9,10},{10,1... | collective-permute-start | bytes 1769480 | tf_op jit(solution)/shard_map/ppermute | solution.py:1338
  199.3 31.0 %collective-permute-start.13 = (f32[8,144,128]{2,1,0:T(8,128)S(1)}, f32[8,144,128]{2,1,0:T(8,128)S(1)}, u32[]{:S(2)}, u32[]{:S(2)}) collective-permute-start(f32[8,144,128]{2,1,0:T(8,128)S(1)} %get-tuple-element.35), channel_id=1, source_target_pairs={{0,7},{1,0},{2,1},{3,2},{4,3},{5,4},{6,5},{7,6},{8,15},{9,8},{10,9... | collective-permute-start | bytes 1769480 | tf_op jit(solution)/shard_map/ppermute | solution.py:1341
  238.8 16.9 %all-to-all-start.4 = ((f32[8,48,256]{2,1,0:T(8,128)}), f32[8,48,256]{2,1,0:T(8,128)S(1)}, u32[]{:S(2)}, u32[]{:S(2)}) async-start(f32[8,48,256]{2,1,0:T(8,128)} %last_chl.1), calls=%async_computation.4 | async-start | bytes 786432 | tf_op jit(solution)/shard_map/all_to_all | solution.py:1344
  242.7 12.9 %copy-start.31 = (s32[16,128]{1,0:T(8,128)S(1)}, s32[16,128]{1,0:T(8,128)}, u32[]{:S(2)}) copy-start(s32[16,128]{1,0:T(8,128)} %land_ref.3) | copy-start | bytes 24580
  (19 other events, 19.6 us)

commit v5 on v4

--- a/solution.py
+++ b/solution.py
@@ -99,7 +99,7 @@
 
         return carry
 
-    lax.fori_loop(0, block_count, visit, 0, unroll=4)
+    lax.fori_loop(0, block_count, visit, 0, unroll=8)
 
     def give(target, filled, line, count):
         def one(i, carry):
@@ -1271,7 +1271,7 @@
         + [pl.BlockSpec(memory_space=pl.ANY)],
         out_specs=vmem,
         scratch_shapes=[
-            pltpu.VMEM((side * levels, LANES), jnp.float32),
+            pltpu.VMEM(((side + 1) * levels, LANES), jnp.float32),
             pltpu.VMEM((side * levels, light.shape[1]), jnp.float32),
         ],
         compiler_params=pltpu.CompilerParams(vmem_limit_bytes=VMEM_LIMIT),

time: 264 us -> 264 us (level)
  no operation moved by 1% of the time
where the time goes in v5:
time: 264 us; the launch traced here: 261 us
  Pallas kernels  107 us (41%)
  waiting for transfers between devices  73.5 us (28%)
  starting transfers between devices  56.4 us (21%)
  local copies, waits for them, and re-layouts  20.2 us (8%)
  other arithmetic  2.66 us (1%)
    all_to_all x5, starting transfers between devices, across(): return lax.all_to_all(x, 'lon', 0, 0, tiled=True)  29.1 us
    pallas_call x2, Pallas kernels, inner(): pl.pallas_call(functools.partial(inner_kernel, levels, side), out_shape=j...  28.1 us
    pallas_call x2, Pallas kernels, step(): pl.pallas_call(functools.partial(step_kernel, levels, side, last), out_sh...  27 us
    all_to_all x5, waiting for transfers between devices, across(): return lax.all_to_all(x, 'lon', 0, 0, tiled=True)  26.7 us
    unnamed x65, local copies, waits for them, and re-layouts  19.8 us
    ppermute x3, waiting for transfers between devices, to_east(): return lax.ppermute(x, 'lon', along('lon', 1, True))  17.5 us
    ppermute x1, waiting for transfers between devices, on_device(): from_east = lax.ppermute(westward, 'lon', along('lon', -1, True))  17.5 us
    pallas_call x1, Pallas kernels, coarse_rows(): pl.pallas_call(functools.partial(rows_kernel, levels, factor), out_shape=...  10.6 us
  transfers between devices with their start and end apart: 19, of which 8 were waited for; matrix products, arithmetic and copies ran while one was open for 1% of the time, Pallas kernels for 31%

profile of v5, /device:TPU:0, one launch (start us, length us, event | category | flops | bytes accessed | tf_op | source)
XLA Modules:
  0.0 261.0 jit_solution(14192512913321780102)
XLA Ops:
  0.6 3.0 %routing.1.table_ref = s32[8,8]{1,0:T(8,128)} custom-call(s32[1,64]{1,0:T(1,128)} %row_ref.1), custom_call_target="tpu_custom_call" | custom-call | tf_op jit(solution)/shard_map/routing/pallas_call | solution.py:131
  4.3 8.5 %first_edges.1 = (f32[8,576,128]{2,1,0:T(8,128)S(1)}, f32[8,144,128]{2,1,0:T(8,128)S(1)}, f32[8,144,128]{2,1,0:T(8,128)S(1)}) custom-call(s32[8,8]{1,0:T(8,128)S(1)} %copy-done.24, f32[8,1152,256]{2,1,0:T(8,128)} %cell_ref.3), custom_call_target="tpu_custom_call" | custom-call | tf_op jit(solution)/shard_map/first_edges/pallas_call | solution.py:210
  15.9 7.4 %all-to-all-start.1 = ((f32[8,576,128]{2,1,0:T(8,128)}), f32[8,576,128]{2,1,0:T(8,128)S(1)}, u32[]{:S(2)}, u32[]{:S(2)}) async-start(f32[8,576,128]{2,1,0:T(8,128)} %copy-done.10), calls=%async_computation.1 | async-start | bytes 4718592 | tf_op jit(solution)/shard_map/all_to_all | solution.py:1344
  25.7 2.1 collective-permute-start.2
  31.2 2.8 %collective-permute-start.3 = (f32[1,128]{1,0:T(1,128)S(1)}, f32[1,128]{1,0:T(1,128)S(1)}, u32[]{:S(2)}, u32[]{:S(2)}) collective-permute-start(f32[1,128]{1,0:T(1,128)S(1)} %pad.22), channel_id=1, source_target_pairs={{0,7},{1,0},{2,1},{3,2},{4,3},{5,4},{6,5},{7,6},{8,15},{9,8},{10,9... | collective-permute-start | bytes 1544 | tf_op jit(solution)/shard_map/ppermute | solution.py:1322
  34.2 10.6 %coarse_rows.1.rows_ref = f32[16,192,128]{2,1,0:T(8,128)S(1)} custom-call(bf16[48,144,384]{2,1,0:T(8,128)(2,1)} %bitcast.13, bf16[16,48,128]{2,1,0:T(8,128)(2,1)S(1)} %bitcast.10, bf16[384,256]{1,0:T(8,128)(2,1)S(1)} %add_convert_fusion.pick_ref), custom_call_target="tpu_custom_call" | custom-call | tf_op jit(solution)/shard_map/coarse_rows/pallas_call | solution.py:840
  44.7 17.5 %collective-permute-done.3.east_ref = f32[1,128]{1,0:T(1,128)S(1)} collective-permute-done((f32[1,128]{1,0:T(1,128)S(1)}, f32[1,128]{1,0:T(1,128)S(1)}, u32[]{:S(2)}, u32[]{:S(2)}) %collective-permute-start.3) | collective-permute-done | bytes 544 | tf_op jit(solution)/shard_map/ppermute | solution.py:1322
  62.2 4.2 %collective-permute-done.2.west_ref = f32[9,128]{1,0:T(8,128)S(1)} collective-permute-done((f32[9,128]{1,0:T(8,128)S(1)}, f32[9,128]{1,0:T(8,128)S(1)}, u32[]{:S(2)}, u32[]{:S(2)}) %collective-permute-start.2) | collective-permute-done | bytes 4640 | tf_op jit(solution)/shard_map/ppermute | solution.py:1321
  66.4 3.6 %coarsen.1 = (f32[8,208,256]{2,1,0:T(8,128)S(1)}, f32[296,256]{1,0:T(8,128)S(1)}) custom-call(s32[8,8]{1,0:T(8,128)S(1)} %copy-done.25, f32[16,192,128]{2,1,0:T(8,128)S(1)} %coarse_rows.1.rows_ref, f32[48,384]{1,0:T(8,128)S(1)} %copy-done.28, s32[16,128]{1,0:T(8,128)S(1)} %copy-done.30, f32[49,384]{1,0:T(8,128)S(1)} %collective-permute-done.south_ref, ...), custom_call_target="tpu_custom_call" | custom-call | tf_op jit(solution)/shard_map/coarsen/pallas_call | solution.py:968
  71.9 5.0 %all-to-all-done.1.quad_ref = f32[8,576,128]{2,1,0:T(8,128)S(1)} async-done(((f32[8,576,128]{2,1,0:T(8,128)}), f32[8,576,128]{2,1,0:T(8,128)S(1)}, u32[]{:S(2)}, u32[]{:S(2)}) %all-to-all-start.1) | async-done | bytes 2359328 | tf_op jit(solution)/shard_map/all_to_all | solution.py:1344
  78.3 8.4 %all-to-all-start = ((f32[8,208,256]{2,1,0:T(8,128)}), f32[8,208,256]{2,1,0:T(8,128)S(1)}, u32[]{:S(2)}, u32[]{:S(2)}) async-start(f32[8,208,256]{2,1,0:T(8,128)} %copy-done.13), calls=%async_computation | async-start | bytes 3407872 | tf_op jit(solution)/shard_map/all_to_all | solution.py:1344
  88.4 6.8 %tile_lines.1 = (f32[1152,128]{1,0:T(8,128)S(1)}, f32[1152,128]{1,0:T(8,128)}, f32[1152,128]{1,0:T(8,128)S(1)}, f32[1152,128]{1,0:T(8,128)S(1)}, f32[48,128]{1,0:T(8,128)}) custom-call(s32[8,8]{1,0:T(8,128)S(1)} %copy-done.25, f32[8,576,128]{2,1,0:T(8,128)S(1)} %copy-done.6), custom_call_target="tpu_custom_call" | custom-call | tf_op jit(solution)/shard_map/tile_lines/pallas_call | solution.py:1017
  102.3 2.8 %collective-permute-start.7 = (f32[48,128]{1,0:T(8,128)}, f32[48,128]{1,0:T(8,128)}, u32[]{:S(2)}, u32[]{:S(2)}) collective-permute-start(f32[48,128]{1,0:T(8,128)} %get-tuple-element.23), channel_id=1, source_target_pairs={{0,7},{1,0},{2,1},{3,2},{4,3},{5,4},{6,5},{7,6},{8,15},{9,8},{10,9... | collective-permute-start | bytes 73736 | tf_op jit(solution)/shard_map/ppermute | solution.py:1341
  105.1 21.7 %all-to-all-done.phys_ref.refs_0_.refs_2_.refs_4_ = f32[8,208,256]{2,1,0:T(8,128)S(1)} async-done(((f32[8,208,256]{2,1,0:T(8,128)}), f32[8,208,256]{2,1,0:T(8,128)S(1)}, u32[]{:S(2)}, u32[]{:S(2)}) %all-to-all-start) | async-done | bytes 1703968 | tf_op jit(solution)/shard_map/all_to_all | solution.py:1344
  126.8 2.2 hand_on.2
  130.0 3.6 %all-to-all-start.2 = ((f32[8,288,128]{2,1,0:T(8,128)}), f32[8,288,128]{2,1,0:T(8,128)S(1)}, u32[]{:S(2)}, u32[]{:S(2)}) async-start(f32[8,288,128]{2,1,0:T(8,128)} %copy-done.7), calls=%async_computation.2 | async-start | bytes 2359296 | tf_op jit(solution)/shard_map/all_to_all | solution.py:1344
  139.0 2.5 line_step.1
  146.3 3.0 %collective-permute-start.9 = (f32[8,144,128]{2,1,0:T(8,128)S(1)}, f32[8,144,128]{2,1,0:T(8,128)}, u32[]{:S(2)}, u32[]{:S(2)}) collective-permute-start(f32[8,144,128]{2,1,0:T(8,128)S(1)} %copy-done.15), channel_id=1, source_target_pairs={{0,7},{1,0},{2,1},{3,2},{4,3},{5,4},{6,5},{7,6},{8,15},{9,8},{10,9... | collective-permute-start | bytes 1769480 | tf_op jit(solution)/shard_map/ppermute | solution.py:1341
  149.3 14.1 %inner.2.part_ref.refs_4_ = f32[8,1152,256]{2,1,0:T(8,128)} custom-call(s32[8,8]{1,0:T(8,128)S(1)} %copy-done.25, f32[8,1152,256]{2,1,0:T(8,128)} %cell_ref.3, f32[8,208,256]{2,1,0:T(8,128)S(1)} %copy-done.1), custom_call_target="tpu_custom_call" | custom-call | tf_op jit(solution)/shard_map/inner/pallas_call | solution.py:542
  163.3 2.2 hand_on.3.refs_0_
  166.5 6.4 %collective-permute-done.8.rim_w_ref.refs_2_ = f32[8,144,128]{2,1,0:T(8,128)S(1)} collective-permute-done((f32[8,144,128]{2,1,0:T(8,128)S(1)}, f32[8,144,128]{2,1,0:T(8,128)S(1)}, u32[]{:S(2)}, u32[]{:S(2)}) %collective-permute-start.8) | collective-permute-done | bytes 589856 | tf_op jit(solution)/shard_map/ppermute | solution.py:1338
  172.9 4.4 %collective-permute-done.9.rim_e_ref.refs_3_ = f32[8,144,128]{2,1,0:T(8,128)} collective-permute-done((f32[8,144,128]{2,1,0:T(8,128)S(1)}, f32[8,144,128]{2,1,0:T(8,128)}, u32[]{:S(2)}, u32[]{:S(2)}) %collective-permute-start.9) | collective-permute-done | bytes 589856 | tf_op jit(solution)/shard_map/ppermute | solution.py:1341
  178.3 5.4 %all-to-all-start.3 = ((f32[8,288,128]{2,1,0:T(8,128)}), f32[8,288,128]{2,1,0:T(8,128)}, u32[]{:S(2)}, u32[]{:S(2)}) async-start(f32[8,288,128]{2,1,0:T(8,128)} %gate.3), calls=%async_computation.3 | async-start | bytes 2359296 | tf_op jit(solution)/shard_map/all_to_all | solution.py:1344
  183.7 13.7 %step.2 = (f32[8,1152,256]{2,1,0:T(8,128)}, f32[8,144,128]{2,1,0:T(8,128)S(1)}, f32[8,144,128]{2,1,0:T(8,128)S(1)}) custom-call(s32[8,8]{1,0:T(8,128)S(1)} %copy-done.25, f32[8,1152,256]{2,1,0:T(8,128)} %inner.2.part_ref.refs_4_, f32[8,208,256]{2,1,0:T(8,128)S(1)} %copy-done.1, f32[8,288,128]{2,1,0:T(8,128)S(1)} %copy-done.3, f32[8,144,128]{2,1,0:T(8,128)S(1)} %copy-done.9, ...), custom_call_target="tpu_custom_call" | custom-call | tf_op jit(solution)/shard_map/step/pallas_call | solution.py:704
  199.5 2.7 %collective-permute-start.13 = (f32[8,144,128]{2,1,0:T(8,128)S(1)}, f32[8,144,128]{2,1,0:T(8,128)S(1)}, u32[]{:S(2)}, u32[]{:S(2)}) collective-permute-start(f32[8,144,128]{2,1,0:T(8,128)S(1)} %get-tuple-element.35), channel_id=1, source_target_pairs={{0,7},{1,0},{2,1},{3,2},{4,3},{5,4},{6,5},{7,6},{8,15},{9,8},{10,9... | collective-permute-start | bytes 1769480 | tf_op jit(solution)/shard_map/ppermute | solution.py:1341
  202.2 14.1 %inner.3.part_ref.refs_0_.refs_1_.refs_2_.refs_3_ = f32[8,1152,256]{2,1,0:T(8,128)} custom-call(s32[8,8]{1,0:T(8,128)S(1)} %copy-done.25, f32[8,1152,256]{2,1,0:T(8,128)} %get-tuple-element.28.cell_ref, f32[8,208,256]{2,1,0:T(8,128)S(1)} %copy-done.1), custom_call_target="tpu_custom_call" | custom-call | tf_op jit(solution)/shard_map/inner/pallas_call | solution.py:542
  216.2 11.2 %collective-permute-done.12.rim_w_ref.refs_6_ = f32[8,144,128]{2,1,0:T(8,128)S(1)} collective-permute-done((f32[8,144,128]{2,1,0:T(8,128)S(1)}, f32[8,144,128]{2,1,0:T(8,128)S(1)}, u32[]{:S(2)}, u32[]{:S(2)}) %collective-permute-start.12) | collective-permute-done | bytes 589856 | tf_op jit(solution)/shard_map/ppermute | solution.py:1338
  227.4 3.2 %collective-permute-done.13.rim_e_ref.refs_7_ = f32[8,144,128]{2,1,0:T(8,128)S(1)} collective-permute-done((f32[8,144,128]{2,1,0:T(8,128)S(1)}, f32[8,144,128]{2,1,0:T(8,128)S(1)}, u32[]{:S(2)}, u32[]{:S(2)}) %collective-permute-start.13) | collective-permute-done | bytes 589856 | tf_op jit(solution)/shard_map/ppermute | solution.py:1341
  230.5 8.5 %last_chl.1 = f32[8,48,256]{2,1,0:T(8,128)} custom-call(s32[8,8]{1,0:T(8,128)S(1)} %copy-done.25, f32[8,1152,256]{2,1,0:T(8,128)} %inner.3.part_ref.refs_0_.refs_1_.refs_2_.refs_3_, f32[8,1152,256]{2,1,0:T(8,128)} %inner.3.part_ref.refs_0_.refs_1_.refs_2_.refs_3_, f32[8,1152,256]{2,1,0:T(8,128)} %inner.3.part_ref.refs_0_.refs_1_.refs_2_.refs_3_, ...), custom_call_target="tpu_custom_call" | custom-call | tf_op jit(solution)/shard_map/last_chl/pallas_call | solution.py:794
  239.0 4.4 %all-to-all-start.4 = ((f32[8,48,256]{2,1,0:T(8,128)}), f32[8,48,256]{2,1,0:T(8,128)S(1)}, u32[]{:S(2)}, u32[]{:S(2)}) async-start(f32[8,48,256]{2,1,0:T(8,128)} %last_chl.1), calls=%async_computation.4 | async-start | bytes 786432 | tf_op jit(solution)/shard_map/all_to_all | solution.py:1344
  243.4 13.3 %step.3.after_ref = f32[8,1152,256]{2,1,0:T(8,128)} custom-call(s32[8,8]{1,0:T(8,128)S(1)} %copy-done.25, f32[8,1152,256]{2,1,0:T(8,128)} %inner.3.part_ref.refs_0_.refs_1_.refs_2_.refs_3_, f32[8,208,256]{2,1,0:T(8,128)S(1)} %copy-done.1, f32[8,288,128]{2,1,0:T(8,128)} %all-to-all-done.3.rim_ref.refs_5_, ...), custom_call_target="tpu_custom_call" | custom-call | tf_op jit(solution)/shard_map/step/pallas_call | solution.py:704
  256.7 4.3 %heat.1 = bf16[48,48,384]{2,1,0:T(8,128)(2,1)} custom-call(s32[8,8]{1,0:T(8,128)S(1)} %copy-done.25, f32[8,48,256]{2,1,0:T(8,128)S(1)} %all-to-all-done.4.chl_ref, f32[48,384]{1,0:T(8,128)S(1)} %copy-done.28, s32[16,128]{1,0:T(8,128)S(1)} %copy-done.31, bf16[128,384]{1,0:T(8,128)(2,1)S(1)} %fusion.widen_ref, f32[8,1152,256]{2,1,0:T(8,128)} %step.3.after_ref), custom_call_target="tpu_custom_call" | custom-call | tf_op jit(solution)/shard_map/heat/pallas_call | solution.py:1267
  (107 shorter events, 36.9 us)
Async XLA Ops:
  15.9 9.6 %copy-start.30 = (s32[16,128]{1,0:T(8,128)S(1)}, s32[16,128]{1,0:T(8,128)}, u32[]{:S(2)}) copy-start(s32[16,128]{1,0:T(8,128)} %land_ref.3) | copy-start | bytes 24580
  15.9 18.2 %copy-start.29 = (bf16[16,128,48]{1,2,0:T(8,128)(2,1)S(1)}, bf16[16,128,48]{1,2,0:T(8,128)(2,1)}, u32[]{:S(2)}) copy-start(bf16[16,128,48]{1,2,0:T(8,128)(2,1)} %param.8) | copy-start | bytes 589828
  15.9 61.0 %all-to-all-start.1 = ((f32[8,576,128]{2,1,0:T(8,128)}), f32[8,576,128]{2,1,0:T(8,128)S(1)}, u32[]{:S(2)}, u32[]{:S(2)}) async-start(f32[8,576,128]{2,1,0:T(8,128)} %copy-done.10), calls=%async_computation.1 | async-start | bytes 4718592 | tf_op jit(solution)/shard_map/all_to_all | solution.py:1344
  25.7 40.7 %collective-permute-start.2 = (f32[9,128]{1,0:T(8,128)S(1)}, f32[9,128]{1,0:T(8,128)S(1)}, u32[]{:S(2)}, u32[]{:S(2)}) collective-permute-start(f32[9,128]{1,0:T(8,128)S(1)} %select_maximum_fusion.1), channel_id=1, source_target_pairs={{0,1},{1,2},{2,3},{3,4},{4,5},{5,6},{6,7},{7,0},{8,9},{9,10},{10,1... | collective-permute-start | bytes 13832 | tf_op jit(solution)/shard_map/ppermute | solution.py:1321
  28.5 37.9 %collective-permute-start = (f32[49,384]{1,0:T(8,128)S(1)}, f32[49,384]{1,0:T(8,128)S(1)}, u32[]{:S(2)}, u32[]{:S(2)}) collective-permute-start(f32[49,384]{1,0:T(8,128)S(1)} %select_maximum_fusion), channel_id=1, source_target_pairs={{0,8},{8,16},{16,24},{1,9},{9,17},{17,25},{2,10},{10,18},{18,26},{... | collective-permute-start | bytes 225800 | tf_op jit(solution)/shard_map/ppermute | solution.py:1319
  29.9 32.4 %collective-permute-start.1 = (f32[1,384]{1,0:T(1,128)S(1)}, f32[1,384]{1,0:T(1,128)S(1)}, u32[]{:S(2)}, u32[]{:S(2)}) collective-permute-start(f32[1,384]{1,0:T(1,128)S(1)} %pad.19), channel_id=1, source_target_pairs={{8,0},{16,8},{24,16},{9,1},{17,9},{25,17},{10,2},{18,10},{26,18},{... | collective-permute-start | bytes 4616 | tf_op jit(solution)/shard_map/ppermute | solution.py:1320
  31.2 31.1 %collective-permute-start.3 = (f32[1,128]{1,0:T(1,128)S(1)}, f32[1,128]{1,0:T(1,128)S(1)}, u32[]{:S(2)}, u32[]{:S(2)}) collective-permute-start(f32[1,128]{1,0:T(1,128)S(1)} %pad.22), channel_id=1, source_target_pairs={{0,7},{1,0},{2,1},{3,2},{4,3},{5,4},{6,5},{7,6},{8,15},{9,8},{10,9... | collective-permute-start | bytes 1544 | tf_op jit(solution)/shard_map/ppermute | solution.py:1322
  34.1 32.3 %copy-start.25 = (s32[8,8]{1,0:T(8,128)S(1)}, s32[8,8]{1,0:T(8,128)}, u32[]{:S(2)}) copy-start(s32[8,8]{1,0:T(8,128)} %routing.1.table_ref) | copy-start | bytes 772
  34.2 32.3 %copy-start.28 = (f32[48,384]{1,0:T(8,128)S(1)}, f32[48,384]{1,0:T(8,128)}, u32[]{:S(2)}) copy-start(f32[48,384]{1,0:T(8,128)} %light_ref.3) | copy-start | bytes 221188
  78.3 48.4 %all-to-all-start = ((f32[8,208,256]{2,1,0:T(8,128)}), f32[8,208,256]{2,1,0:T(8,128)S(1)}, u32[]{:S(2)}, u32[]{:S(2)}) async-start(f32[8,208,256]{2,1,0:T(8,128)} %copy-done.13), calls=%async_computation | async-start | bytes 3407872 | tf_op jit(solution)/shard_map/all_to_all | solution.py:1344
  96.8 29.9 %collective-permute-start.4 = (f32[1152,128]{1,0:T(8,128)}, f32[1152,128]{1,0:T(8,128)S(1)}, u32[]{:S(2)}, u32[]{:S(2)}) collective-permute-start(f32[1152,128]{1,0:T(8,128)} %get-tuple-element.21.high_ref), channel_id=1, source_target_pairs={{0,8},{8,16},{16,24},{1,9},{9,17},{17,25},{2,10},{10,18},{18,26},{... | collective-permute-start | bytes 1769480 | tf_op jit(solution)/shard_map/ppermute | solution.py:1332
  98.2 28.5 %collective-permute-start.5 = (f32[1152,128]{1,0:T(8,128)S(1)}, f32[1152,128]{1,0:T(8,128)S(1)}, u32[]{:S(2)}, u32[]{:S(2)}) collective-permute-start(f32[1152,128]{1,0:T(8,128)S(1)} %get-tuple-element.22.low_ref), channel_id=1, source_target_pairs={{8,0},{16,8},{24,16},{9,1},{17,9},{25,17},{10,2},{18,10},{26,18},{... | collective-permute-start | bytes 1769480 | tf_op jit(solution)/shard_map/ppermute | solution.py:1335
  100.3 26.4 %collective-permute-start.6 = (f32[48,128]{1,0:T(8,128)}, f32[48,128]{1,0:T(8,128)}, u32[]{:S(2)}, u32[]{:S(2)}) collective-permute-start(f32[48,128]{1,0:T(8,128)} %get-tuple-element.23), channel_id=1, source_target_pairs={{0,1},{1,2},{2,3},{3,4},{4,5},{5,6},{6,7},{7,0},{8,9},{9,10},{10,1... | collective-permute-start | bytes 73736 | tf_op jit(solution)/shard_map/ppermute | solution.py:1338
  102.3 24.4 %collective-permute-start.7 = (f32[48,128]{1,0:T(8,128)}, f32[48,128]{1,0:T(8,128)}, u32[]{:S(2)}, u32[]{:S(2)}) collective-permute-start(f32[48,128]{1,0:T(8,128)} %get-tuple-element.23), channel_id=1, source_target_pairs={{0,7},{1,0},{2,1},{3,2},{4,3},{5,4},{6,5},{7,6},{8,15},{9,8},{10,9... | collective-permute-start | bytes 73736 | tf_op jit(solution)/shard_map/ppermute | solution.py:1341
  126.7 3.3 %copy-start = (f32[8,208,256]{2,1,0:T(8,128)}, f32[8,208,256]{2,1,0:T(8,128)S(1)}, u32[]{:S(2)}) copy-start(f32[8,208,256]{2,1,0:T(8,128)S(1)} %all-to-all-done.phys_ref.refs_0_.refs_2_.refs_4_) | copy-start | bytes 5111812
  126.7 3.3 %copy-start.11 = (f32[1152,128]{1,0:T(8,128)}, f32[1152,128]{1,0:T(8,128)S(1)}, u32[]{:S(2)}) copy-start(f32[1152,128]{1,0:T(8,128)S(1)} %collective-permute-done.5.above_ref) | copy-start | bytes 1769476
  130.0 47.3 %all-to-all-start.2 = ((f32[8,288,128]{2,1,0:T(8,128)}), f32[8,288,128]{2,1,0:T(8,128)S(1)}, u32[]{:S(2)}, u32[]{:S(2)}) async-start(f32[8,288,128]{2,1,0:T(8,128)} %copy-done.7), calls=%async_computation.2 | async-start | bytes 2359296 | tf_op jit(solution)/shard_map/all_to_all | solution.py:1344
  133.6 15.7 %copy-start.1 = (f32[8,208,256]{2,1,0:T(8,128)S(1)}, f32[8,208,256]{2,1,0:T(8,128)}, u32[]{:S(2)}) copy-start(f32[8,208,256]{2,1,0:T(8,128)} %copy-done) | copy-start | bytes 5111812
  138.9 5.5 %copy-start.17 = (f32[8,144,128]{2,1,0:T(8,128)S(1)}, f32[8,144,128]{2,1,0:T(8,128)}, u32[]{:S(2)}) copy-start(f32[8,144,128]{2,1,0:T(8,128)} %get-tuple-element.26) | copy-start | bytes 1769476
  139.0 7.3 %copy-start.15 = (f32[8,144,128]{2,1,0:T(8,128)S(1)}, f32[8,144,128]{2,1,0:T(8,128)}, u32[]{:S(2)}) copy-start(f32[8,144,128]{2,1,0:T(8,128)} %get-tuple-element.27) | copy-start | bytes 1769476
  141.5 21.8 %collective-permute-start.10 = (f32[1152,128]{1,0:T(8,128)S(1)}, f32[1152,128]{1,0:T(8,128)S(1)}, u32[]{:S(2)}, u32[]{:S(2)}) collective-permute-start(f32[1152,128]{1,0:T(8,128)S(1)} %get-tuple-element.32), channel_id=1, source_target_pairs={{0,8},{8,16},{16,24},{1,9},{9,17},{17,25},{2,10},{10,18},{18,26},{... | collective-permute-start | bytes 1769480 | tf_op jit(solution)/shard_map/ppermute | solution.py:1332
  143.2 20.2 %collective-permute-start.11 = (f32[1152,128]{1,0:T(8,128)S(1)}, f32[1152,128]{1,0:T(8,128)S(1)}, u32[]{:S(2)}, u32[]{:S(2)}) collective-permute-start(f32[1152,128]{1,0:T(8,128)S(1)} %get-tuple-element.33), channel_id=1, source_target_pairs={{8,0},{16,8},{24,16},{9,1},{17,9},{25,17},{10,2},{18,10},{26,18},{... | collective-permute-start | bytes 1769480 | tf_op jit(solution)/shard_map/ppermute | solution.py:1335
  144.5 28.4 %collective-permute-start.8 = (f32[8,144,128]{2,1,0:T(8,128)S(1)}, f32[8,144,128]{2,1,0:T(8,128)S(1)}, u32[]{:S(2)}, u32[]{:S(2)}) collective-permute-start(f32[8,144,128]{2,1,0:T(8,128)S(1)} %copy-done.17), channel_id=1, source_target_pairs={{0,1},{1,2},{2,3},{3,4},{4,5},{5,6},{6,7},{7,0},{8,9},{9,10},{10,1... | collective-permute-start | bytes 1769480 | tf_op jit(solution)/shard_map/ppermute | solution.py:1338
  146.3 31.0 %collective-permute-start.9 = (f32[8,144,128]{2,1,0:T(8,128)S(1)}, f32[8,144,128]{2,1,0:T(8,128)}, u32[]{:S(2)}, u32[]{:S(2)}) collective-permute-start(f32[8,144,128]{2,1,0:T(8,128)S(1)} %copy-done.15), channel_id=1, source_target_pairs={{0,7},{1,0},{2,1},{3,2},{4,3},{5,4},{6,5},{7,6},{8,15},{9,8},{10,9... | collective-permute-start | bytes 1769480 | tf_op jit(solution)/shard_map/ppermute | solution.py:1341
  172.9 4.4 %copy-start.8 = (f32[8,144,128]{2,1,0:T(8,128)}, f32[8,144,128]{2,1,0:T(8,128)S(1)}, u32[]{:S(2)}) copy-start(f32[8,144,128]{2,1,0:T(8,128)S(1)} %collective-permute-done.8.rim_w_ref.refs_2_) | copy-start | bytes 1769476
  178.3 5.4 %copy-start.3 = (f32[8,288,128]{2,1,0:T(8,128)S(1)}, f32[8,288,128]{2,1,0:T(8,128)}, u32[]{:S(2)}) copy-start(f32[8,288,128]{2,1,0:T(8,128)} %copy-done.2) | copy-start | bytes 3538948
  178.3 5.4 %copy-start.9 = (f32[8,144,128]{2,1,0:T(8,128)S(1)}, f32[8,144,128]{2,1,0:T(8,128)}, u32[]{:S(2)}) copy-start(f32[8,144,128]{2,1,0:T(8,128)} %copy-done.8) | copy-start | bytes 1769476
  178.3 52.2 %all-to-all-start.3 = ((f32[8,288,128]{2,1,0:T(8,128)}), f32[8,288,128]{2,1,0:T(8,128)}, u32[]{:S(2)}, u32[]{:S(2)}) async-start(f32[8,288,128]{2,1,0:T(8,128)} %gate.3), calls=%async_computation.3 | async-start | bytes 2359296 | tf_op jit(solution)/shard_map/all_to_all | solution.py:1344
  197.4 29.9 %collective-permute-start.12 = (f32[8,144,128]{2,1,0:T(8,128)S(1)}, f32[8,144,128]{2,1,0:T(8,128)S(1)}, u32[]{:S(2)}, u32[]{:S(2)}) collective-permute-start(f32[8,144,128]{2,1,0:T(8,128)S(1)} %get-tuple-element.34), channel_id=1, source_target_pairs={{0,1},{1,2},{2,3},{3,4},{4,5},{5,6},{6,7},{7,0},{8,9},{9,10},{10,1... | collective-permute-start | bytes 1769480 | tf_op jit(solution)/shard_map/ppermute | solution.py:1338
  199.5 31.1 %collective-permute-start.13 = (f32[8,144,128]{2,1,0:T(8,128)S(1)}, f32[8,144,128]{2,1,0:T(8,128)S(1)}, u32[]{:S(2)}, u32[]{:S(2)}) collective-permute-start(f32[8,144,128]{2,1,0:T(8,128)S(1)} %get-tuple-element.35), channel_id=1, source_target_pairs={{0,7},{1,0},{2,1},{3,2},{4,3},{5,4},{6,5},{7,6},{8,15},{9,8},{10,9... | collective-permute-start | bytes 1769480 | tf_op jit(solution)/shard_map/ppermute | solution.py:1341
  239.0 17.7 %all-to-all-start.4 = ((f32[8,48,256]{2,1,0:T(8,128)}), f32[8,48,256]{2,1,0:T(8,128)S(1)}, u32[]{:S(2)}, u32[]{:S(2)}) async-start(f32[8,48,256]{2,1,0:T(8,128)} %last_chl.1), calls=%async_computation.4 | async-start | bytes 786432 | tf_op jit(solution)/shard_map/all_to_all | solution.py:1344
  243.4 13.3 %copy-start.31 = (s32[16,128]{1,0:T(8,128)S(1)}, s32[16,128]{1,0:T(8,128)}, u32[]{:S(2)}) copy-start(s32[16,128]{1,0:T(8,128)} %land_ref.3) | copy-start | bytes 24580
  (19 other events, 19.6 us)

commit v6 on v5

--- a/solution.py
+++ b/solution.py
@@ -177,7 +177,7 @@
     return values
 
 
-def edges_kernel(levels, side, table_ref, cell_ref, rows_ref, west_ref, east_ref):
+def edges_kernel(levels, side, table_ref, cell_ref, *refs):
     group = LANES // side
     rounds = cell_ref.shape[1] // levels // group
     level_tiles = levels // SUB
@@ -190,42 +190,40 @@
                 at = pl.multiple_of((i * group + g) * levels + lt * SUB, SUB)
                 first.append(cell_ref[0, pl.ds(at, SUB), 0:LANES])
                 second.append(cell_ref[0, pl.ds(at, SUB), LANES : 2 * LANES])
-            west, east = pack_columns(first, second, side)
-            west_ref[0, pl.ds(row, SUB), :] = west
-            east_ref[0, pl.ds(row, SUB), :] = east
+            if len(refs) == 2:
+                for ref, column in zip(refs, pack_columns(first, second, side)):
+                    ref[0, pl.ds(row, SUB), :] = column
+                continue
             for n, quad in enumerate(pack_quads(first, second, side)):
                 at = pl.multiple_of((i * (group // 2) + n) * levels + lt * SUB, SUB)
-                rows_ref[0, pl.ds(at, SUB), :] = quad
+                refs[0][0, pl.ds(at, SUB), :] = quad
         return carry
 
     lax.fori_loop(0, level_tiles, body, 0, unroll=True)
 
 
-def first_edges(table, tracers, levels, side):
+def first_edges(table, tracers, levels, side, columns):
     slot_count, channels, cell_count = tracers.shape
     lon_count = lax.axis_size("lon")
     rows = channels * side // LANES
     f32 = jnp.float32
-    by_slot = pl.BlockSpec((1, rows, LANES), lambda s, t: (s, 0, 0))
+    if columns:
+        shapes = [jax.ShapeDtypeStruct((slot_count, rows, LANES), f32)] * 2
+        specs = [pl.BlockSpec((1, rows, LANES), lambda s, t: (s, 0, 0))] * 2
+    else:
+        shapes = [jax.ShapeDtypeStruct((lon_count, 4 * rows, LANES), f32)]
+        specs = [pl.BlockSpec((1, 4 * rows, LANES), lambda s, t: (t[SLOT_TILE, s], 0, 0))]
     return pl.pallas_call(
         functools.partial(edges_kernel, levels, side),
-        out_shape=[
-            jax.ShapeDtypeStruct((lon_count, 4 * rows, LANES), f32),
-            jax.ShapeDtypeStruct((slot_count, rows, LANES), f32),
-            jax.ShapeDtypeStruct((slot_count, rows, LANES), f32),
-        ],
+        out_shape=shapes,
         grid_spec=pltpu.PrefetchScalarGridSpec(
             num_scalar_prefetch=1,
             grid=(slot_count,),
             in_specs=[pl.BlockSpec((1, channels, cell_count), lambda s, t: (s, 0, 0))],
-            out_specs=[
-                pl.BlockSpec((1, 4 * rows, LANES), lambda s, t: (t[SLOT_TILE, s], 0, 0)),
-                by_slot,
-                by_slot,
-            ],
+            out_specs=specs,
         ),
         compiler_params=pltpu.CompilerParams(vmem_limit_bytes=VMEM_LIMIT),
-        name="first_edges",
+        name="first_columns" if columns else "first_rows",
     )(table, tracers)
 
 
@@ -1343,8 +1341,9 @@
     def across(x):
         return lax.all_to_all(x, "lon", 0, 0, tiled=True)
 
-    quads, west, east = first_edges(table, tracers, levels, side)
+    (quads,) = first_edges(table, tracers, levels, side, False)
     quads = across(quads)
+    west, east = first_edges(table, tracers, levels, side, True)
     rows = coarse_rows(fine, mix, picks)
     phys, line_phys = coarsen(
         table, rows, surf_light, land_mask, from_south, from_north, from_west, from_east, picks

time: 264 us -> 268 us (1.015)
  Pallas kernels: 107 us -> 117 us
  waiting for transfers between devices: 73.5 us -> 68.7 us
    pallas_call x1 -> x2, Pallas kernels: 8.51 us -> 15 us  [first_edges(): pl.pallas_call(functools.partial(edges_kernel, levels, side), out_shape=s...]
    ppermute x3, waiting for transfers between devices: 7.53 us -> 4.03 us  [to_west(): return lax.ppermute(x, 'lon', along('lon', -1, True))]
  transfers between devices with their start and end apart: 19 -> 19, of which waited for: 8 -> 8; matrix products, arithmetic and copies ran while one was open for 1% -> 1% of each run, Pallas kernels for 31% -> 34%
where the time goes in v6:
time: 268 us; the launch traced here: 265 us
  Pallas kernels  117 us (44%)
  waiting for transfers between devices  68.7 us (26%)
  starting transfers between devices  55.6 us (21%)
  local copies, waits for them, and re-layouts  20.2 us (8%)
    pallas_call x2, Pallas kernels, inner(): pl.pallas_call(functools.partial(inner_kernel, levels, side), out_shape=j...  29.8 us
    pallas_call x2, Pallas kernels, step(): pl.pallas_call(functools.partial(step_kernel, levels, side, last), out_sh...  28.3 us
    all_to_all x5, starting transfers between devices, across(): return lax.all_to_all(x, 'lon', 0, 0, tiled=True)  27.9 us
    all_to_all x5, waiting for transfers between devices, across(): return lax.all_to_all(x, 'lon', 0, 0, tiled=True)  26.7 us
    unnamed x65, local copies, waits for them, and re-layouts  19.8 us
    ppermute x1, waiting for transfers between devices, on_device(): from_east = lax.ppermute(westward, 'lon', along('lon', -1, True))  18.2 us
    ppermute x3, waiting for transfers between devices, to_east(): return lax.ppermute(x, 'lon', along('lon', 1, True))  15.9 us
    pallas_call x2, Pallas kernels, first_edges(): pl.pallas_call(functools.partial(edges_kernel, levels, side), out_shape=s...  15 us
  transfers between devices with their start and end apart: 19, of which 8 were waited for; matrix products, arithmetic and copies ran while one was open for 1% of the time, Pallas kernels for 34%

profile of v6, /device:TPU:0, one launch (start us, length us, event | category | flops | bytes accessed | tf_op | source)
XLA Modules:
  0.0 265.1 jit_solution(16850493319086808837)
XLA Ops:
  0.6 2.8 %routing.1.table_ref = s32[8,8]{1,0:T(8,128)} custom-call(s32[1,64]{1,0:T(1,128)} %row_ref.1), custom_call_target="tpu_custom_call" | custom-call | tf_op jit(solution)/shard_map/routing/pallas_call | solution.py:131
  4.1 7.2 %first_rows.1 = f32[8,576,128]{2,1,0:T(8,128)S(1)} custom-call(s32[8,8]{1,0:T(8,128)S(1)} %copy-done.14, f32[8,1152,256]{2,1,0:T(8,128)} %cell_ref.5), custom_call_target="tpu_custom_call" | custom-call | tf_op jit(solution)/shard_map/first_rows/pallas_call | solution.py:216
  12.7 7.4 %all-to-all-start.1 = ((f32[8,576,128]{2,1,0:T(8,128)}), f32[8,576,128]{2,1,0:T(8,128)S(1)}, u32[]{:S(2)}, u32[]{:S(2)}) async-start(f32[8,576,128]{2,1,0:T(8,128)} %copy-done.7), calls=%async_computation.1 | async-start | bytes 4718592 | tf_op jit(solution)/shard_map/all_to_all | solution.py:1342
  28.1 3.1 %collective-permute-start.3 = (f32[1,128]{1,0:T(1,128)S(1)}, f32[1,128]{1,0:T(1,128)S(1)}, u32[]{:S(2)}, u32[]{:S(2)}) collective-permute-start(f32[1,128]{1,0:T(1,128)S(1)} %pad.22), channel_id=1, source_target_pairs={{0,7},{1,0},{2,1},{3,2},{4,3},{5,4},{6,5},{7,6},{8,15},{9,8},{10,9... | collective-permute-start | bytes 1544 | tf_op jit(solution)/shard_map/ppermute | solution.py:1320
  31.4 10.6 %coarse_rows.1.rows_ref = f32[16,192,128]{2,1,0:T(8,128)S(1)} custom-call(bf16[48,144,384]{2,1,0:T(8,128)(2,1)} %bitcast.13, bf16[16,48,128]{2,1,0:T(8,128)(2,1)S(1)} %bitcast.10, bf16[384,256]{1,0:T(8,128)(2,1)S(1)} %add_convert_fusion.pick_ref), custom_call_target="tpu_custom_call" | custom-call | tf_op jit(solution)/shard_map/coarse_rows/pallas_call | solution.py:838
  42.0 18.2 %collective-permute-done.3.east_ref = f32[1,128]{1,0:T(1,128)S(1)} collective-permute-done((f32[1,128]{1,0:T(1,128)S(1)}, f32[1,128]{1,0:T(1,128)S(1)}, u32[]{:S(2)}, u32[]{:S(2)}) %collective-permute-start.3) | collective-permute-done | bytes 544 | tf_op jit(solution)/shard_map/ppermute | solution.py:1320
  60.2 3.8 %collective-permute-done.2.west_ref = f32[9,128]{1,0:T(8,128)S(1)} collective-permute-done((f32[9,128]{1,0:T(8,128)S(1)}, f32[9,128]{1,0:T(8,128)S(1)}, u32[]{:S(2)}, u32[]{:S(2)}) %collective-permute-start.2) | collective-permute-done | bytes 4640 | tf_op jit(solution)/shard_map/ppermute | solution.py:1319
  64.0 3.6 %coarsen.1 = (f32[8,208,256]{2,1,0:T(8,128)S(1)}, f32[296,256]{1,0:T(8,128)S(1)}) custom-call(s32[8,8]{1,0:T(8,128)S(1)} %copy-done.15, f32[16,192,128]{2,1,0:T(8,128)S(1)} %coarse_rows.1.rows_ref, f32[48,384]{1,0:T(8,128)S(1)} %copy-done.28, s32[16,128]{1,0:T(8,128)S(1)} %copy-done.30, f32[49,384]{1,0:T(8,128)S(1)} %collective-permute-done.south_ref, ...), custom_call_target="tpu_custom_call" | custom-call | tf_op jit(solution)/shard_map/coarsen/pallas_call | solution.py:966
  69.5 5.0 %all-to-all-done.1.quad_ref = f32[8,576,128]{2,1,0:T(8,128)S(1)} async-done(((f32[8,576,128]{2,1,0:T(8,128)}), f32[8,576,128]{2,1,0:T(8,128)S(1)}, u32[]{:S(2)}, u32[]{:S(2)}) %all-to-all-start.1) | async-done | bytes 2359328 | tf_op jit(solution)/shard_map/all_to_all | solution.py:1342
  75.9 8.4 %all-to-all-start = ((f32[8,208,256]{2,1,0:T(8,128)}), f32[8,208,256]{2,1,0:T(8,128)S(1)}, u32[]{:S(2)}, u32[]{:S(2)}) async-start(f32[8,208,256]{2,1,0:T(8,128)} %copy-done.13), calls=%async_computation | async-start | bytes 3407872 | tf_op jit(solution)/shard_map/all_to_all | solution.py:1342
  86.0 6.8 %tile_lines.1 = (f32[1152,128]{1,0:T(8,128)S(1)}, f32[1152,128]{1,0:T(8,128)}, f32[1152,128]{1,0:T(8,128)S(1)}, f32[1152,128]{1,0:T(8,128)S(1)}, f32[48,128]{1,0:T(8,128)}) custom-call(s32[8,8]{1,0:T(8,128)S(1)} %copy-done.15, f32[8,576,128]{2,1,0:T(8,128)S(1)} %copy-done.6), custom_call_target="tpu_custom_call" | custom-call | tf_op jit(solution)/shard_map/tile_lines/pallas_call | solution.py:1015
  99.9 2.8 %collective-permute-start.7 = (f32[48,128]{1,0:T(8,128)}, f32[48,128]{1,0:T(8,128)}, u32[]{:S(2)}, u32[]{:S(2)}) collective-permute-start(f32[48,128]{1,0:T(8,128)} %get-tuple-element.21), channel_id=1, source_target_pairs={{0,7},{1,0},{2,1},{3,2},{4,3},{5,4},{6,5},{7,6},{8,15},{9,8},{10,9... | collective-permute-start | bytes 73736 | tf_op jit(solution)/shard_map/ppermute | solution.py:1339
  102.7 21.7 %all-to-all-done.phys_ref.refs_0_.refs_2_.refs_4_ = f32[8,208,256]{2,1,0:T(8,128)S(1)} async-done(((f32[8,208,256]{2,1,0:T(8,128)}), f32[8,208,256]{2,1,0:T(8,128)S(1)}, u32[]{:S(2)}, u32[]{:S(2)}) %all-to-all-start) | async-done | bytes 1703968 | tf_op jit(solution)/shard_map/all_to_all | solution.py:1342
  124.4 2.2 hand_on.2
  127.6 3.6 %all-to-all-start.2 = ((f32[8,288,128]{2,1,0:T(8,128)}), f32[8,288,128]{2,1,0:T(8,128)S(1)}, u32[]{:S(2)}, u32[]{:S(2)}) async-start(f32[8,288,128]{2,1,0:T(8,128)} %copy-done.8), calls=%async_computation.2 | async-start | bytes 2359296 | tf_op jit(solution)/shard_map/all_to_all | solution.py:1342
  131.2 7.8 %first_columns.1 = (f32[8,144,128]{2,1,0:T(8,128)S(1)}, f32[8,144,128]{2,1,0:T(8,128)S(1)}) custom-call(s32[8,8]{1,0:T(8,128)S(1)} %copy-done.15, f32[8,1152,256]{2,1,0:T(8,128)} %cell_ref.5), custom_call_target="tpu_custom_call" | custom-call | tf_op jit(solution)/shard_map/first_columns/pallas_call | solution.py:216
  146.0 2.5 line_step.1
  153.3 3.0 %collective-permute-start.9 = (f32[8,144,128]{2,1,0:T(8,128)S(1)}, f32[8,144,128]{2,1,0:T(8,128)}, u32[]{:S(2)}, u32[]{:S(2)}) collective-permute-start(f32[8,144,128]{2,1,0:T(8,128)S(1)} %copy-done.17), channel_id=1, source_target_pairs={{0,7},{1,0},{2,1},{3,2},{4,3},{5,4},{6,5},{7,6},{8,15},{9,8},{10,9... | collective-permute-start | bytes 1769480 | tf_op jit(solution)/shard_map/ppermute | solution.py:1339
  156.3 14.9 %inner.2.part_ref.refs_4_ = f32[8,1152,256]{2,1,0:T(8,128)} custom-call(s32[8,8]{1,0:T(8,128)S(1)} %copy-done.15, f32[8,1152,256]{2,1,0:T(8,128)} %cell_ref.5, f32[8,208,256]{2,1,0:T(8,128)S(1)} %copy-done.1), custom_call_target="tpu_custom_call" | custom-call | tf_op jit(solution)/shard_map/inner/pallas_call | solution.py:540
  171.2 2.2 hand_on.3.refs_0_
  174.4 6.1 %collective-permute-done.8.rim_w_ref.refs_2_ = f32[8,144,128]{2,1,0:T(8,128)S(1)} collective-permute-done((f32[8,144,128]{2,1,0:T(8,128)S(1)}, f32[8,144,128]{2,1,0:T(8,128)S(1)}, u32[]{:S(2)}, u32[]{:S(2)}) %collective-permute-start.8) | collective-permute-done | bytes 589856 | tf_op jit(solution)/shard_map/ppermute | solution.py:1336
  182.4 4.7 %all-to-all-start.3 = ((f32[8,288,128]{2,1,0:T(8,128)}), f32[8,288,128]{2,1,0:T(8,128)}, u32[]{:S(2)}, u32[]{:S(2)}) async-start(f32[8,288,128]{2,1,0:T(8,128)} %gate.3), calls=%async_computation.3 | async-start | bytes 2359296 | tf_op jit(solution)/shard_map/all_to_all | solution.py:1342
  187.1 14.4 %step.2 = (f32[8,1152,256]{2,1,0:T(8,128)}, f32[8,144,128]{2,1,0:T(8,128)S(1)}, f32[8,144,128]{2,1,0:T(8,128)S(1)}) custom-call(s32[8,8]{1,0:T(8,128)S(1)} %copy-done.15, f32[8,1152,256]{2,1,0:T(8,128)} %inner.2.part_ref.refs_4_, f32[8,208,256]{2,1,0:T(8,128)S(1)} %copy-done.1, f32[8,288,128]{2,1,0:T(8,128)S(1)} %copy-done.3, f32[8,144,128]{2,1,0:T(8,128)S(1)} %copy-done.10, ...), custom_call_target="tpu_custom_call" | custom-call | tf_op jit(solution)/shard_map/step/pallas_call | solution.py:702
  201.5 2.2 collective-permute-start.12
  203.7 2.5 collective-permute-start.13
  206.2 14.9 %inner.3.part_ref.refs_0_.refs_1_.refs_2_.refs_3_ = f32[8,1152,256]{2,1,0:T(8,128)} custom-call(s32[8,8]{1,0:T(8,128)S(1)} %copy-done.15, f32[8,1152,256]{2,1,0:T(8,128)} %get-tuple-element.26.cell_ref, f32[8,208,256]{2,1,0:T(8,128)S(1)} %copy-done.1), custom_call_target="tpu_custom_call" | custom-call | tf_op jit(solution)/shard_map/inner/pallas_call | solution.py:540
  221.1 9.7 %collective-permute-done.12.rim_w_ref.refs_6_ = f32[8,144,128]{2,1,0:T(8,128)S(1)} collective-permute-done((f32[8,144,128]{2,1,0:T(8,128)S(1)}, f32[8,144,128]{2,1,0:T(8,128)S(1)}, u32[]{:S(2)}, u32[]{:S(2)}) %collective-permute-start.12) | collective-permute-done | bytes 589856 | tf_op jit(solution)/shard_map/ppermute | solution.py:1336
  230.9 3.2 %collective-permute-done.13.rim_e_ref.refs_7_ = f32[8,144,128]{2,1,0:T(8,128)S(1)} collective-permute-done((f32[8,144,128]{2,1,0:T(8,128)S(1)}, f32[8,144,128]{2,1,0:T(8,128)S(1)}, u32[]{:S(2)}, u32[]{:S(2)}) %collective-permute-start.13) | collective-permute-done | bytes 589856 | tf_op jit(solution)/shard_map/ppermute | solution.py:1339
  234.1 9.1 %last_chl.1 = f32[8,48,256]{2,1,0:T(8,128)} custom-call(s32[8,8]{1,0:T(8,128)S(1)} %copy-done.15, f32[8,1152,256]{2,1,0:T(8,128)} %inner.3.part_ref.refs_0_.refs_1_.refs_2_.refs_3_, f32[8,1152,256]{2,1,0:T(8,128)} %inner.3.part_ref.refs_0_.refs_1_.refs_2_.refs_3_, f32[8,1152,256]{2,1,0:T(8,128)} %inner.3.part_ref.refs_0_.refs_1_.refs_2_.refs_3_, ...), custom_call_target="tpu_custom_call" | custom-call | tf_op jit(solution)/shard_map/last_chl/pallas_call | solution.py:792
  243.2 3.8 %all-to-all-start.4 = ((f32[8,48,256]{2,1,0:T(8,128)}), f32[8,48,256]{2,1,0:T(8,128)S(1)}, u32[]{:S(2)}, u32[]{:S(2)}) async-start(f32[8,48,256]{2,1,0:T(8,128)} %last_chl.1), calls=%async_computation.4 | async-start | bytes 786432 | tf_op jit(solution)/shard_map/all_to_all | solution.py:1342
  247.0 13.9 %step.3.after_ref = f32[8,1152,256]{2,1,0:T(8,128)} custom-call(s32[8,8]{1,0:T(8,128)S(1)} %copy-done.15, f32[8,1152,256]{2,1,0:T(8,128)} %inner.3.part_ref.refs_0_.refs_1_.refs_2_.refs_3_, f32[8,208,256]{2,1,0:T(8,128)S(1)} %copy-done.1, f32[8,288,128]{2,1,0:T(8,128)} %all-to-all-done.3.rim_ref.refs_5_, ...), custom_call_target="tpu_custom_call" | custom-call | tf_op jit(solution)/shard_map/step/pallas_call | solution.py:702
  260.9 4.3 %heat.1 = bf16[48,48,384]{2,1,0:T(8,128)(2,1)} custom-call(s32[8,8]{1,0:T(8,128)S(1)} %copy-done.15, f32[8,48,256]{2,1,0:T(8,128)S(1)} %all-to-all-done.4.chl_ref, f32[48,384]{1,0:T(8,128)S(1)} %copy-done.28, s32[16,128]{1,0:T(8,128)S(1)} %copy-done.31, bf16[128,384]{1,0:T(8,128)(2,1)S(1)} %fusion.widen_ref, f32[8,1152,256]{2,1,0:T(8,128)} %step.3.after_ref), custom_call_target="tpu_custom_call" | custom-call | tf_op jit(solution)/shard_map/heat/pallas_call | solution.py:1265
  (108 shorter events, 37.9 us)
Async XLA Ops:
  12.7 9.6 %copy-start.30 = (s32[16,128]{1,0:T(8,128)S(1)}, s32[16,128]{1,0:T(8,128)}, u32[]{:S(2)}) copy-start(s32[16,128]{1,0:T(8,128)} %land_ref.3) | copy-start | bytes 24580
  12.7 18.6 %copy-start.29 = (bf16[16,128,48]{1,2,0:T(8,128)(2,1)S(1)}, bf16[16,128,48]{1,2,0:T(8,128)(2,1)}, u32[]{:S(2)}) copy-start(bf16[16,128,48]{1,2,0:T(8,128)(2,1)} %param.8) | copy-start | bytes 589828
  12.7 61.8 %all-to-all-start.1 = ((f32[8,576,128]{2,1,0:T(8,128)}), f32[8,576,128]{2,1,0:T(8,128)S(1)}, u32[]{:S(2)}, u32[]{:S(2)}) async-start(f32[8,576,128]{2,1,0:T(8,128)} %copy-done.7), calls=%async_computation.1 | async-start | bytes 4718592 | tf_op jit(solution)/shard_map/all_to_all | solution.py:1342
  22.5 41.5 %collective-permute-start.2 = (f32[9,128]{1,0:T(8,128)S(1)}, f32[9,128]{1,0:T(8,128)S(1)}, u32[]{:S(2)}, u32[]{:S(2)}) collective-permute-start(f32[9,128]{1,0:T(8,128)S(1)} %select_maximum_fusion.1), channel_id=1, source_target_pairs={{0,1},{1,2},{2,3},{3,4},{4,5},{5,6},{6,7},{7,0},{8,9},{9,10},{10,1... | collective-permute-start | bytes 13832 | tf_op jit(solution)/shard_map/ppermute | solution.py:1319
  25.4 38.7 %collective-permute-start = (f32[49,384]{1,0:T(8,128)S(1)}, f32[49,384]{1,0:T(8,128)S(1)}, u32[]{:S(2)}, u32[]{:S(2)}) collective-permute-start(f32[49,384]{1,0:T(8,128)S(1)} %select_maximum_fusion), channel_id=1, source_target_pairs={{0,8},{8,16},{16,24},{1,9},{9,17},{17,25},{2,10},{10,18},{18,26},{... | collective-permute-start | bytes 225800 | tf_op jit(solution)/shard_map/ppermute | solution.py:1317
  26.8 33.4 %collective-permute-start.1 = (f32[1,384]{1,0:T(1,128)S(1)}, f32[1,384]{1,0:T(1,128)S(1)}, u32[]{:S(2)}, u32[]{:S(2)}) collective-permute-start(f32[1,384]{1,0:T(1,128)S(1)} %pad.19), channel_id=1, source_target_pairs={{8,0},{16,8},{24,16},{9,1},{17,9},{25,17},{10,2},{18,10},{26,18},{... | collective-permute-start | bytes 4616 | tf_op jit(solution)/shard_map/ppermute | solution.py:1318
  28.1 32.1 %collective-permute-start.3 = (f32[1,128]{1,0:T(1,128)S(1)}, f32[1,128]{1,0:T(1,128)S(1)}, u32[]{:S(2)}, u32[]{:S(2)}) collective-permute-start(f32[1,128]{1,0:T(1,128)S(1)} %pad.22), channel_id=1, source_target_pairs={{0,7},{1,0},{2,1},{3,2},{4,3},{5,4},{6,5},{7,6},{8,15},{9,8},{10,9... | collective-permute-start | bytes 1544 | tf_op jit(solution)/shard_map/ppermute | solution.py:1320
  31.4 32.6 %copy-start.15 = (s32[8,8]{1,0:T(8,128)S(1)}, s32[8,8]{1,0:T(8,128)}, u32[]{:S(2)}) copy-start(s32[8,8]{1,0:T(8,128)} %routing.1.table_ref) | copy-start | bytes 772
  31.4 32.6 %copy-start.28 = (f32[48,384]{1,0:T(8,128)S(1)}, f32[48,384]{1,0:T(8,128)}, u32[]{:S(2)}) copy-start(f32[48,384]{1,0:T(8,128)} %light_ref.3) | copy-start | bytes 221188
  75.9 48.4 %all-to-all-start = ((f32[8,208,256]{2,1,0:T(8,128)}), f32[8,208,256]{2,1,0:T(8,128)S(1)}, u32[]{:S(2)}, u32[]{:S(2)}) async-start(f32[8,208,256]{2,1,0:T(8,128)} %copy-done.13), calls=%async_computation | async-start | bytes 3407872 | tf_op jit(solution)/shard_map/all_to_all | solution.py:1342
  84.4 1.7 copy-start.6
  94.4 29.9 %collective-permute-start.4 = (f32[1152,128]{1,0:T(8,128)}, f32[1152,128]{1,0:T(8,128)S(1)}, u32[]{:S(2)}, u32[]{:S(2)}) collective-permute-start(f32[1152,128]{1,0:T(8,128)} %get-tuple-element.19.high_ref), channel_id=1, source_target_pairs={{0,8},{8,16},{16,24},{1,9},{9,17},{17,25},{2,10},{10,18},{18,26},{... | collective-permute-start | bytes 1769480 | tf_op jit(solution)/shard_map/ppermute | solution.py:1330
  95.8 28.5 %collective-permute-start.5 = (f32[1152,128]{1,0:T(8,128)S(1)}, f32[1152,128]{1,0:T(8,128)S(1)}, u32[]{:S(2)}, u32[]{:S(2)}) collective-permute-start(f32[1152,128]{1,0:T(8,128)S(1)} %get-tuple-element.20.low_ref), channel_id=1, source_target_pairs={{8,0},{16,8},{24,16},{9,1},{17,9},{25,17},{10,2},{18,10},{26,18},{... | collective-permute-start | bytes 1769480 | tf_op jit(solution)/shard_map/ppermute | solution.py:1333
  97.9 26.4 %collective-permute-start.6 = (f32[48,128]{1,0:T(8,128)}, f32[48,128]{1,0:T(8,128)}, u32[]{:S(2)}, u32[]{:S(2)}) collective-permute-start(f32[48,128]{1,0:T(8,128)} %get-tuple-element.21), channel_id=1, source_target_pairs={{0,1},{1,2},{2,3},{3,4},{4,5},{5,6},{6,7},{7,0},{8,9},{9,10},{10,1... | collective-permute-start | bytes 73736 | tf_op jit(solution)/shard_map/ppermute | solution.py:1336
  99.9 24.4 %collective-permute-start.7 = (f32[48,128]{1,0:T(8,128)}, f32[48,128]{1,0:T(8,128)}, u32[]{:S(2)}, u32[]{:S(2)}) collective-permute-start(f32[48,128]{1,0:T(8,128)} %get-tuple-element.21), channel_id=1, source_target_pairs={{0,7},{1,0},{2,1},{3,2},{4,3},{5,4},{6,5},{7,6},{8,15},{9,8},{10,9... | collective-permute-start | bytes 73736 | tf_op jit(solution)/shard_map/ppermute | solution.py:1339
  124.3 3.3 %copy-start = (f32[8,208,256]{2,1,0:T(8,128)}, f32[8,208,256]{2,1,0:T(8,128)S(1)}, u32[]{:S(2)}) copy-start(f32[8,208,256]{2,1,0:T(8,128)S(1)} %all-to-all-done.phys_ref.refs_0_.refs_2_.refs_4_) | copy-start | bytes 5111812
  124.4 3.3 %copy-start.11 = (f32[1152,128]{1,0:T(8,128)}, f32[1152,128]{1,0:T(8,128)S(1)}, u32[]{:S(2)}) copy-start(f32[1152,128]{1,0:T(8,128)S(1)} %collective-permute-done.5.above_ref) | copy-start | bytes 1769476
  127.6 53.7 %all-to-all-start.2 = ((f32[8,288,128]{2,1,0:T(8,128)}), f32[8,288,128]{2,1,0:T(8,128)S(1)}, u32[]{:S(2)}, u32[]{:S(2)}) async-start(f32[8,288,128]{2,1,0:T(8,128)} %copy-done.8), calls=%async_computation.2 | async-start | bytes 2359296 | tf_op jit(solution)/shard_map/all_to_all | solution.py:1342
  140.6 15.7 %copy-start.1 = (f32[8,208,256]{2,1,0:T(8,128)S(1)}, f32[8,208,256]{2,1,0:T(8,128)}, u32[]{:S(2)}) copy-start(f32[8,208,256]{2,1,0:T(8,128)} %copy-done) | copy-start | bytes 5111812
  146.0 5.5 %copy-start.19 = (f32[8,144,128]{2,1,0:T(8,128)S(1)}, f32[8,144,128]{2,1,0:T(8,128)}, u32[]{:S(2)}) copy-start(f32[8,144,128]{2,1,0:T(8,128)} %get-tuple-element.24) | copy-start | bytes 1769476
  146.0 7.3 %copy-start.17 = (f32[8,144,128]{2,1,0:T(8,128)S(1)}, f32[8,144,128]{2,1,0:T(8,128)}, u32[]{:S(2)}) copy-start(f32[8,144,128]{2,1,0:T(8,128)} %get-tuple-element.25) | copy-start | bytes 1769476
  148.5 22.7 %collective-permute-start.10 = (f32[1152,128]{1,0:T(8,128)S(1)}, f32[1152,128]{1,0:T(8,128)S(1)}, u32[]{:S(2)}, u32[]{:S(2)}) collective-permute-start(f32[1152,128]{1,0:T(8,128)S(1)} %get-tuple-element.30), channel_id=1, source_target_pairs={{0,8},{8,16},{16,24},{1,9},{9,17},{17,25},{2,10},{10,18},{18,26},{... | collective-permute-start | bytes 1769480 | tf_op jit(solution)/shard_map/ppermute | solution.py:1330
  150.2 21.0 %collective-permute-start.11 = (f32[1152,128]{1,0:T(8,128)S(1)}, f32[1152,128]{1,0:T(8,128)S(1)}, u32[]{:S(2)}, u32[]{:S(2)}) collective-permute-start(f32[1152,128]{1,0:T(8,128)S(1)} %get-tuple-element.31), channel_id=1, source_target_pairs={{8,0},{16,8},{24,16},{9,1},{17,9},{25,17},{10,2},{18,10},{26,18},{... | collective-permute-start | bytes 1769480 | tf_op jit(solution)/shard_map/ppermute | solution.py:1333
  151.5 29.0 %collective-permute-start.8 = (f32[8,144,128]{2,1,0:T(8,128)S(1)}, f32[8,144,128]{2,1,0:T(8,128)S(1)}, u32[]{:S(2)}, u32[]{:S(2)}) collective-permute-start(f32[8,144,128]{2,1,0:T(8,128)S(1)} %copy-done.19), channel_id=1, source_target_pairs={{0,1},{1,2},{2,3},{3,4},{4,5},{5,6},{6,7},{7,0},{8,9},{9,10},{10,1... | collective-permute-start | bytes 1769480 | tf_op jit(solution)/shard_map/ppermute | solution.py:1336
  153.3 28.0 %collective-permute-start.9 = (f32[8,144,128]{2,1,0:T(8,128)S(1)}, f32[8,144,128]{2,1,0:T(8,128)}, u32[]{:S(2)}, u32[]{:S(2)}) collective-permute-start(f32[8,144,128]{2,1,0:T(8,128)S(1)} %copy-done.17), channel_id=1, source_target_pairs={{0,7},{1,0},{2,1},{3,2},{4,3},{5,4},{6,5},{7,6},{8,15},{9,8},{10,9... | collective-permute-start | bytes 1769480 | tf_op jit(solution)/shard_map/ppermute | solution.py:1339
  182.4 4.7 %copy-start.3 = (f32[8,288,128]{2,1,0:T(8,128)S(1)}, f32[8,288,128]{2,1,0:T(8,128)}, u32[]{:S(2)}) copy-start(f32[8,288,128]{2,1,0:T(8,128)} %copy-done.2) | copy-start | bytes 3538948
  182.4 4.7 %copy-start.10 = (f32[8,144,128]{2,1,0:T(8,128)S(1)}, f32[8,144,128]{2,1,0:T(8,128)}, u32[]{:S(2)}) copy-start(f32[8,144,128]{2,1,0:T(8,128)} %copy-done.9) | copy-start | bytes 1769476
  182.4 51.7 %all-to-all-start.3 = ((f32[8,288,128]{2,1,0:T(8,128)}), f32[8,288,128]{2,1,0:T(8,128)}, u32[]{:S(2)}, u32[]{:S(2)}) async-start(f32[8,288,128]{2,1,0:T(8,128)} %gate.3), calls=%async_computation.3 | async-start | bytes 2359296 | tf_op jit(solution)/shard_map/all_to_all | solution.py:1342
  201.5 29.4 %collective-permute-start.12 = (f32[8,144,128]{2,1,0:T(8,128)S(1)}, f32[8,144,128]{2,1,0:T(8,128)S(1)}, u32[]{:S(2)}, u32[]{:S(2)}) collective-permute-start(f32[8,144,128]{2,1,0:T(8,128)S(1)} %get-tuple-element.32), channel_id=1, source_target_pairs={{0,1},{1,2},{2,3},{3,4},{4,5},{5,6},{6,7},{7,0},{8,9},{9,10},{10,1... | collective-permute-start | bytes 1769480 | tf_op jit(solution)/shard_map/ppermute | solution.py:1336
  203.7 30.4 %collective-permute-start.13 = (f32[8,144,128]{2,1,0:T(8,128)S(1)}, f32[8,144,128]{2,1,0:T(8,128)S(1)}, u32[]{:S(2)}, u32[]{:S(2)}) collective-permute-start(f32[8,144,128]{2,1,0:T(8,128)S(1)} %get-tuple-element.33), channel_id=1, source_target_pairs={{0,7},{1,0},{2,1},{3,2},{4,3},{5,4},{6,5},{7,6},{8,15},{9,8},{10,9... | collective-permute-start | bytes 1769480 | tf_op jit(solution)/shard_map/ppermute | solution.py:1339
  243.2 17.7 %all-to-all-start.4 = ((f32[8,48,256]{2,1,0:T(8,128)}), f32[8,48,256]{2,1,0:T(8,128)S(1)}, u32[]{:S(2)}, u32[]{:S(2)}) async-start(f32[8,48,256]{2,1,0:T(8,128)} %last_chl.1), calls=%async_computation.4 | async-start | bytes 786432 | tf_op jit(solution)/shard_map/all_to_all | solution.py:1342
  247.0 13.9 %copy-start.31 = (s32[16,128]{1,0:T(8,128)S(1)}, s32[16,128]{1,0:T(8,128)}, u32[]{:S(2)}) copy-start(s32[16,128]{1,0:T(8,128)} %land_ref.3) | copy-start | bytes 24580
  (19 other events, 18.8 us)
